TPU v7x, 32 devices: a whole 2x2x4 slice. The times are simulated.
32 devices in a mesh: space: 16 (over z, x, core), chan: 2 (over y).
Axes of the slice: x: 2, y: 2, z: 4, core: 2. Of those that a mesh axis runs over, the one named last changes fastest.
Arguments:
- field: bfloat16 [256, 8, 2048], P('chan', None, 'space'), may hold values from -6 to 6
- first_weight: bfloat16 [256, 9, 256], P('chan'), may hold values from -0.125 to 0.125
- second_weight: bfloat16 [256, 9, 256], P('chan'), may hold values from -0.125 to 0.125
- cotangent: bfloat16 [256, 8, 2048], P('chan', None, 'space'), may hold values from -6 to 6
Outputs:
- field_grad: bfloat16 [256, 8, 2048], P('chan', None, 'space')
- first_grad: float32 [256, 9, 256], P('chan')
- second_grad: float32 [256, 9, 256], P('chan')
All inputs are finite; a program needn't handle non-finite values.
Results may differ from a plain program's by a relative error of at most 0.0053.
Values may be sent and summed in bfloat16 or wider, within the bound.
No kernel may reach another device: no remote copies, remote signals or barrier semaphores. Data moves between devices by JAX's collectives and lax.ppermute only.
A program may use at most 64 MiB of HBM per device.

v0:
```python
import math

import jax
import jax.numpy as jnp
from jax import lax
from jax.sharding import PartitionSpec as P


def with_halo(block, sides, width):
    for axis, dim in sides:
        count = lax.axis_size(axis)
        forward = [(i, i + 1) for i in range(count - 1)]
        forward.append((count - 1, 0))
        backward = [(target, source) for source, target in forward]
        low = lax.ppermute(
            lax.slice_in_dim(block, block.shape[dim] - width, None, axis=dim), axis, forward
        )
        high = lax.ppermute(lax.slice_in_dim(block, 0, width, axis=dim), axis, backward)
        block = jnp.concatenate([low, block, high], axis=dim)
    return block


def pad_rows(values):
    return jnp.pad(values, ((0, 0), (1, 1), (0, 0)))


def widen(values):
    return with_halo(values, (("space", 2),), 2)


def collect(values):
    return lax.all_gather(values, "chan", axis=0, tiled=True)


def conv_forward(padded, weight):
    height = padded.shape[1] - 2
    length = padded.shape[2] - 2
    total = jnp.zeros((weight.shape[0], height, length), jnp.float32)
    for tap_row in range(3):
        for tap_col in range(3):
            window = padded[:, tap_row : tap_row + height, tap_col : tap_col + length]
            total = total + jnp.einsum(
                "oi,irc->orc",
                weight[:, 3 * tap_row + tap_col, :],
                window,
                preferred_element_type=jnp.float32,
            )
    return total


def conv_back(padded, weight):
    height = padded.shape[1] - 2
    length = padded.shape[2] - 2
    total = jnp.zeros((weight.shape[2], height, length), jnp.float32)
    for tap_row in range(3):
        for tap_col in range(3):
            window = padded[
                :, 2 - tap_row : 2 - tap_row + height, 2 - tap_col : 2 - tap_col + length
            ]
            total = total + jnp.einsum(
                "oi,orc->irc",
                weight[:, 3 * tap_row + tap_col, :],
                window,
                preferred_element_type=jnp.float32,
            )
    return total


def reduce_back(padded, weight):
    return lax.psum_scatter(conv_back(padded, weight), "chan", scatter_dimension=0, tiled=True)


def weight_grad(upstream, padded):
    height = upstream.shape[1]
    length = upstream.shape[2]
    pieces = []
    for tap_row in range(3):
        for tap_col in range(3):
            window = padded[:, tap_row : tap_row + height, tap_col : tap_col + length]
            pieces.append(
                jnp.einsum("orc,irc->oi", upstream, window, preferred_element_type=jnp.float32)
            )
    return jnp.stack(pieces, axis=1)


def smooth_gelu(values):
    return jax.nn.gelu(values, approximate=True)


def resample(extended):
    lower = jnp.pad(extended, ((0, 0), (0, 1), (0, 0)))
    top_left = lower[:, :-1, :-1]
    top_right = lower[:, :-1, 1:]
    low_left = lower[:, 1:, :-1]
    low_right = lower[:, 1:, 1:]
    even_even = smooth_gelu(top_left)
    even_odd = smooth_gelu((top_left + top_right) * 0.5)
    odd_even = smooth_gelu((top_left + low_left) * 0.5)
    odd_odd = smooth_gelu((top_left + top_right + low_left + low_right) * 0.25)
    row_even = (even_odd[:, :, :-1] + 2.0 * even_even[:, :, 1:] + even_odd[:, :, 1:]) * 0.25
    row_odd = (odd_odd[:, :, :-1] + 2.0 * odd_even[:, :, 1:] + odd_odd[:, :, 1:]) * 0.25
    shifted = jnp.pad(row_odd, ((0, 0), (1, 0), (0, 0)))[:, :-1]
    return (shifted + 2.0 * row_even + row_odd) * 0.25


def split_plan(field, first_weight, second_weight, cotangent, grad_scale):
    field_all = collect(widen(field))
    field_pad = pad_rows(field_all[:, :, 1:-1])
    hidden = conv_forward(field_pad, first_weight).astype(jnp.bfloat16)
    hidden_wide = widen(hidden)
    smooth_values, pullback = jax.vjp(resample, hidden_wide.astype(jnp.float32))
    smooth = smooth_values[:, :, 1:-1].astype(jnp.bfloat16)
    smooth_all = collect(widen(smooth))
    smooth_pad = pad_rows(smooth_all[:, :, 1:-1])
    cot_wide = widen(cotangent)
    second_grad = weight_grad(cotangent, smooth_pad) * grad_scale
    smooth_sum = reduce_back(pad_rows(cot_wide[:, :, 1:-1]), second_weight)
    smooth_grad = smooth_sum.astype(jnp.bfloat16)
    grad_wide = widen(smooth_grad)
    hidden_full = pullback(grad_wide[:, :, 1:-1].astype(jnp.float32))[0]
    hidden_grad = hidden_full[:, :, 2:-2].astype(jnp.bfloat16)
    first_grad = weight_grad(hidden_grad, field_pad) * grad_scale
    hidden_grad_wide = widen(hidden_grad)
    field_sum = reduce_back(pad_rows(hidden_grad_wide[:, :, 1:-1]), first_weight)
    field_grad = (cotangent.astype(jnp.float32) + field_sum).astype(jnp.bfloat16)
    return (field_grad, first_grad, second_grad)


def on_device(field, first_weight, second_weight, cotangent):
    height = field.shape[1]
    length = field.shape[2]
    grad_scale = 1.0 / math.sqrt(height * length * lax.axis_size("space"))
    field_grad, first_grad, second_grad = split_plan(
        field, first_weight, second_weight, cotangent, grad_scale
    )
    first_grad, second_grad = lax.psum((first_grad, second_grad), "space")
    return (field_grad, first_grad, second_grad)


def solution(mesh):
    in_specs = (
        P("chan", None, "space"),
        P("chan", None, None),
        P("chan", None, None),
        P("chan", None, "space"),
    )
    out_specs = (P("chan", None, "space"), P("chan", None, None), P("chan", None, None))
    return jax.shard_map(
        on_device, mesh=mesh, in_specs=in_specs, out_specs=out_specs, check_vma=False
    )
```

profile of v0, /device:TPU:0, one launch (start us, length us, event | category | flops | bytes accessed | tf_op | source)
XLA Modules:
  0.0 224.3 jit_solution(18248751908028576083)
XLA Ops:
  7.2 1.2 copy.7
  8.9 5.0 %collective-permute-start.1 = (bf16[128,8,2]{0,2,1:T(2,128)(2,1)S(1)}, bf16[128,8,2]{0,2,1:T(2,128)(2,1)S(1)}, u32[]{:S(2)}, u32[]{:S(2)}) collective-permute-start(bf16[128,8,2]{0,2,1:T(2,128)(2,1)S(1)} %get-tuple-element.37), channel_id=1, source_target_pairs={{2,0},{4,2},{6,4},{8,6},{10,8},{12,10},{14,12},{16,14},{18,16},{20... | collective-permute-start | bytes 12296 | tf_op jit(solution)/shard_map/ppermute | solution.py:18
  13.9 1.1 copy.16
  15.2 4.4 %collective-permute-start.5 = (bf16[128,8,2]{0,2,1:T(2,128)(2,1)S(1)}, bf16[128,8,2]{0,2,1:T(2,128)(2,1)S(1)}, u32[]{:S(2)}, u32[]{:S(2)}) collective-permute-start(bf16[128,8,2]{0,2,1:T(2,128)(2,1)S(1)} %get-tuple-element.33), channel_id=1, source_target_pairs={{2,0},{4,2},{6,4},{8,6},{10,8},{12,10},{14,12},{16,14},{18,16},{20... | collective-permute-start | bytes 12296 | tf_op jit(solution)/shard_map/ppermute | solution.py:18
  19.6 1.1 fusion.105
  20.8 1.1 convolution_bitcast_fusion.1
  22.0 1.1 convolution_bitcast_fusion.2
  23.1 1.1 fusion.102
  24.2 1.1 convolution_bitcast_fusion
  25.5 7.4 %all_gather.6 = bf16[256,8,132]{0,2,1:T(8,128)(2,1)S(1)} all-gather(bf16[128,8,132]{0,2,1:T(8,128)(2,1)S(1)} %pad_maximum_fusion.2), channel_id=1, replica_groups=mesh['space'=16,'chan'=2] {'chan'}, dimensions={0}, use_global_device_ids=true | all-gather | bytes 811008 | tf_op jit(solution)/shard_map/all_gather | solution.py:32
  33.9 1.1 convolution_add_fusion.8
  35.1 1.1 convolution_add_fusion.7
  36.2 1.1 fusion.8
  37.3 2.2 fusion.3
  41.5 4.4 %collective-permute-start.7 = (bf16[128,8,2]{0,2,1:T(2,128)(2,1)S(1)}, bf16[128,8,2]{0,2,1:T(2,128)(2,1)S(1)}, u32[]{:S(2)}, u32[]{:S(2)}) collective-permute-start(bf16[128,8,2]{0,2,1:T(2,128)(2,1)S(1)} %get-tuple-element.31), channel_id=1, source_target_pairs={{2,0},{4,2},{6,4},{8,6},{10,8},{12,10},{14,12},{16,14},{18,16},{20... | collective-permute-start | bytes 12296 | tf_op jit(solution)/shard_map/ppermute | solution.py:18
  46.0 1.3 collective-permute-done.6
  47.4 1.4 add_multiply_fusion.2
  48.8 10.1 %reduce-scatter.3.cloned.1.call-done = f32[128,8,128]{0,2,1:T(8,128)} async-done(((f32[256,8,128]{0,2,1:T(8,128)}), f32[128,8,128]{0,2,1:T(8,128)}) %reduce-scatter.3.cloned.1.call-update) | async-done | bytes 524304 | tf_op jit(solution)/shard_map/reduce_scatter | solution.py:70
  58.9 1.1 convert_element_type.31
  60.1 4.4 %collective-permute-start.3 = (bf16[128,8,2]{0,2,1:T(2,128)(2,1)S(1)}, bf16[128,8,2]{0,2,1:T(2,128)(2,1)S(1)}, u32[]{:S(2)}, u32[]{:S(2)}) collective-permute-start(bf16[128,8,2]{0,2,1:T(2,128)(2,1)S(1)} %get-tuple-element.35), channel_id=1, source_target_pairs={{2,0},{4,2},{6,4},{8,6},{10,8},{12,10},{14,12},{16,14},{18,16},{20... | collective-permute-start | bytes 12296 | tf_op jit(solution)/shard_map/ppermute | solution.py:18
  64.7 1.1 collective-permute-done.2
  68.0 1.1 fusion.64
  69.7 4.5 %collective-permute-start.9 = (bf16[128,8,2]{0,2,1:T(2,128)(2,1)S(1)}, bf16[128,8,2]{0,2,1:T(2,128)(2,1)S(1)}, u32[]{:S(2)}, u32[]{:S(2)}) collective-permute-start(bf16[128,8,2]{0,2,1:T(2,128)(2,1)S(1)} %get-tuple-element.18), channel_id=1, source_target_pairs={{2,0},{4,2},{6,4},{8,6},{10,8},{12,10},{14,12},{16,14},{18,16},{20... | collective-permute-start | bytes 12296 | tf_op jit(solution)/shard_map/ppermute | solution.py:18
  74.2 4.4 %collective-permute-start.11 = (bf16[128,8,2]{0,2,1:T(2,128)(2,1)S(1)}, bf16[128,8,2]{0,2,1:T(2,128)(2,1)S(1)}, u32[]{:S(2)}, u32[]{:S(2)}) collective-permute-start(bf16[128,8,2]{0,2,1:T(2,128)(2,1)S(1)} %get-tuple-element.27), channel_id=1, source_target_pairs={{2,0},{4,2},{6,4},{8,6},{10,8},{12,10},{14,12},{16,14},{18,16},{20... | collective-permute-start | bytes 12296 | tf_op jit(solution)/shard_map/ppermute | solution.py:18
  81.7 1.1 broadcast_multiply_fusion.1
  84.2 7.2 %all_gather.7 = bf16[256,8,132]{0,2,1:T(8,128)(2,1)S(1)} all-gather(bf16[128,8,132]{0,2,1:T(8,128)(2,1)S(1)} %pad_maximum_fusion.3), channel_id=1, replica_groups=mesh['space'=16,'chan'=2] {'chan'}, dimensions={0}, use_global_device_ids=true | all-gather | bytes 811008 | tf_op jit(solution)/shard_map/all_gather | solution.py:32
  93.0 1.2 fusion.4
  97.1 1.1 broadcast_multiply_fusion
  98.2 12.8 %reduce-scatter.5.cloned.1.call-done = f32[128,8,128]{0,2,1:T(8,128)} async-done(((f32[256,8,128]{0,2,1:T(8,128)}), f32[128,8,128]{0,2,1:T(8,128)}) %reduce-scatter.5.cloned.1.call-update) | async-done | bytes 524304 | tf_op jit(solution)/shard_map/reduce_scatter | solution.py:70
  111.0 1.1 add_convert_fusion.1
  113.0 101.3 %all-reduce.20.cloned.1.call-done = (f32[128,9,256]{2,0,1:T(8,128)}, f32[128,9,256]{2,0,1:T(8,128)}) async-done(((f32[128,9,256]{2,0,1:T(8,128)}, f32[128,9,256]{2,0,1:T(8,128)}), (f32[128,9,256]{2,0,1:T(8,128)}, f32[128,9,256]{2,0,1:T(8,128)})) %all-reduce.20.cloned.1.call-update) | async-done | bytes 2359312 | tf_op jit(solution)/shard_map/psum | solution.py:136
  214.3 2.5 %copy.130 = f32[128,9,256]{2,0,1:T(8,128)} copy(f32[128,9,256]{2,0,1:T(8,128)} %get-tuple-element.39) | data formatting | bytes 2359296
  (90 shorter events, 17.4 us)
Async XLA Ops:
  7.2 51.7 %reduce-scatter.3.cloned.1.call-start = ((), (), s32[]{:S(2)}) async-start(), calls=%async_computation.2 | async-start | bytes 1572864 | tf_op jit(solution)/shard_map/reduce_scatter | solution.py:70
  8.4 12.3 %collective-permute-start = (bf16[128,8,2]{0,2,1:T(2,128)(2,1)S(1)}, bf16[128,8,2]{0,2,1:T(2,128)(2,1)S(1)}, u32[]{:S(2)}, u32[]{:S(2)}) collective-permute-start(bf16[128,8,2]{0,2,1:T(2,128)(2,1)S(1)} %get-tuple-element.36), channel_id=1, source_target_pairs={{0,2},{2,4},{4,6},{6,8},{8,10},{10,12},{12,14},{14,16},{16,18},{18... | collective-permute-start | bytes 12296 | tf_op jit(solution)/shard_map/ppermute | solution.py:15
  8.9 11.8 %collective-permute-start.1 = (bf16[128,8,2]{0,2,1:T(2,128)(2,1)S(1)}, bf16[128,8,2]{0,2,1:T(2,128)(2,1)S(1)}, u32[]{:S(2)}, u32[]{:S(2)}) collective-permute-start(bf16[128,8,2]{0,2,1:T(2,128)(2,1)S(1)} %get-tuple-element.37), channel_id=1, source_target_pairs={{2,0},{4,2},{6,4},{8,6},{10,8},{12,10},{14,12},{16,14},{18,16},{20... | collective-permute-start | bytes 12296 | tf_op jit(solution)/shard_map/ppermute | solution.py:18
  15.1 10.3 %collective-permute-start.4 = (bf16[128,8,2]{0,2,1:T(2,128)(2,1)S(1)}, bf16[128,8,2]{0,2,1:T(2,128)(2,1)S(1)}, u32[]{:S(2)}, u32[]{:S(2)}) collective-permute-start(bf16[128,8,2]{0,2,1:T(2,128)(2,1)S(1)} %get-tuple-element.32), channel_id=1, source_target_pairs={{0,2},{2,4},{4,6},{6,8},{8,10},{10,12},{12,14},{14,16},{16,18},{18... | collective-permute-start | bytes 12296 | tf_op jit(solution)/shard_map/ppermute | solution.py:15
  15.2 10.2 %collective-permute-start.5 = (bf16[128,8,2]{0,2,1:T(2,128)(2,1)S(1)}, bf16[128,8,2]{0,2,1:T(2,128)(2,1)S(1)}, u32[]{:S(2)}, u32[]{:S(2)}) collective-permute-start(bf16[128,8,2]{0,2,1:T(2,128)(2,1)S(1)} %get-tuple-element.33), channel_id=1, source_target_pairs={{2,0},{4,2},{6,4},{8,6},{10,8},{12,10},{14,12},{16,14},{18,16},{20... | collective-permute-start | bytes 12296 | tf_op jit(solution)/shard_map/ppermute | solution.py:18
  25.4 7.6 %copy-start.2 = (bf16[128,9,256]{2,0,1:T(8,128)(2,1)S(1)}, bf16[128,9,256]{2,0,1:T(8,128)(2,1)}, u32[]{:S(2)}) copy-start(bf16[128,9,256]{2,0,1:T(8,128)(2,1)} %param.5) | copy-start | bytes 1769476
  39.5 71.5 %reduce-scatter.5.cloned.1.call-start = ((), (), s32[]{:S(2)}) async-start(), calls=%async_computation.3 | async-start | bytes 1572864 | tf_op jit(solution)/shard_map/reduce_scatter | solution.py:70
  41.5 5.8 %collective-permute-start.6 = (bf16[128,8,2]{0,2,1:T(2,128)(2,1)S(1)}, bf16[128,8,2]{0,2,1:T(2,128)(2,1)S(1)}, u32[]{:S(2)}, u32[]{:S(2)}) collective-permute-start(bf16[128,8,2]{0,2,1:T(2,128)(2,1)S(1)} %get-tuple-element.30), channel_id=1, source_target_pairs={{0,2},{2,4},{4,6},{6,8},{8,10},{10,12},{12,14},{14,16},{16,18},{18... | collective-permute-start | bytes 12296 | tf_op jit(solution)/shard_map/ppermute | solution.py:15
  41.5 5.8 %collective-permute-start.7 = (bf16[128,8,2]{0,2,1:T(2,128)(2,1)S(1)}, bf16[128,8,2]{0,2,1:T(2,128)(2,1)S(1)}, u32[]{:S(2)}, u32[]{:S(2)}) collective-permute-start(bf16[128,8,2]{0,2,1:T(2,128)(2,1)S(1)} %get-tuple-element.31), channel_id=1, source_target_pairs={{2,0},{4,2},{6,4},{8,6},{10,8},{12,10},{14,12},{16,14},{18,16},{20... | collective-permute-start | bytes 12296 | tf_op jit(solution)/shard_map/ppermute | solution.py:18
  58.9 5.7 %copy-start.1 = (f32[128,8,131]{0,2,1:T(8,128)S(1)}, f32[128,8,131]{0,2,1:T(8,128)}, u32[]{:S(2)}) copy-start(f32[128,8,131]{0,2,1:T(8,128)} %get-tuple-element.8) | copy-start | bytes 1609732
  60.0 5.8 %collective-permute-start.2 = (bf16[128,8,2]{0,2,1:T(2,128)(2,1)S(1)}, bf16[128,8,2]{0,2,1:T(2,128)(2,1)S(1)}, u32[]{:S(2)}, u32[]{:S(2)}) collective-permute-start(bf16[128,8,2]{0,2,1:T(2,128)(2,1)S(1)} %get-tuple-element.34), channel_id=1, source_target_pairs={{0,2},{2,4},{4,6},{6,8},{8,10},{10,12},{12,14},{14,16},{16,18},{18... | collective-permute-start | bytes 12296 | tf_op jit(solution)/shard_map/ppermute | solution.py:15
  60.1 5.8 %collective-permute-start.3 = (bf16[128,8,2]{0,2,1:T(2,128)(2,1)S(1)}, bf16[128,8,2]{0,2,1:T(2,128)(2,1)S(1)}, u32[]{:S(2)}, u32[]{:S(2)}) collective-permute-start(bf16[128,8,2]{0,2,1:T(2,128)(2,1)S(1)} %get-tuple-element.35), channel_id=1, source_target_pairs={{2,0},{4,2},{6,4},{8,6},{10,8},{12,10},{14,12},{16,14},{18,16},{20... | collective-permute-start | bytes 12296 | tf_op jit(solution)/shard_map/ppermute | solution.py:18
  66.0 1.1 copy-start
  69.7 13.7 %collective-permute-start.8 = (bf16[128,8,2]{0,2,1:T(2,128)(2,1)S(1)}, bf16[128,8,2]{0,2,1:T(2,128)(2,1)S(1)}, u32[]{:S(2)}, u32[]{:S(2)}) collective-permute-start(bf16[128,8,2]{0,2,1:T(2,128)(2,1)S(1)} %get-tuple-element.17), channel_id=1, source_target_pairs={{0,2},{2,4},{4,6},{6,8},{8,10},{10,12},{12,14},{14,16},{16,18},{18... | collective-permute-start | bytes 12296 | tf_op jit(solution)/shard_map/ppermute | solution.py:15
  69.7 13.7 %collective-permute-start.9 = (bf16[128,8,2]{0,2,1:T(2,128)(2,1)S(1)}, bf16[128,8,2]{0,2,1:T(2,128)(2,1)S(1)}, u32[]{:S(2)}, u32[]{:S(2)}) collective-permute-start(bf16[128,8,2]{0,2,1:T(2,128)(2,1)S(1)} %get-tuple-element.18), channel_id=1, source_target_pairs={{2,0},{4,2},{6,4},{8,6},{10,8},{12,10},{14,12},{16,14},{18,16},{20... | collective-permute-start | bytes 12296 | tf_op jit(solution)/shard_map/ppermute | solution.py:18
  74.2 9.9 %collective-permute-start.10 = (bf16[128,8,2]{0,2,1:T(2,128)(2,1)S(1)}, bf16[128,8,2]{0,2,1:T(2,128)(2,1)S(1)}, u32[]{:S(2)}, u32[]{:S(2)}) collective-permute-start(bf16[128,8,2]{0,2,1:T(2,128)(2,1)S(1)} %get-tuple-element.26), channel_id=1, source_target_pairs={{0,2},{2,4},{4,6},{6,8},{8,10},{10,12},{12,14},{14,16},{16,18},{18... | collective-permute-start | bytes 12296 | tf_op jit(solution)/shard_map/ppermute | solution.py:15
  74.2 9.9 %collective-permute-start.11 = (bf16[128,8,2]{0,2,1:T(2,128)(2,1)S(1)}, bf16[128,8,2]{0,2,1:T(2,128)(2,1)S(1)}, u32[]{:S(2)}, u32[]{:S(2)}) collective-permute-start(bf16[128,8,2]{0,2,1:T(2,128)(2,1)S(1)} %get-tuple-element.27), channel_id=1, source_target_pairs={{2,0},{4,2},{6,4},{8,6},{10,8},{12,10},{14,12},{16,14},{18,16},{20... | collective-permute-start | bytes 12296 | tf_op jit(solution)/shard_map/ppermute | solution.py:18
  81.7 1.2 copy-start.3
  94.3 120.0 %all-reduce.20.cloned.1.call-start = ((), (), s32[]{:S(2)}) async-start(), calls=%async_computation.4 | async-start | bytes 4718592 | tf_op jit(solution)/shard_map/psum | solution.py:136
  214.3 2.5 %copy-start.4 = (f32[128,9,256]{2,0,1:T(8,128)S(1)}, f32[128,9,256]{2,0,1:T(8,128)}, u32[]{:S(2)}) copy-start(f32[128,9,256]{2,0,1:T(8,128)} %get-tuple-element.40) | copy-start | bytes 3538948
Sparse Core Ops, SparseCore 0:
  39.6 19.1 reduce-scatter.2
  94.4 16.4 reduce-scatter.4
  115.2 99.0 all-reduce.19
where the time goes:
time: 225 us; the launch traced here: 224 us
  waiting for transfers between devices  127 us (56%)
  starting transfers between devices  28.1 us (12%)
  matrix products  23.2 us (10%)
  blocking collectives  14.6 us (6%)
  between operations  14.3 us (6%)
  other arithmetic  9.29 us (4%)
  local copies, waits for them, and re-layouts  8.19 us (4%)
    psum x1, waiting for transfers between devices, on_device(): first_grad, second_grad = lax.psum((first_grad, second_grad), 'space')  101 us
    ppermute x6, starting transfers between devices, with_halo(): lax.ppermute(lax.slice_in_dim(block, 0, width, axis=dim), axis, backward)  27.2 us
    reduce_scatter x2, waiting for transfers between devices, reduce_back(): lax.psum_scatter(conv_back(padded, weight), 'chan', scatter_dimension=0,...  22.8 us
    dot_general x18, matrix products, conv_back(): jnp.einsum('oi,orc->irc', weight[:, 3 * tap_row + tap_col, :], window, pr...  14.7 us
    all_gather x2, blocking collectives, collect(): return lax.all_gather(values, 'chan', axis=0, tiled=True)  14.6 us
    unnamed x15, local copies, waits for them, and re-layouts  7.72 us
    dot_general x18, matrix products, weight_grad(): jnp.einsum('orc,irc->oi', upstream, window, preferred_element_type=jnp.fl...  5.67 us
  transfers between devices with their start and end apart: 15, of which 5 were waited for; matrix products, arithmetic and copies ran while one was open for 10% of the time, Pallas kernels for 0%

commit v1 on v0

v1 whole, which is shorter than its diff:
```python
import functools
import math

import jax
import jax.numpy as jnp
from jax import lax
from jax.experimental import pallas as pl
from jax.experimental.pallas import tpu as pltpu
from jax.sharding import PartitionSpec as P

EDGE = 8
SENT = 4
SHARES = 4
GELU_RATE = math.sqrt(2.0 / math.pi)
GELU_CUBE = 0.044715
PARAMS = pltpu.CompilerParams(vmem_limit_bytes=12 * 1024 * 1024)
F32 = jnp.float32
BF16 = jnp.bfloat16


def swap_pairs(count, distance):
    return [(i, i ^ distance) for i in range(count)]


def shift(values, by):
    if by == 0:
        return values
    return pltpu.roll(values, by % values.shape[0], 0)


def matmul(left, right):
    return lax.dot_general(left, right, (((1,), (0,)), ((), ())), preferred_element_type=F32)


def matmul_nt(left, right):
    return lax.dot_general(left, right, (((1,), (1,)), ((), ())), preferred_element_type=F32)


def gelu_pair(values):
    square = values * values
    bent = jnp.tanh(GELU_RATE * (values + GELU_CUBE * (square * values)))
    inner_slope = GELU_RATE * (1.0 + 3.0 * GELU_CUBE * square)
    lifted = 0.5 * (1.0 + bent)
    return values * lifted, lifted + 0.5 * values * (1.0 - bent * bent) * inner_slope


def fill_block(scratch, lane, body, low, high):
    rows, length, width = body.shape
    lanes = pl.ds(lane, width)
    unused = jnp.zeros((rows, EDGE - SENT, width), F32)
    scratch[1 : rows + 1, EDGE : EDGE + length, lanes] = body
    low = jnp.concatenate([unused, low.astype(F32)], axis=1).astype(BF16)
    scratch[1 : rows + 1, 0:EDGE, lanes] = low
    high = jnp.concatenate([high.astype(F32), unused], axis=1).astype(BF16)
    scratch[1 : rows + 1, EDGE + length :, lanes] = high


def clear_rows(scratch):
    scratch[0] = jnp.zeros(scratch.shape[1:], scratch.dtype)
    scratch[scratch.shape[0] - 1] = jnp.zeros(scratch.shape[1:], scratch.dtype)


def chan_lanes(width):
    mine = lax.axis_index("chan")
    own = pl.multiple_of(mine * width, width)
    other = pl.multiple_of((1 - mine) * width, width)
    return own, other


def prepare_kernel(
    field, cot, weight,
    packed, field_out, cot_out, flat_out, last_out, first_out, weight_own,
    raw, wide, sems,
):
    width, rows, length = field.shape
    part = width // SHARES
    pieces = rows * length // part
    lane_own, lane_oth = chan_lanes(width)
    start = pl.multiple_of(lax.axis_index("space") % SHARES * part, part)
    away = weight.at[:, pl.ds(start, part), pl.ds(lane_oth, width)]
    copies = [
        pltpu.make_async_copy(field, raw.at[0], sems.at[0]),
        pltpu.make_async_copy(cot, raw.at[1], sems.at[1]),
        pltpu.make_async_copy(away, packed.at[pl.ds(pieces, 9)], sems.at[2]),
        pltpu.make_async_copy(weight.at[:, :, pl.ds(lane_own, width)], weight_own, sems.at[3]),
    ]
    for copy in copies:
        copy.start()
    for number, target in enumerate((field_out, cot_out)):
        copies[number].wait()
        wide[...] = raw[number].astype(F32).reshape(width * rows, length)
        for r in range(rows):
            row = wide[pl.ds(r, width, stride=rows), :]
            turned = row.T
            last_out[number, r] = turned[length - SENT :].astype(BF16)
            first_out[number, r] = turned[:SENT].astype(BF16)
            turned = turned.astype(BF16)
            target[r] = turned
            if number == 0:
                step = length // part
                packed[r * step : (r + 1) * step] = turned.reshape(step, part, width)
            else:
                flat_out[:, r * length : (r + 1) * length] = row.astype(BF16)
    copies[2].wait()
    copies[3].wait()


def forward_kernel(
    scale, own, packed, both, sides, weight, cot_flat,
    slopes_out, right_out, smooth_out, sums_out, block, hidden,
):
    rows, length, width = own.shape
    wide = length + 2 * EDGE
    lane_own, lane_oth = chan_lanes(width)
    clear_rows(block)
    other = packed[: packed.shape[0] - 9].reshape(own.shape)
    fill_block(block, lane_own, own[...], both[0, 0], both[1, 0])
    fill_block(block, lane_oth, other, sides[0, 0], sides[1, 0])
    clear_rows(right_out)
    right_out[1 : rows + 1, :, pl.ds(lane_own, width)] = own[...]
    right_out[1 : rows + 1, :, pl.ds(lane_oth, width)] = other
    total = None
    for p in range(3):
        taps = weight[3 * p : 3 * p + 3].reshape(3 * width, 2 * width)
        part = matmul_nt(block[p : p + rows].reshape(rows * wide, 2 * width), taps)
        total = part if total is None else total + part
    flat = (
        shift(total[:, :width], 1)
        + total[:, width : 2 * width]
        + shift(total[:, 2 * width :], -1)
    )
    hidden[...] = flat.astype(BF16).astype(F32).reshape(rows, wide, width)
    odd_before = jnp.zeros((wide, width), F32)
    for r in range(rows):
        here = hidden[r]
        pair = here + hidden[r + 1] if r + 1 < rows else here
        even_even, slopes_out[0, r] = gelu_pair(here)
        even_odd, slopes_out[1, r] = gelu_pair((here + shift(here, -1)) * 0.5)
        odd_even, slopes_out[2, r] = gelu_pair(pair * 0.5)
        odd_odd, slopes_out[3, r] = gelu_pair((pair + shift(pair, -1)) * 0.25)
        row_even = (shift(even_odd, 1) + 2.0 * even_even + even_odd) * 0.25
        row_odd = (shift(odd_odd, 1) + 2.0 * odd_even + odd_odd) * 0.25
        smooth = (odd_before + 2.0 * row_even + row_odd) * 0.25
        for q in range(3):
            moved = shift(smooth, 1 - q)[EDGE : EDGE + length].astype(BF16)
            for p in range(3):
                target = r + 1 - p
                if 0 <= target < rows:
                    lanes = slice((3 * p + q) * width, (3 * p + q + 1) * width)
                    smooth_out[target * length : (target + 1) * length, lanes] = moved
        odd_before = row_odd
    nothing = jnp.zeros((length, 3 * width), BF16)
    smooth_out[:length, : 3 * width] = nothing
    smooth_out[(rows - 1) * length :, 6 * width :] = nothing
    sums_out[...] = scale * matmul(cot_flat[...], smooth_out[...])


def weight_sums(scale, upstream, right, left, result, keep, send):
    rows, length, lanes = right.shape[0] - 2, right.shape[1], right.shape[2]
    width = left.shape[0] // 3
    for r in range(rows):
        row = upstream(r)
        for q in range(3):
            moved = shift(row, q - 1)[EDGE : EDGE + length].astype(BF16)
            left[q * width : (q + 1) * width, r * length : (r + 1) * length] = moved.T
    for p in range(3):
        result[...] = scale * matmul(left[...], right[p : p + rows].reshape(rows * length, lanes))
        for q in range(3):
            split_rows(result, q * width, width, slice(None), keep, send, 3 * p + q)


def split_rows(result, start, width, lanes, keep, send, place):
    upper = lax.axis_index("space") % 2
    half = width // 2
    first = pl.multiple_of(start + upper * half, half)
    second = pl.multiple_of(start + (1 - upper) * half, half)
    keep[place] = result[pl.ds(first, half), lanes]
    send[place] = result[pl.ds(second, half), lanes].astype(BF16)


def backward_kernel(
    scale, cot_own, cot_oth, both, sides, weight_own, weight_pair, weight_rest, slopes,
    right,
    grad_out, keep, send, block, left, result, grads, weight_oth,
):
    rows, length, width = cot_own.shape
    wide = length + 2 * EDGE
    clear_rows(block)
    fill_block(block, 0, cot_own[...], both[0, 1], both[1, 1])
    fill_block(block, width, cot_oth[...], sides[0, 1], sides[1, 1])
    part = width // SHARES
    share = lax.axis_index("space") % SHARES
    for source, number, distance in (
        (weight_pair, 0, 0), (weight_pair, 1, 2), (weight_rest, 0, 1), (weight_rest, 1, 3)
    ):
        start = pl.multiple_of((share ^ distance) * part, part)
        weight_oth[:, pl.ds(start, part)] = source[number]
    total = None
    for p in range(3):
        taps = jnp.concatenate(
            [
                jnp.concatenate([weight_own[3 * p + q] for q in range(3)], axis=1),
                jnp.concatenate([weight_oth[3 * p + q] for q in range(3)], axis=1),
            ],
            axis=0,
        )
        part = matmul(block[2 - p : 2 - p + rows].reshape(rows * wide, 2 * width), taps)
        total = part if total is None else total + part
    flat = (
        shift(total[:, :width], -1)
        + total[:, width : 2 * width]
        + shift(total[:, 2 * width :], 1)
    )
    grads[...] = flat.astype(BF16).astype(F32).reshape(rows, wide, width)
    odd_before = jnp.zeros((wide, width), F32)
    for r in range(rows):
        grad = grads[r]
        pair = grad + grads[r + 1] if r + 1 < rows else grad
        even_even = slopes[0, r] * grad * 0.25
        even_odd = slopes[1, r] * (grad + shift(grad, -1)) * 0.125
        odd_even = slopes[2, r] * pair * 0.125
        odd_odd = slopes[3, r] * (pair + shift(pair, -1)) * 0.0625
        row_even = even_even + 0.5 * (even_odd + shift(even_odd, 1))
        row_odd = 0.5 * odd_even + 0.25 * (odd_odd + shift(odd_odd, 1))
        rounded = (row_even + row_odd + odd_before).astype(BF16)
        grad_out[r] = rounded
        grads[r] = rounded.astype(F32)
        odd_before = row_odd
    weight_sums(scale, lambda r: grads[r], right, left, result, keep, send)


def second_kernel(scale, sums_own, cot_oth, smooth, keep, send, left, result):
    rows, length, width = cot_oth.shape
    for r in range(rows):
        left[:, r * length : (r + 1) * length] = cot_oth[r].T
    result[...] = scale * matmul(left[...], smooth[...])
    for side, sums in enumerate((sums_own, result)):
        for tap in range(9):
            lanes = slice(tap * width, (tap + 1) * width)
            split_rows(sums, 0, width, lanes, keep, send, 9 * side + tap)


def spread_kernel(grad, weight, keep, send, block, result):
    rows, wide, width = grad.shape
    length = wide - 2 * EDGE
    lane_own, lane_oth = chan_lanes(width)
    clear_rows(block)
    block[1 : rows + 1] = grad[...]
    columns = jnp.concatenate(
        [block[2 - p : 2 - p + rows].reshape(rows * wide, width) for p in range(3)], axis=1
    )
    total = None
    for q in range(3):
        taps = jnp.concatenate([weight[3 * p + q] for p in range(3)], axis=0)
        part = shift(matmul(columns, taps), q - 1)
        total = part if total is None else total + part
    result[...] = total.reshape(rows, wide, 2 * width)
    keep[...] = result[:, EDGE : EDGE + length, pl.ds(lane_own, width)]
    send[...] = result[:, EDGE : EDGE + length, pl.ds(lane_oth, width)].astype(BF16)


def run_kernel(kernel, outs, scratch, flops, *args, fetch=False):
    moved = sum(math.prod(shape) * jnp.dtype(kind).itemsize for shape, kind in outs)
    moved += sum(arg.size * arg.dtype.itemsize for arg in args)
    space = pltpu.HBM if fetch else pltpu.VMEM
    if fetch:
        args = [pltpu.with_memory_space_constraint(arg, pltpu.HBM) for arg in args]
    sems = [pltpu.SemaphoreType.DMA((4,))] if fetch else []
    return pl.pallas_call(
        kernel,
        cost_estimate=pl.CostEstimate(flops=flops, transcendentals=0, bytes_accessed=moved),
        out_shape=[jax.ShapeDtypeStruct(shape, kind) for shape, kind in outs],
        in_specs=[pl.BlockSpec(memory_space=space)] * len(args),
        out_specs=[pl.BlockSpec(memory_space=pltpu.VMEM)] * len(outs),
        scratch_shapes=[pltpu.VMEM(shape, kind) for shape, kind in scratch] + sems,
        compiler_params=PARAMS,
    )(*args)


def after(values, *others):
    return lax.optimization_barrier((values, *others))[0]


def split_half(values, upper):
    half = values.shape[1] // 2
    low, high = values[:, :half], values[:, half:]
    return jnp.where(upper, high, low), jnp.where(upper, low, high).astype(BF16)


def reduce_space(keep, send, count, steps, upper, others=None):
    sent = []
    for number, step in enumerate(steps[:-1]):
        sent.append(send)
        got = lax.ppermute(send, "space", swap_pairs(count, step))
        if others is not None:
            got = after(got, *others[number])
        values = keep + got.astype(F32)
        if number + 2 < len(steps):
            keep, send = split_half(values, upper[steps[number + 1]])
    mine = values.astype(BF16)
    sent.append(mine)
    got = lax.ppermute(mine, "space", swap_pairs(count, steps[-1]))
    if others is not None:
        got = after(got, *others[-1])
    return (mine.astype(F32) + got.astype(F32)).astype(BF16), sent


def gather_space(values, count, steps, upper):
    for step in reversed(steps[:-1]):
        got = lax.ppermute(values, "space", swap_pairs(count, step))
        values = jnp.concatenate(
            [
                jnp.where(upper[step], got, values),
                jnp.where(upper[step], values, got),
            ],
            axis=1,
        )
    return values.astype(F32).transpose(1, 0, 2)


def in_order(second, mine, theirs, axis):
    return jnp.concatenate(
        [jnp.where(second, theirs, mine), jnp.where(second, mine, theirs)], axis=axis
    )


def on_device(field, first_weight, second_weight, cotangent):
    width, rows, length = field.shape
    wide = length + 2 * EDGE
    count = lax.axis_size("space")
    scale = 1.0 / math.sqrt(rows * length * count)
    steps = [1 << b for b in range(count.bit_length() - 1)]
    bits = [(lax.axis_index("space") & step) != 0 for step in steps]
    field, second_part, *bits = lax.optimization_barrier(
        (field, lax.axis_index("chan") != 0, *bits)
    )
    upper = dict(zip(steps, bits))
    half = width // 2
    chan_swap = swap_pairs(2, 1)
    forward = [(i, (i + 1) % count) for i in range(count)]
    backward = [(target, source) for source, target in forward]

    block = (rows, length, width), BF16
    edge = (2, rows, SENT, width), BF16
    part = width // SHARES
    packed, field_own, cot_own, cot_flat, last, first, weight_own = run_kernel(
        prepare_kernel,
        [
            ((rows * length // part + 9, part, width), BF16),
            block, block, ((width, rows * length), BF16), edge, edge, ((9, width, width), BF16),
        ],
        [((2, width, rows, length), BF16), ((width * rows, length), F32)],
        0,
        field, cotangent, second_weight.transpose(1, 0, 2),
        fetch=True,
    )
    packed = lax.ppermute(packed, "chan", chan_swap)
    low = lax.ppermute(last, "space", forward)
    high = lax.ppermute(first, "space", backward)
    both = jnp.stack([low, high])
    sides = lax.ppermute(both, "chan", chan_swap)
    cot_oth = lax.ppermute(after(cot_own, low, high), "chan", chan_swap)
    weight_part = after(packed[-9:], sides)
    weight_next = lax.ppermute(weight_part, "space", swap_pairs(count, 2))
    first_taps = first_weight.transpose(1, 0, 2)

    conv_flops = 2 * rows * wide * 2 * width * 9 * width
    sums_flops = 2 * rows * length * 2 * width * 9 * width
    padded = (rows + 2, length, 2 * width), BF16
    slopes, field_rows, smooth, sums_own = run_kernel(
        functools.partial(forward_kernel, scale),
        [
            ((4, rows, wide, width), F32), padded,
            ((rows * length, 9 * width), BF16), ((width, 9 * width), F32),
        ],
        [((rows + 2, wide, 2 * width), BF16), ((rows, wide, width), F32)],
        2 * conv_flops + sums_flops // 2,
        field_own, packed, both, sides, first_taps, cot_flat,
    )
    weight_pair = jnp.stack([weight_part, after(weight_next, sums_own)])
    weight_rest = lax.ppermute(weight_pair, "space", swap_pairs(count, 1))
    second_keep, second_send = run_kernel(
        functools.partial(second_kernel, scale),
        [((18, half, width), F32), ((18, half, width), BF16)],
        [((width, rows * length), BF16), ((width, 9 * width), F32)],
        sums_flops // 2,
        sums_own, cot_oth, smooth,
    )
    hidden_grad, first_keep, first_send = run_kernel(
        functools.partial(backward_kernel, scale),
        [((rows, wide, width), BF16), ((9, half, 2 * width), F32), ((9, half, 2 * width), BF16)],
        [
            ((rows + 2, wide, 2 * width), BF16),
            ((3 * width, rows * length), BF16),
            ((3 * width, 2 * width), F32),
            ((rows, wide, width), F32),
            ((9, width, width), BF16),
        ],
        2 * conv_flops + sums_flops,
        cot_own, cot_oth, both, sides, weight_own, weight_pair, weight_rest, slopes, field_rows,
    )

    first_steps = steps[:1] + steps[2:-1] + steps[1:2] + steps[-1:] if count >= 8 else steps
    first_piece, sent = reduce_space(first_keep, first_send, count, first_steps, upper)

    field_keep, field_send = run_kernel(
        spread_kernel,
        [((rows, length, width), F32), ((rows, length, width), BF16)],
        [((rows + 2, wide, width), BF16), ((rows, wide, 2 * width), F32)],
        conv_flops,
        after(hidden_grad, sent[1]), first_taps,
    )
    field_got = lax.ppermute(field_send, "chan", chan_swap)
    field_sum = field_keep + after(field_got, sent[-1]).astype(F32)
    field_grad = (cot_own.astype(F32) + field_sum).astype(BF16).transpose(2, 0, 1)

    others = [(value,) for value in sent]
    others[1] += (field_send,)
    others[-1] += (field_grad,)
    second_piece, _ = reduce_space(second_keep, second_send, count, steps, upper, others)
    second_got = lax.ppermute(second_piece[9:], "chan", chan_swap)
    second_piece = in_order(second_part, second_piece[:9], second_got, 2)
    first_grad = gather_space(first_piece, count, first_steps, upper)
    second_grad = gather_space(second_piece, count, steps, upper)
    return (field_grad, first_grad, second_grad)


HALO = 3


def with_halo(block, width):
    count = lax.axis_size("space")
    forward = [(i, (i + 1) % count) for i in range(count)]
    backward = [(target, source) for source, target in forward]
    low = lax.ppermute(block[..., -width:], "space", forward)
    high = lax.ppermute(block[..., :width], "space", backward)
    return jnp.concatenate([low, block, high], axis=-1)


def pad_rows(values):
    return jnp.pad(values, ((0, 0), (1, 1), (0, 0)))


def collect(values):
    return lax.all_gather(values, "chan", axis=0, tiled=True)


def conv_forward(padded, weight):
    height = padded.shape[1] - 2
    length = padded.shape[2] - 2
    total = jnp.zeros((weight.shape[0], height, length), jnp.float32)
    for tap_row in range(3):
        for tap_col in range(3):
            window = padded[:, tap_row : tap_row + height, tap_col : tap_col + length]
            total = total + jnp.einsum(
                "oi,irc->orc",
                weight[:, 3 * tap_row + tap_col, :],
                window,
                preferred_element_type=jnp.float32,
            )
    return total


def conv_back(padded, weight):
    height = padded.shape[1] - 2
    length = padded.shape[2] - 2
    total = jnp.zeros((weight.shape[2], height, length), jnp.float32)
    for tap_row in range(3):
        for tap_col in range(3):
            window = padded[
                :, 2 - tap_row : 2 - tap_row + height, 2 - tap_col : 2 - tap_col + length
            ]
            total = total + jnp.einsum(
                "oi,orc->irc",
                weight[:, 3 * tap_row + tap_col, :],
                window,
                preferred_element_type=jnp.float32,
            )
    return total


def reduce_back(padded, weight):
    return lax.psum_scatter(conv_back(padded, weight), "chan", scatter_dimension=0, tiled=True)


def weight_grad(upstream, padded):
    height = upstream.shape[1]
    length = upstream.shape[2]
    pieces = []
    for tap_row in range(3):
        for tap_col in range(3):
            window = padded[:, tap_row : tap_row + height, tap_col : tap_col + length]
            pieces.append(
                jnp.einsum("orc,irc->oi", upstream, window, preferred_element_type=jnp.float32)
            )
    return jnp.stack(pieces, axis=0)


def smooth_gelu(values):
    return jax.nn.gelu(values, approximate=True)


def resample(extended):
    lower = jnp.pad(extended, ((0, 0), (0, 1), (0, 0)))
    top_left = lower[:, :-1, :-1]
    top_right = lower[:, :-1, 1:]
    low_left = lower[:, 1:, :-1]
    low_right = lower[:, 1:, 1:]
    even_even = smooth_gelu(top_left)
    even_odd = smooth_gelu((top_left + top_right) * 0.5)
    odd_even = smooth_gelu((top_left + low_left) * 0.5)
    odd_odd = smooth_gelu((top_left + top_right + low_left + low_right) * 0.25)
    row_even = (even_odd[:, :, :-1] + 2.0 * even_even[:, :, 1:] + even_odd[:, :, 1:]) * 0.25
    row_odd = (odd_odd[:, :, :-1] + 2.0 * odd_even[:, :, 1:] + odd_odd[:, :, 1:]) * 0.25
    shifted = jnp.pad(row_odd, ((0, 0), (1, 0), (0, 0)))[:, :-1]
    return (shifted + 2.0 * row_even + row_odd) * 0.25


def sum_over_space(values):
    count = lax.axis_size("space")
    place = lax.axis_index("space")
    steps = [1 << b for b in range(count.bit_length() - 1)]
    for step in steps:
        half = values.shape[1] // 2
        upper = (place & step) != 0
        low, high = values[:, :half], values[:, half:]
        sent = jnp.where(upper, low, high).astype(jnp.bfloat16)
        got = lax.ppermute(sent, "space", swap_pairs(count, step))
        values = jnp.where(upper, high, low) + got.astype(jnp.float32)
    values = values.astype(jnp.bfloat16)
    for step in reversed(steps):
        upper = (place & step) != 0
        got = lax.ppermute(values, "space", swap_pairs(count, step))
        values = jnp.concatenate(
            [jnp.where(upper, got, values), jnp.where(upper, values, got)], axis=1
        )
    return values.astype(jnp.float32).transpose(1, 0, 2)


def on_device_parts(field, first_weight, second_weight, cotangent):
    height = field.shape[1]
    length = field.shape[2]
    grad_scale = 1.0 / math.sqrt(height * length * lax.axis_size("space"))
    both = with_halo(jnp.concatenate([field, cotangent], axis=0), HALO)
    field_wide, cot_wide = jnp.split(both, 2, axis=0)
    field_all = collect(field_wide)
    field_pad = pad_rows(field_all)
    hidden = conv_forward(field_pad, first_weight).astype(jnp.bfloat16)
    smooth_sum = reduce_back(pad_rows(cot_wide), second_weight)
    smooth_grad = smooth_sum.astype(jnp.bfloat16)
    smooth = resample(hidden.astype(jnp.float32)).astype(jnp.bfloat16)
    smooth_all = collect(smooth)
    second_grad = weight_grad(cotangent, pad_rows(smooth_all)) * grad_scale
    wide_grad = smooth_grad.astype(jnp.float32)
    _, pull_wide = jax.vjp(
        resample, jnp.pad(hidden.astype(jnp.float32), ((0, 0), (0, 0), (1, 1)))
    )
    hidden_grad = pull_wide(wide_grad)[0][:, :, 2:-2].astype(jnp.bfloat16)
    first_grad = weight_grad(hidden_grad[:, :, 1:-1], field_pad[:, :, 2:-2]) * grad_scale
    field_sum = reduce_back(pad_rows(hidden_grad), first_weight)
    field_grad = (cotangent.astype(jnp.float32) + field_sum).astype(jnp.bfloat16)
    return (field_grad, sum_over_space(first_grad), sum_over_space(second_grad))


def solution(mesh):
    in_specs = (
        P("chan", None, "space"),
        P("chan", None, None),
        P("chan", None, None),
        P("chan", None, "space"),
    )
    out_specs = (P("chan", None, "space"), P("chan", None, None), P("chan", None, None))
    body = on_device if mesh.shape["chan"] == 2 else on_device_parts
    return jax.shard_map(
        body, mesh=mesh, in_specs=in_specs, out_specs=out_specs, check_vma=False
    )
```

time: 225 us -> 60.2 us (0.27)
  waiting for transfers between devices: 127 us -> 17.6 us
  matrix products: 23.2 us -> 0 us
  blocking collectives: 14.6 us -> 0 us
  between operations: 14.3 us -> 0.9 us
  Pallas kernels: 0 us -> 10.3 us
  local copies, waits for them, and re-layouts: 8.19 us -> 0.9 us
  other arithmetic: 9.29 us -> 3.35 us
    psum x1 -> x0, waiting for transfers between devices: 101 us -> none  [on_device(): first_grad, second_grad = lax.psum((first_grad, second_grad), 'space')]
    dot_general x45 -> x0, matrix products: 23.2 us -> none  [the longest x18 14.7 us: conv_back(): jnp.einsum('oi,orc->irc', weight[:, 3 * tap_row + tap_col, :], window, pr...]
    reduce_scatter x2 -> x0, waiting for transfers between devices: 22.8 us -> none  [reduce_back(): lax.psum_scatter(conv_back(padded, weight), 'chan', scatter_dimension=0,...]
    ppermute x12 -> x23, waiting for transfers between devices: 2.47 us -> 17.6 us  [the longest x6 6.7 us: gather_space(): got = lax.ppermute(values, 'space', swap_pairs(count, step))]
    all_gather x2 -> x0, blocking collectives: 14.6 us -> none  [collect(): return lax.all_gather(values, 'chan', axis=0, tiled=True)]
    pallas_call x0 -> x5, Pallas kernels: none -> 10.3 us  [run_kernel(): pl.pallas_call(kernel, cost_estimate=pl.CostEstimate(flops=flops, transce...]
    unnamed x15 -> x3, local copies, waits for them, and re-layouts: 7.72 us -> 0.89 us
    mul x6 -> x0, other arithmetic: 4.04 us -> none  [the longest x1 1.43 us: smooth_gelu(): return jax.nn.gelu(values, approximate=True)]
  transfers between devices with their start and end apart: 15 -> 23, of which waited for: 5 -> 14; matrix products, arithmetic and copies ran while one was open for 10% -> 5% of each run, Pallas kernels for 0% -> 15%
where the time goes in v1:
time: 60.2 us; the launch traced here: 60.1 us
  starting transfers between devices  27.1 us (45%)
  waiting for transfers between devices  17.6 us (29%)
  Pallas kernels  10.3 us (17%)
  other arithmetic  3.35 us (6%)
  local copies, waits for them, and re-layouts  0.9 us (1%)
  between operations  0.9 us (1%)
    pallas_call x5, Pallas kernels, run_kernel(): pl.pallas_call(kernel, cost_estimate=pl.CostEstimate(flops=flops, transce...  10.3 us
    ppermute x6, waiting for transfers between devices, gather_space(): got = lax.ppermute(values, 'space', swap_pairs(count, step))  6.7 us
    ppermute x6, starting transfers between devices, reduce_space(): got = lax.ppermute(send, 'space', swap_pairs(count, step))  5.57 us
    ppermute x1, starting transfers between devices, on_device(): high = lax.ppermute(first, 'space', backward)  4.44 us
    ppermute x6, starting transfers between devices, gather_space(): got = lax.ppermute(values, 'space', swap_pairs(count, step))  4.42 us
    ppermute x2, starting transfers between devices, reduce_space(): got = lax.ppermute(mine, 'space', swap_pairs(count, steps[-1]))  4.2 us
    ppermute x1, starting transfers between devices, on_device(): packed = lax.ppermute(packed, 'chan', chan_swap)  3.03 us
    ppermute x2, waiting for transfers between devices, reduce_space(): got = lax.ppermute(mine, 'space', swap_pairs(count, steps[-1]))  2.94 us
  transfers between devices with their start and end apart: 23, of which 14 were waited for; matrix products, arithmetic and copies ran while one was open for 5% of the time, Pallas kernels for 15%

profile of v1, /device:TPU:0, one launch (start us, length us, event | category | flops | bytes accessed | tf_op | source)
XLA Modules:
  0.0 60.1 jit_solution(5836924865817757820)
XLA Ops:
  0.7 1.4 %shard_map.67 = (bf16[41,32,128]{2,1,0:T(8,128)(2,1)S(1)}, bf16[8,128,128]{2,1,0:T(8,128)(2,1)S(1)}, bf16[8,128,128]{2,1,0:T(8,128)(2,1)S(1)}, bf16[128,1024]{1,...) custom-call(bf16[128,8,128]{2,1,0:T(8,128)(2,1)} %field, ...), custom_call_target="tpu_custom_call" | custom-call | bytes 2564096 | tf_op jit(solution)/shard_map/pallas_call | solution.py:269
  2.1 3.0 %collective-permute-start.4 = (bf16[41,32,128]{2,1,0:T(8,128)(2,1)S(1)}, bf16[41,32,128]{2,1,0:T(8,128)(2,1)S(1)}, u32[]{:S(2)}, u32[]{:S(2)}) collective-permute-start(bf16[41,32,128]{2,1,0:T(8,128)(2,1)S(1)} %get-tuple-element.41), channel_id=1, source_target_pairs={{0,1},{1,0},{2,3},{3,2},{4,5},{5,4},{6,7},{7,6},{8,9},{9,8},{10,11... | collective-permute-start | bytes 1007624 | tf_op jit(solution)/shard_map/ppermute | solution.py:357
  5.1 4.4 %collective-permute-start.1 = (bf16[2,8,4,128]{3,2,1,0:T(4,128)(2,1)S(1)}, bf16[2,8,4,128]{3,2,1,0:T(4,128)(2,1)S(1)}, u32[]{:S(2)}, u32[]{:S(2)}) collective-permute-start(bf16[2,8,4,128]{3,2,1,0:T(4,128)(2,1)S(1)} %get-tuple-element.38), channel_id=1, source_target_pairs={{2,0},{4,2},{6,4},{8,6},{10,8},{12,10},{14,12},{16,14},{18,16},{20... | collective-permute-start | bytes 49160 | tf_op jit(solution)/shard_map/ppermute | solution.py:359
  9.6 1.4 %collective-permute-done = bf16[2,8,4,128]{3,2,1,0:T(4,128)(2,1)S(1)} collective-permute-done((bf16[2,8,4,128]{3,2,1,0:T(4,128)(2,1)S(1)}, bf16[2,8,4,128]{3,2,1,0:T(4,128)(2,1)S(1)}, u32[]{:S(2)}, u32[]{:S(2)}) %collective-permute-start) | collective-permute-done | bytes 16416 | tf_op jit(solution)/shard_map/ppermute | solution.py:358
  11.2 2.0 %collective-permute-start.2 = (bf16[8,128,128]{2,1,0:T(8,128)(2,1)S(1)}, bf16[8,128,128]{2,1,0:T(8,128)(2,1)S(1)}, u32[]{:S(2)}, u32[]{:S(2)}) collective-permute-start(bf16[8,128,128]{2,1,0:T(8,128)(2,1)S(1)} %get-tuple-element.39.cot_own), channel_id=1, source_target_pairs={{0,1},{1,0},{2,3},{3,2},{4,5},{5,4},{6,7},{7,6},{8,9},{9,8},{10,11... | collective-permute-start | bytes 786440 | tf_op jit(solution)/shard_map/ppermute | solution.py:362
  13.1 2.3 %collective-permute-done.3.sides = bf16[2,2,8,4,128]{4,3,2,1,0:T(4,128)(2,1)S(1)} collective-permute-done((bf16[2,2,8,4,128]{4,3,2,1,0:T(4,128)(2,1)S(1)}, bf16[2,2,8,4,128]{4,3,2,1,0:T(4,128)(2,1)S(1)}, u32[]{:S(2)}, u32[]{:S(2)}) %collective-permute-start.3) | collective-permute-done | bytes 32800 | tf_op jit(solution)/shard_map/ppermute | solution.py:361
  15.4 3.9 %shard_map.68 = (f32[4,8,144,128]{3,2,1,0:T(8,128)S(1)}, bf16[10,128,256]{2,1,0:T(8,128)(2,1)S(1)}, bf16[1024,1152]{1,0:T(8,128)(2,1)S(1)}, f32[128,1152]{1,0:T(8,128)S(1)}) custom-call(bf16[8,128,128]{2,1,0:T(8,128)(2,1)S(1)} %get-tuple-element.43.own, bf16[41,32,128]{2,1,0:T(8,128)(2,1)S(1)} %collective-permute-done.4.packed, ...), custom_call_target="tpu_custom_call" | custom-call | flops 1660944384 | bytes 7479296 | tf_op jit(solution)/shard_map/pallas_call | solution.py:269
  19.9 0.6 %shard_map.71 = (f32[18,64,128]{2,1,0:T(8,128)S(1)}, bf16[18,64,128]{2,1,0:T(8,128)(2,1)S(1)}) custom-call(f32[128,1152]{1,0:T(8,128)S(1)} %get-tuple-element.45.sums_own, bf16[8,128,128]{2,1,0:T(8,128)(2,1)S(1)} %collective-permute-done.2.cot_oth, bf16[1024,1152]{1,0:T(8,128)(2,1)S(1)} %get-tuple-element.60.smooth), custom_call_target="tpu_custom_call" | custom-call | flops 301989888 | bytes 4096000 | tf_op jit(solution)/shard_map/pallas_call | solution.py:269
  21.2 2.9 %shard_map.69 = (bf16[8,144,128]{2,1,0:T(8,128)(2,1)S(1)}, f32[9,64,256]{2,1,0:T(8,128)S(1)}, bf16[9,64,256]{2,1,0:T(8,128)(2,1)S(1)}) custom-call(bf16[8,128,128]{2,1,0:T(8,128)(2,1)S(1)} %get-tuple-element.39.cot_own, bf16[8,128,128]{2,1,0:T(8,128)(2,1)S(1)} %collective-permute-done.2.cot_oth, bf16[2,2,8,4,128]{4,3,2,1,0:T(4,128)(2,1)S(1)} %pad_maximum_fusion.6.both, ...), custom_call_target="tpu_custom_call" | custom-call | flops 1962934272 | bytes 5373952 | tf_op jit(solution)/shard_map/pallas_call | solution.py:269
  24.5 1.7 %collective-permute-start.16 = (bf16[18,32,128]{2,1,0:T(8,128)(2,1)S(1)}, bf16[18,32,128]{2,1,0:T(8,128)(2,1)S(1)}, u32[]{:S(2)}, u32[]{:S(2)}) collective-permute-start(bf16[18,32,128]{2,1,0:T(8,128)(2,1)S(1)} %select_convert_fusion), channel_id=1, source_target_pairs={{0,4},{2,6},{4,0},{6,2},{8,12},{10,14},{12,8},{14,10},{16,20},{18,... | collective-permute-start | bytes 442376 | tf_op jit(solution)/shard_map/ppermute | solution.py:294
  26.3 0.7 %collective-permute-start.9 = (bf16[9,32,256]{2,1,0:T(8,128)(2,1)S(1)}, bf16[9,32,256]{2,1,0:T(8,128)(2,1)S(1)}, u32[]{:S(2)}, u32[]{:S(2)}) collective-permute-start(bf16[9,32,256]{2,1,0:T(8,128)(2,1)S(1)} %select_convert_fusion.1), channel_id=1, source_target_pairs={{0,8},{2,10},{4,12},{6,14},{8,0},{10,2},{12,4},{14,6},{16,24},{18,... | collective-permute-start | bytes 442376 | tf_op jit(solution)/shard_map/ppermute | solution.py:294
  27.0 1.4 %shard_map.70 = (f32[8,128,128]{2,1,0:T(8,128)S(1)}, bf16[8,128,128]{2,1,0:T(8,128)(2,1)S(1)}) custom-call(bf16[8,144,128]{2,1,0:T(8,128)(2,1)S(1)} %get-tuple-element.53.grad, bf16[9,128,256]{2,1,0:T(8,128)(2,1)S(1)} %bitcast.13), custom_call_target="tpu_custom_call" | custom-call | flops 679477248 | bytes 1671168 | tf_op jit(solution)/shard_map/pallas_call | solution.py:269
  28.4 1.8 %collective-permute-start.8 = (bf16[8,128,128]{2,1,0:T(8,128)(2,1)S(1)}, bf16[8,128,128]{2,1,0:T(8,128)(2,1)S(1)}, u32[]{:S(2)}, u32[]{:S(2)}) collective-permute-start(bf16[8,128,128]{2,1,0:T(8,128)(2,1)S(1)} %get-tuple-element.55), channel_id=1, source_target_pairs={{0,1},{1,0},{2,3},{3,2},{4,5},{5,4},{6,7},{7,6},{8,9},{9,8},{10,11... | collective-permute-start | bytes 786440 | tf_op jit(solution)/shard_map/ppermute | solution.py:413
  30.8 1.1 %collective-permute-start.17 = (bf16[18,16,128]{2,1,0:T(8,128)(2,1)S(1)}, bf16[18,16,128]{2,1,0:T(8,128)(2,1)S(1)}, u32[]{:S(2)}, u32[]{:S(2)}) collective-permute-start(bf16[18,16,128]{2,1,0:T(8,128)(2,1)S(1)} %select_convert_fusion.2), channel_id=1, source_target_pairs={{0,8},{2,10},{4,12},{6,14},{8,0},{10,2},{12,4},{14,6},{16,24},{18,... | collective-permute-start | bytes 221192 | tf_op jit(solution)/shard_map/ppermute | solution.py:294
  32.2 1.4 %collective-permute-start.10 = (bf16[9,16,256]{2,1,0:T(8,128)(2,1)S(1)}, bf16[9,16,256]{2,1,0:T(8,128)(2,1)S(1)}, u32[]{:S(2)}, u32[]{:S(2)}) collective-permute-start(bf16[9,16,256]{2,1,0:T(8,128)(2,1)S(1)} %select_convert_fusion.3), channel_id=1, source_target_pairs={{0,4},{2,6},{4,0},{6,2},{8,12},{10,14},{12,8},{14,10},{16,20},{18,... | collective-permute-start | bytes 221192 | tf_op jit(solution)/shard_map/ppermute | solution.py:294
  33.6 1.6 %collective-permute-done.17 = bf16[18,16,128]{2,1,0:T(8,128)(2,1)S(1)} collective-permute-done((bf16[18,16,128]{2,1,0:T(8,128)(2,1)S(1)}, bf16[18,16,128]{2,1,0:T(8,128)(2,1)S(1)}, u32[]{:S(2)}, u32[]{:S(2)}) %collective-permute-start.17) | collective-permute-done | bytes 73760 | tf_op jit(solution)/shard_map/ppermute | solution.py:294
  35.2 2.2 %collective-permute-start.18 = (bf16[18,16,128]{2,1,0:T(8,128)(2,1)S(1)}, bf16[18,16,128]{2,1,0:T(8,128)(2,1)S(1)}, u32[]{:S(2)}, u32[]{:S(2)}) collective-permute-start(bf16[18,16,128]{2,1,0:T(8,128)(2,1)S(1)} %add_convert_fusion.2), channel_id=1, source_target_pairs={{0,16},{2,18},{4,20},{6,22},{8,24},{10,26},{12,28},{14,30},{16,0},... | collective-permute-start | bytes 221192 | tf_op jit(solution)/shard_map/ppermute | solution.py:302
  37.4 2.0 %collective-permute-start.11 = (bf16[9,16,256]{2,1,0:T(8,128)(2,1)S(1)}, bf16[9,16,256]{2,1,0:T(8,128)(2,1)S(1)}, u32[]{:S(2)}, u32[]{:S(2)}) collective-permute-start(bf16[9,16,256]{2,1,0:T(8,128)(2,1)S(1)} %add_convert_fusion.4), channel_id=1, source_target_pairs={{0,16},{2,18},{4,20},{6,22},{8,24},{10,26},{12,28},{14,30},{16,0},... | collective-permute-start | bytes 221192 | tf_op jit(solution)/shard_map/ppermute | solution.py:302
  39.6 2.9 %collective-permute-done.18 = bf16[18,16,128]{2,1,0:T(8,128)(2,1)S(1)} collective-permute-done((bf16[18,16,128]{2,1,0:T(8,128)(2,1)S(1)}, bf16[18,16,128]{2,1,0:T(8,128)(2,1)S(1)}, u32[]{:S(2)}, u32[]{:S(2)}) %collective-permute-start.18) | collective-permute-done | bytes 73760 | tf_op jit(solution)/shard_map/ppermute | solution.py:302
  42.5 0.9 %copy.7 = bf16[128,8,128]{2,1,0:T(8,128)(2,1)} copy(bf16[128,8,128]{0,2,1:T(8,128)(2,1)S(1)} %fusion) | data formatting | bytes 524288
  43.4 1.4 %collective-permute-start.19 = (bf16[9,16,128]{2,1,0:T(8,128)(2,1)S(1)}, bf16[9,16,128]{2,1,0:T(8,128)(2,1)S(1)}, u32[]{:S(2)}, u32[]{:S(2)}) collective-permute-start(bf16[9,16,128]{2,1,0:T(8,128)(2,1)S(1)} %slice.53), channel_id=1, source_target_pairs={{0,1},{1,0},{2,3},{3,2},{4,5},{5,4},{6,7},{7,6},{8,9},{9,8},{10,11... | collective-permute-start | bytes 110600 | tf_op jit(solution)/shard_map/ppermute | solution.py:421
  44.9 1.3 %collective-permute-start.12 = (bf16[9,16,256]{2,1,0:T(8,128)(2,1)S(1)}, bf16[9,16,256]{2,1,0:T(8,128)(2,1)S(1)}, u32[]{:S(2)}, u32[]{:S(2)}) collective-permute-start(bf16[9,16,256]{2,1,0:T(8,128)(2,1)S(1)} %add_convert_fusion.3), channel_id=1, source_target_pairs={{0,4},{2,6},{4,0},{6,2},{8,12},{10,14},{12,8},{14,10},{16,20},{18,... | collective-permute-start | bytes 221192 | tf_op jit(solution)/shard_map/ppermute | solution.py:310
  46.2 1.2 %collective-permute-done.19 = bf16[9,16,128]{2,1,0:T(8,128)(2,1)S(1)} collective-permute-done((bf16[9,16,128]{2,1,0:T(8,128)(2,1)S(1)}, bf16[9,16,128]{2,1,0:T(8,128)(2,1)S(1)}, u32[]{:S(2)}, u32[]{:S(2)}) %collective-permute-start.19) | collective-permute-done | bytes 36896 | tf_op jit(solution)/shard_map/ppermute | solution.py:421
  47.4 1.0 %collective-permute-start.20 = (bf16[9,16,256]{2,1,0:T(8,128)(2,1)S(1)}, bf16[9,16,256]{2,1,0:T(8,128)(2,1)S(1)}, u32[]{:S(2)}, u32[]{:S(2)}) collective-permute-start(bf16[9,16,256]{2,1,0:T(8,128)(2,1)S(1)} %pad_maximum_fusion.5), channel_id=1, source_target_pairs={{0,8},{2,10},{4,12},{6,14},{8,0},{10,2},{12,4},{14,6},{16,24},{18,... | collective-permute-start | bytes 221192 | tf_op jit(solution)/shard_map/ppermute | solution.py:310
  48.4 1.1 %collective-permute-done.12 = bf16[9,16,256]{2,1,0:T(8,128)(2,1)S(1)} collective-permute-done((bf16[9,16,256]{2,1,0:T(8,128)(2,1)S(1)}, bf16[9,16,256]{2,1,0:T(8,128)(2,1)S(1)}, u32[]{:S(2)}, u32[]{:S(2)}) %collective-permute-start.12) | collective-permute-done | bytes 73760 | tf_op jit(solution)/shard_map/ppermute | solution.py:310
  49.5 0.6 %collective-permute-start.13 = (bf16[9,32,256]{2,1,0:T(8,128)(2,1)S(1)}, bf16[9,32,256]{2,1,0:T(8,128)(2,1)S(1)}, u32[]{:S(2)}, u32[]{:S(2)}) collective-permute-start(bf16[9,32,256]{2,1,0:T(8,128)(2,1)S(1)} %pad_maximum_fusion.3), channel_id=1, source_target_pairs={{0,8},{2,10},{4,12},{6,14},{8,0},{10,2},{12,4},{14,6},{16,24},{18,... | collective-permute-start | bytes 442376 | tf_op jit(solution)/shard_map/ppermute | solution.py:310
  50.2 1.7 %collective-permute-done.20 = bf16[9,16,256]{2,1,0:T(8,128)(2,1)S(1)} collective-permute-done((bf16[9,16,256]{2,1,0:T(8,128)(2,1)S(1)}, bf16[9,16,256]{2,1,0:T(8,128)(2,1)S(1)}, u32[]{:S(2)}, u32[]{:S(2)}) %collective-permute-start.20) | collective-permute-done | bytes 73760 | tf_op jit(solution)/shard_map/ppermute | solution.py:310
  51.9 1.4 %collective-permute-start.21 = (bf16[9,32,256]{2,1,0:T(8,128)(2,1)S(1)}, bf16[9,32,256]{2,1,0:T(8,128)(2,1)S(1)}, u32[]{:S(2)}, u32[]{:S(2)}) collective-permute-start(bf16[9,32,256]{2,1,0:T(8,128)(2,1)S(1)} %pad_maximum_fusion.4), channel_id=1, source_target_pairs={{0,4},{2,6},{4,0},{6,2},{8,12},{10,14},{12,8},{14,10},{16,20},{18,... | collective-permute-start | bytes 442376 | tf_op jit(solution)/shard_map/ppermute | solution.py:310
  53.3 1.5 %collective-permute-done.13 = bf16[9,32,256]{2,1,0:T(8,128)(2,1)S(1)} collective-permute-done((bf16[9,32,256]{2,1,0:T(8,128)(2,1)S(1)}, bf16[9,32,256]{2,1,0:T(8,128)(2,1)S(1)}, u32[]{:S(2)}, u32[]{:S(2)}) %collective-permute-start.13) | collective-permute-done | bytes 147488 | tf_op jit(solution)/shard_map/ppermute | solution.py:310
  54.9 2.2 %collective-permute-done.21 = bf16[9,32,256]{2,1,0:T(8,128)(2,1)S(1)} collective-permute-done((bf16[9,32,256]{2,1,0:T(8,128)(2,1)S(1)}, bf16[9,32,256]{2,1,0:T(8,128)(2,1)S(1)}, u32[]{:S(2)}, u32[]{:S(2)}) %collective-permute-start.21) | collective-permute-done | bytes 147488 | tf_op jit(solution)/shard_map/ppermute | solution.py:310
  57.4 1.1 %convert_bitcast_fusion.1 = f32[128,9,256]{2,0,1:T(8,128)} fusion(bf16[9,64,256]{2,1,0:T(8,128)(2,1)S(1)} %get-tuple-element.73, bf16[9,64,256]{2,1,0:T(8,128)(2,1)S(1)} %get-tuple-element.72), kind=kLoop, calls=%fused_computation.1 | loop fusion | flops 1179648 | bytes 1769472 | tf_op jit(solution)/shard_map/transpose | solution.py:318
  59.0 1.1 %convert_bitcast_fusion = f32[128,9,256]{2,0,1:T(8,128)} fusion(bf16[9,64,256]{2,1,0:T(8,128)(2,1)S(1)} %get-tuple-element.71, bf16[9,64,256]{2,1,0:T(8,128)(2,1)S(1)} %get-tuple-element.70), kind=kLoop, calls=%fused_computation | loop fusion | flops 1179648 | bytes 1769472 | tf_op jit(solution)/shard_map/transpose | solution.py:318
  (53 shorter events, 4.0 us)
Async XLA Ops:
  0.6 14.8 %copy-start = (bf16[128,9,256]{2,0,1:T(8,128)(2,1)S(1)}, bf16[128,9,256]{2,0,1:T(8,128)(2,1)}, u32[]{:S(2)}) copy-start(bf16[128,9,256]{2,0,1:T(8,128)(2,1)} %param.5) | copy-start | bytes 1769476
  2.1 11.0 %collective-permute-start.4 = (bf16[41,32,128]{2,1,0:T(8,128)(2,1)S(1)}, bf16[41,32,128]{2,1,0:T(8,128)(2,1)S(1)}, u32[]{:S(2)}, u32[]{:S(2)}) collective-permute-start(bf16[41,32,128]{2,1,0:T(8,128)(2,1)S(1)} %get-tuple-element.41), channel_id=1, source_target_pairs={{0,1},{1,0},{2,3},{3,2},{4,5},{5,4},{6,7},{7,6},{8,9},{9,8},{10,11... | collective-permute-start | bytes 1007624 | tf_op jit(solution)/shard_map/ppermute | solution.py:357
  5.1 5.9 %collective-permute-start = (bf16[2,8,4,128]{3,2,1,0:T(4,128)(2,1)S(1)}, bf16[2,8,4,128]{3,2,1,0:T(4,128)(2,1)S(1)}, u32[]{:S(2)}, u32[]{:S(2)}) collective-permute-start(bf16[2,8,4,128]{3,2,1,0:T(4,128)(2,1)S(1)} %get-tuple-element.37), channel_id=1, source_target_pairs={{0,2},{2,4},{4,6},{6,8},{8,10},{10,12},{12,14},{14,16},{16,18},{18... | collective-permute-start | bytes 49160 | tf_op jit(solution)/shard_map/ppermute | solution.py:358
  5.1 5.9 %collective-permute-start.1 = (bf16[2,8,4,128]{3,2,1,0:T(4,128)(2,1)S(1)}, bf16[2,8,4,128]{3,2,1,0:T(4,128)(2,1)S(1)}, u32[]{:S(2)}, u32[]{:S(2)}) collective-permute-start(bf16[2,8,4,128]{3,2,1,0:T(4,128)(2,1)S(1)} %get-tuple-element.38), channel_id=1, source_target_pairs={{2,0},{4,2},{6,4},{8,6},{10,8},{12,10},{14,12},{16,14},{18,16},{20... | collective-permute-start | bytes 49160 | tf_op jit(solution)/shard_map/ppermute | solution.py:359
  11.0 4.4 %collective-permute-start.3 = (bf16[2,2,8,4,128]{4,3,2,1,0:T(4,128)(2,1)S(1)}, bf16[2,2,8,4,128]{4,3,2,1,0:T(4,128)(2,1)S(1)}, u32[]{:S(2)}, u32[]{:S(2)}) collective-permute-start(bf16[2,2,8,4,128]{4,3,2,1,0:T(4,128)(2,1)S(1)} %pad_maximum_fusion.6.both), channel_id=1, source_target_pairs={{0,1},{1,0},{2,3},{3,2},{4,5},{5,4},{6,7},{7,6},{8,9},{9,8},{10,11... | collective-permute-start | bytes 98312 | tf_op jit(solution)/shard_map/ppermute | solution.py:361
  11.2 8.7 %collective-permute-start.2 = (bf16[8,128,128]{2,1,0:T(8,128)(2,1)S(1)}, bf16[8,128,128]{2,1,0:T(8,128)(2,1)S(1)}, u32[]{:S(2)}, u32[]{:S(2)}) collective-permute-start(bf16[8,128,128]{2,1,0:T(8,128)(2,1)S(1)} %get-tuple-element.39.cot_own), channel_id=1, source_target_pairs={{0,1},{1,0},{2,3},{3,2},{4,5},{5,4},{6,7},{7,6},{8,9},{9,8},{10,11... | collective-permute-start | bytes 786440 | tf_op jit(solution)/shard_map/ppermute | solution.py:362
  15.4 4.4 %collective-permute-start.5 = (bf16[9,32,128]{2,1,0:T(8,128)(2,1)S(1)}, bf16[9,32,128]{2,1,0:T(8,128)(2,1)S(1)}, u32[]{:S(2)}, u32[]{:S(2)}) collective-permute-start(bf16[9,32,128]{2,1,0:T(8,128)(2,1)S(1)} %slice.44), channel_id=1, source_target_pairs={{0,4},{2,6},{4,0},{6,2},{8,12},{10,14},{12,8},{14,10},{16,20},{18,... | collective-permute-start | bytes 221192 | tf_op jit(solution)/shard_map/ppermute | solution.py:364
  19.8 1.4 %collective-permute-start.6 = (bf16[2,9,32,128]{3,2,1,0:T(8,128)(2,1)S(1)}, bf16[2,9,32,128]{3,2,1,0:T(8,128)(2,1)S(1)}, u32[]{:S(2)}, u32[]{:S(2)}) collective-permute-start(bf16[2,9,32,128]{3,2,1,0:T(8,128)(2,1)S(1)} %pad_maximum_fusion.2.weight_pair), channel_id=1, source_target_pairs={{0,2},{2,0},{4,6},{6,4},{8,10},{10,8},{12,14},{14,12},{16,18},{18,... | collective-permute-start | bytes 442376 | tf_op jit(solution)/shard_map/ppermute | solution.py:381
  20.5 3.8 %collective-permute-start.15 = (bf16[18,64,128]{2,1,0:T(8,128)(2,1)S(1)}, bf16[18,64,128]{2,1,0:T(8,128)(2,1)S(1)}, u32[]{:S(2)}, u32[]{:S(2)}) collective-permute-start(bf16[18,64,128]{2,1,0:T(8,128)(2,1)S(1)} %get-tuple-element.62), channel_id=1, source_target_pairs={{0,2},{2,0},{4,6},{6,4},{8,10},{10,8},{12,14},{14,12},{16,18},{18,... | collective-permute-start | bytes 884744 | tf_op jit(solution)/shard_map/ppermute | solution.py:294
  24.1 2.0 %collective-permute-start.7 = (bf16[9,64,256]{2,1,0:T(8,128)(2,1)S(1)}, bf16[9,64,256]{2,1,0:T(8,128)(2,1)S(1)}, u32[]{:S(2)}, u32[]{:S(2)}) collective-permute-start(bf16[9,64,256]{2,1,0:T(8,128)(2,1)S(1)} %get-tuple-element.52), channel_id=1, source_target_pairs={{0,2},{2,0},{4,6},{6,4},{8,10},{10,8},{12,14},{14,12},{16,18},{18,... | collective-permute-start | bytes 884744 | tf_op jit(solution)/shard_map/ppermute | solution.py:294
  24.5 6.2 %collective-permute-start.16 = (bf16[18,32,128]{2,1,0:T(8,128)(2,1)S(1)}, bf16[18,32,128]{2,1,0:T(8,128)(2,1)S(1)}, u32[]{:S(2)}, u32[]{:S(2)}) collective-permute-start(bf16[18,32,128]{2,1,0:T(8,128)(2,1)S(1)} %select_convert_fusion), channel_id=1, source_target_pairs={{0,4},{2,6},{4,0},{6,2},{8,12},{10,14},{12,8},{14,10},{16,20},{18,... | collective-permute-start | bytes 442376 | tf_op jit(solution)/shard_map/ppermute | solution.py:294
  26.3 5.9 %collective-permute-start.9 = (bf16[9,32,256]{2,1,0:T(8,128)(2,1)S(1)}, bf16[9,32,256]{2,1,0:T(8,128)(2,1)S(1)}, u32[]{:S(2)}, u32[]{:S(2)}) collective-permute-start(bf16[9,32,256]{2,1,0:T(8,128)(2,1)S(1)} %select_convert_fusion.1), channel_id=1, source_target_pairs={{0,8},{2,10},{4,12},{6,14},{8,0},{10,2},{12,4},{14,6},{16,24},{18,... | collective-permute-start | bytes 442376 | tf_op jit(solution)/shard_map/ppermute | solution.py:294
  28.4 11.1 %collective-permute-start.8 = (bf16[8,128,128]{2,1,0:T(8,128)(2,1)S(1)}, bf16[8,128,128]{2,1,0:T(8,128)(2,1)S(1)}, u32[]{:S(2)}, u32[]{:S(2)}) collective-permute-start(bf16[8,128,128]{2,1,0:T(8,128)(2,1)S(1)} %get-tuple-element.55), channel_id=1, source_target_pairs={{0,1},{1,0},{2,3},{3,2},{4,5},{5,4},{6,7},{7,6},{8,9},{9,8},{10,11... | collective-permute-start | bytes 786440 | tf_op jit(solution)/shard_map/ppermute | solution.py:413
  30.8 4.4 %collective-permute-start.17 = (bf16[18,16,128]{2,1,0:T(8,128)(2,1)S(1)}, bf16[18,16,128]{2,1,0:T(8,128)(2,1)S(1)}, u32[]{:S(2)}, u32[]{:S(2)}) collective-permute-start(bf16[18,16,128]{2,1,0:T(8,128)(2,1)S(1)} %select_convert_fusion.2), channel_id=1, source_target_pairs={{0,8},{2,10},{4,12},{6,14},{8,0},{10,2},{12,4},{14,6},{16,24},{18,... | collective-permute-start | bytes 221192 | tf_op jit(solution)/shard_map/ppermute | solution.py:294
  32.2 5.1 %collective-permute-start.10 = (bf16[9,16,256]{2,1,0:T(8,128)(2,1)S(1)}, bf16[9,16,256]{2,1,0:T(8,128)(2,1)S(1)}, u32[]{:S(2)}, u32[]{:S(2)}) collective-permute-start(bf16[9,16,256]{2,1,0:T(8,128)(2,1)S(1)} %select_convert_fusion.3), channel_id=1, source_target_pairs={{0,4},{2,6},{4,0},{6,2},{8,12},{10,14},{12,8},{14,10},{16,20},{18,... | collective-permute-start | bytes 221192 | tf_op jit(solution)/shard_map/ppermute | solution.py:294
  35.2 7.3 %collective-permute-start.18 = (bf16[18,16,128]{2,1,0:T(8,128)(2,1)S(1)}, bf16[18,16,128]{2,1,0:T(8,128)(2,1)S(1)}, u32[]{:S(2)}, u32[]{:S(2)}) collective-permute-start(bf16[18,16,128]{2,1,0:T(8,128)(2,1)S(1)} %add_convert_fusion.2), channel_id=1, source_target_pairs={{0,16},{2,18},{4,20},{6,22},{8,24},{10,26},{12,28},{14,30},{16,0},... | collective-permute-start | bytes 221192 | tf_op jit(solution)/shard_map/ppermute | solution.py:302
  37.4 7.5 %collective-permute-start.11 = (bf16[9,16,256]{2,1,0:T(8,128)(2,1)S(1)}, bf16[9,16,256]{2,1,0:T(8,128)(2,1)S(1)}, u32[]{:S(2)}, u32[]{:S(2)}) collective-permute-start(bf16[9,16,256]{2,1,0:T(8,128)(2,1)S(1)} %add_convert_fusion.4), channel_id=1, source_target_pairs={{0,16},{2,18},{4,20},{6,22},{8,24},{10,26},{12,28},{14,30},{16,0},... | collective-permute-start | bytes 221192 | tf_op jit(solution)/shard_map/ppermute | solution.py:302
  43.4 4.0 %collective-permute-start.19 = (bf16[9,16,128]{2,1,0:T(8,128)(2,1)S(1)}, bf16[9,16,128]{2,1,0:T(8,128)(2,1)S(1)}, u32[]{:S(2)}, u32[]{:S(2)}) collective-permute-start(bf16[9,16,128]{2,1,0:T(8,128)(2,1)S(1)} %slice.53), channel_id=1, source_target_pairs={{0,1},{1,0},{2,3},{3,2},{4,5},{5,4},{6,7},{7,6},{8,9},{9,8},{10,11... | collective-permute-start | bytes 110600 | tf_op jit(solution)/shard_map/ppermute | solution.py:421
  44.9 4.6 %collective-permute-start.12 = (bf16[9,16,256]{2,1,0:T(8,128)(2,1)S(1)}, bf16[9,16,256]{2,1,0:T(8,128)(2,1)S(1)}, u32[]{:S(2)}, u32[]{:S(2)}) collective-permute-start(bf16[9,16,256]{2,1,0:T(8,128)(2,1)S(1)} %add_convert_fusion.3), channel_id=1, source_target_pairs={{0,4},{2,6},{4,0},{6,2},{8,12},{10,14},{12,8},{14,10},{16,20},{18,... | collective-permute-start | bytes 221192 | tf_op jit(solution)/shard_map/ppermute | solution.py:310
  47.4 4.4 %collective-permute-start.20 = (bf16[9,16,256]{2,1,0:T(8,128)(2,1)S(1)}, bf16[9,16,256]{2,1,0:T(8,128)(2,1)S(1)}, u32[]{:S(2)}, u32[]{:S(2)}) collective-permute-start(bf16[9,16,256]{2,1,0:T(8,128)(2,1)S(1)} %pad_maximum_fusion.5), channel_id=1, source_target_pairs={{0,8},{2,10},{4,12},{6,14},{8,0},{10,2},{12,4},{14,6},{16,24},{18,... | collective-permute-start | bytes 221192 | tf_op jit(solution)/shard_map/ppermute | solution.py:310
  49.5 5.2 %collective-permute-start.13 = (bf16[9,32,256]{2,1,0:T(8,128)(2,1)S(1)}, bf16[9,32,256]{2,1,0:T(8,128)(2,1)S(1)}, u32[]{:S(2)}, u32[]{:S(2)}) collective-permute-start(bf16[9,32,256]{2,1,0:T(8,128)(2,1)S(1)} %pad_maximum_fusion.3), channel_id=1, source_target_pairs={{0,8},{2,10},{4,12},{6,14},{8,0},{10,2},{12,4},{14,6},{16,24},{18,... | collective-permute-start | bytes 442376 | tf_op jit(solution)/shard_map/ppermute | solution.py:310
  51.9 5.2 %collective-permute-start.21 = (bf16[9,32,256]{2,1,0:T(8,128)(2,1)S(1)}, bf16[9,32,256]{2,1,0:T(8,128)(2,1)S(1)}, u32[]{:S(2)}, u32[]{:S(2)}) collective-permute-start(bf16[9,32,256]{2,1,0:T(8,128)(2,1)S(1)} %pad_maximum_fusion.4), channel_id=1, source_target_pairs={{0,4},{2,6},{4,0},{6,2},{8,12},{10,14},{12,8},{14,10},{16,20},{18,... | collective-permute-start | bytes 442376 | tf_op jit(solution)/shard_map/ppermute | solution.py:310
  54.8 2.5 %collective-permute-start.14 = (bf16[9,64,256]{2,1,0:T(8,128)(2,1)S(1)}, bf16[9,64,256]{2,1,0:T(8,128)(2,1)S(1)}, u32[]{:S(2)}, u32[]{:S(2)}) collective-permute-start(bf16[9,64,256]{2,1,0:T(8,128)(2,1)S(1)} %pad_maximum_fusion), channel_id=1, source_target_pairs={{0,2},{2,0},{4,6},{6,4},{8,10},{10,8},{12,14},{14,12},{16,18},{18,... | collective-permute-start | bytes 884744 | tf_op jit(solution)/shard_map/ppermute | solution.py:310
  57.2 1.6 %collective-permute-start.22 = (bf16[9,64,256]{2,1,0:T(8,128)(2,1)S(1)}, bf16[9,64,256]{2,1,0:T(8,128)(2,1)S(1)}, u32[]{:S(2)}, u32[]{:S(2)}) collective-permute-start(bf16[9,64,256]{2,1,0:T(8,128)(2,1)S(1)} %pad_maximum_fusion.1), channel_id=1, source_target_pairs={{0,2},{2,0},{4,6},{6,4},{8,10},{10,8},{12,14},{14,12},{16,18},{18,... | collective-permute-start | bytes 884744 | tf_op jit(solution)/shard_map/ppermute | solution.py:310

commit v2 on v1

--- a/solution.py
+++ b/solution.py
@@ -178,10 +178,8 @@
     send[place] = result[pl.ds(second, half), lanes].astype(BF16)
 
 
-def backward_kernel(
-    scale, cot_own, cot_oth, both, sides, weight_own, weight_pair, weight_rest, slopes,
-    right,
-    grad_out, keep, send, block, left, result, grads, weight_oth,
+def back_kernel(
+    cot_own, cot_oth, both, sides, weight_own, weight_pair, weight_rest, grad_out, block, weight_oth
 ):
     rows, length, width = cot_own.shape
     wide = length + 2 * EDGE
@@ -211,11 +209,16 @@
         + total[:, width : 2 * width]
         + shift(total[:, 2 * width :], 1)
     )
-    grads[...] = flat.astype(BF16).astype(F32).reshape(rows, wide, width)
+    grad_out[...] = flat.astype(BF16).reshape(rows, wide, width)
+
+
+def slope_kernel(scale, smooth_grad, slopes, right, grad_out, keep, send, left, result, grads):
+    rows, wide, width = smooth_grad.shape
     odd_before = jnp.zeros((wide, width), F32)
+    grad = smooth_grad[0].astype(F32)
     for r in range(rows):
-        grad = grads[r]
-        pair = grad + grads[r + 1] if r + 1 < rows else grad
+        below = smooth_grad[r + 1].astype(F32) if r + 1 < rows else None
+        pair = grad if below is None else grad + below
         even_even = slopes[0, r] * grad * 0.25
         even_odd = slopes[1, r] * (grad + shift(grad, -1)) * 0.125
         odd_even = slopes[2, r] * pair * 0.125
@@ -226,6 +229,7 @@
         grad_out[r] = rounded
         grads[r] = rounded.astype(F32)
         odd_before = row_odd
+        grad = below
     weight_sums(scale, lambda r: grads[r], right, left, result, keep, send)
 
 
@@ -297,12 +301,12 @@
         values = keep + got.astype(F32)
         if number + 2 < len(steps):
             keep, send = split_half(values, upper[steps[number + 1]])
-    mine = values.astype(BF16)
-    sent.append(mine)
-    got = lax.ppermute(mine, "space", swap_pairs(count, steps[-1]))
-    if others is not None:
-        got = after(got, *others[-1])
-    return (mine.astype(F32) + got.astype(F32)).astype(BF16), sent
+    return values.astype(BF16), sent
+
+
+def swap_pieces(piece, count, step, *others):
+    got = after(lax.ppermute(piece, "space", swap_pairs(count, step)), *others)
+    return (piece.astype(F32) + got.astype(F32)).astype(BF16)
 
 
 def gather_space(values, count, steps, upper):
@@ -384,41 +388,51 @@
         [((18, half, width), F32), ((18, half, width), BF16)],
         [((width, rows * length), BF16), ((width, 9 * width), F32)],
         sums_flops // 2,
-        sums_own, cot_oth, smooth,
-    )
+        after(sums_own, weight_pair), cot_oth, smooth,
+    )
+    smooth_grad, = run_kernel(
+        back_kernel,
+        [((rows, wide, width), BF16)],
+        [((rows + 2, wide, 2 * width), BF16), ((9, width, width), BF16)],
+        3 * conv_flops,
+        cot_own, cot_oth, both, sides, weight_own, weight_pair, weight_rest,
+    )
+    first_steps = steps[:1] + steps[2:-1] + steps[1:2] + steps[-1:] if count >= 8 else steps
+    second_got = lax.ppermute(second_send, "space", swap_pairs(count, steps[0]))
+    second_sum = second_keep + after(second_got, smooth_grad).astype(F32)
+    second_keep, second_send = split_half(second_sum, upper[steps[1]])
     hidden_grad, first_keep, first_send = run_kernel(
-        functools.partial(backward_kernel, scale),
+        functools.partial(slope_kernel, scale),
         [((rows, wide, width), BF16), ((9, half, 2 * width), F32), ((9, half, 2 * width), BF16)],
         [
-            ((rows + 2, wide, 2 * width), BF16),
             ((3 * width, rows * length), BF16),
             ((3 * width, 2 * width), F32),
             ((rows, wide, width), F32),
-            ((9, width, width), BF16),
         ],
-        2 * conv_flops + sums_flops,
-        cot_own, cot_oth, both, sides, weight_own, weight_pair, weight_rest, slopes, field_rows,
-    )
-
-    first_steps = steps[:1] + steps[2:-1] + steps[1:2] + steps[-1:] if count >= 8 else steps
+        conv_flops + sums_flops,
+        after(smooth_grad, second_send), slopes, field_rows,
+    )
     first_piece, sent = reduce_space(first_keep, first_send, count, first_steps, upper)
-
     field_keep, field_send = run_kernel(
         spread_kernel,
         [((rows, length, width), F32), ((rows, length, width), BF16)],
         [((rows + 2, wide, width), BF16), ((rows, wide, 2 * width), F32)],
-        conv_flops,
-        after(hidden_grad, sent[1]), first_taps,
-    )
+        0,
+        hidden_grad, first_taps,
+    )
+    second_got = lax.ppermute(second_send, "space", swap_pairs(count, steps[1]))
+    second_sum = second_keep + after(second_got, field_send).astype(F32)
+    second_keep, second_send = split_half(second_sum, upper[steps[2]])
+
     field_got = lax.ppermute(field_send, "chan", chan_swap)
-    field_sum = field_keep + after(field_got, sent[-1]).astype(F32)
+    field_sum = field_keep + after(field_got, first_piece).astype(F32)
     field_grad = (cot_own.astype(F32) + field_sum).astype(BF16).transpose(2, 0, 1)
 
-    others = [(value,) for value in sent]
-    others[1] += (field_send,)
-    others[-1] += (field_grad,)
-    second_piece, _ = reduce_space(second_keep, second_send, count, steps, upper, others)
-    second_got = lax.ppermute(second_piece[9:], "chan", chan_swap)
+    others = [(sent[2],)] + [(value,) for value in sent[2:]]
+    second_piece, _ = reduce_space(second_keep, second_send, count, steps[2:], upper, others)
+    second_piece = swap_pieces(second_piece, count, steps[-1], sent[-1])
+    first_piece = swap_pieces(first_piece, count, steps[-1])
+    second_got = after(lax.ppermute(second_piece[9:], "chan", chan_swap), field_grad)
     second_piece = in_order(second_part, second_piece[:9], second_got, 2)
     first_grad = gather_space(first_piece, count, first_steps, upper)
     second_grad = gather_space(second_piece, count, steps, upper)
@@ -570,7 +584,8 @@
         P("chan", None, "space"),
     )
     out_specs = (P("chan", None, "space"), P("chan", None, None), P("chan", None, None))
-    body = on_device if mesh.shape["chan"] == 2 else on_device_parts
+    sizes = mesh.shape["chan"], mesh.shape["space"]
+    body = on_device if sizes == (2, 16) else on_device_parts
     return jax.shard_map(
         body, mesh=mesh, in_specs=in_specs, out_specs=out_specs, check_vma=False
     )

time: 60.2 us -> 62.8 us (1.043)
  waiting for transfers between devices: 17.6 us -> 22.9 us
  starting transfers between devices: 27.1 us -> 24.5 us
    ppermute x6 -> x4, waiting for transfers between devices: 2.39 us -> 5.11 us  [reduce_space(): got = lax.ppermute(send, 'space', swap_pairs(count, step))]
    ppermute x6 -> x4, starting transfers between devices: 5.57 us -> 3.59 us  [reduce_space(): got = lax.ppermute(send, 'space', swap_pairs(count, step))]
    ppermute x6, waiting for transfers between devices: 6.7 us -> 8.51 us  [gather_space(): got = lax.ppermute(values, 'space', swap_pairs(count, step))]
    ppermute x3 -> x5, starting transfers between devices: 5.65 us -> 7.36 us  [the longest x2 4.68 us: swap_pieces(): got = after(lax.ppermute(piece, 'space', swap_pairs(count, step)), *others)]
    ppermute x6, starting transfers between devices: 4.42 us -> 3.02 us  [gather_space(): got = lax.ppermute(values, 'space', swap_pairs(count, step))]
    ppermute x1, starting transfers between devices: 1.84 us -> 0.91 us  [on_device(): field_got = lax.ppermute(field_send, 'chan', chan_swap)]
    ppermute x3 -> x5, waiting for transfers between devices: 4.16 us -> 4.95 us  [the longest x1 2.59 us: on_device(): lax.ppermute(second_piece[9:], 'chan', chan_swap)]
    pallas_call x5 -> x6, Pallas kernels: 10.3 us -> 10.1 us  [run_kernel(): pl.pallas_call(kernel, cost_estimate=pl.CostEstimate(flops=flops, transce...]
  transfers between devices with their start and end apart: 23 -> 23, of which waited for: 14 -> 13; matrix products, arithmetic and copies ran while one was open for 5% -> 5% of each run, Pallas kernels for 15% -> 14%
where the time goes in v2:
time: 62.8 us; the launch traced here: 62.7 us
  starting transfers between devices  24.5 us (39%)
  waiting for transfers between devices  22.9 us (36%)
  Pallas kernels  10.1 us (16%)
  other arithmetic  3.35 us (5%)
  between operations  0.93 us (1%)
  local copies, waits for them, and re-layouts  0.9 us (1%)
    pallas_call x6, Pallas kernels, run_kernel(): pl.pallas_call(kernel, cost_estimate=pl.CostEstimate(flops=flops, transce...  10.1 us
    ppermute x6, waiting for transfers between devices, gather_space(): got = lax.ppermute(values, 'space', swap_pairs(count, step))  8.51 us
    ppermute x4, waiting for transfers between devices, reduce_space(): got = lax.ppermute(send, 'space', swap_pairs(count, step))  5.11 us
    ppermute x2, starting transfers between devices, swap_pieces(): got = after(lax.ppermute(piece, 'space', swap_pairs(count, step)), *others)  4.68 us
    ppermute x1, starting transfers between devices, on_device(): high = lax.ppermute(first, 'space', backward)  4.44 us
    ppermute x4, starting transfers between devices, reduce_space(): got = lax.ppermute(send, 'space', swap_pairs(count, step))  3.59 us
    ppermute x1, starting transfers between devices, on_device(): packed = lax.ppermute(packed, 'chan', chan_swap)  3.03 us
    ppermute x6, starting transfers between devices, gather_space(): got = lax.ppermute(values, 'space', swap_pairs(count, step))  3.02 us
  transfers between devices with their start and end apart: 23, of which 13 were waited for; matrix products, arithmetic and copies ran while one was open for 5% of the time, Pallas kernels for 14%

profile of v2, /device:TPU:0, one launch (start us, length us, event | category | flops | bytes accessed | tf_op | source)
XLA Modules:
  0.0 62.7 jit_solution(9846900303320656065)
XLA Ops:
  0.7 1.4 %shard_map.67 = (bf16[41,32,128]{2,1,0:T(8,128)(2,1)S(1)}, bf16[8,128,128]{2,1,0:T(8,128)(2,1)S(1)}, bf16[8,128,128]{2,1,0:T(8,128)(2,1)S(1)}, bf16[128,1024]{1,...) custom-call(bf16[128,8,128]{2,1,0:T(8,128)(2,1)} %field, ...), custom_call_target="tpu_custom_call" | custom-call | bytes 2564096 | tf_op jit(solution)/shard_map/pallas_call | solution.py:273
  2.1 3.0 %collective-permute-start.4 = (bf16[41,32,128]{2,1,0:T(8,128)(2,1)S(1)}, bf16[41,32,128]{2,1,0:T(8,128)(2,1)S(1)}, u32[]{:S(2)}, u32[]{:S(2)}) collective-permute-start(bf16[41,32,128]{2,1,0:T(8,128)(2,1)S(1)} %get-tuple-element.43), channel_id=1, source_target_pairs={{0,1},{1,0},{2,3},{3,2},{4,5},{5,4},{6,7},{7,6},{8,9},{9,8},{10,11... | collective-permute-start | bytes 1007624 | tf_op jit(solution)/shard_map/ppermute | solution.py:361
  5.1 4.4 %collective-permute-start.1 = (bf16[2,8,4,128]{3,2,1,0:T(4,128)(2,1)S(1)}, bf16[2,8,4,128]{3,2,1,0:T(4,128)(2,1)S(1)}, u32[]{:S(2)}, u32[]{:S(2)}) collective-permute-start(bf16[2,8,4,128]{3,2,1,0:T(4,128)(2,1)S(1)} %get-tuple-element.40), channel_id=1, source_target_pairs={{2,0},{4,2},{6,4},{8,6},{10,8},{12,10},{14,12},{16,14},{18,16},{20... | collective-permute-start | bytes 49160 | tf_op jit(solution)/shard_map/ppermute | solution.py:363
  9.6 1.4 %collective-permute-done = bf16[2,8,4,128]{3,2,1,0:T(4,128)(2,1)S(1)} collective-permute-done((bf16[2,8,4,128]{3,2,1,0:T(4,128)(2,1)S(1)}, bf16[2,8,4,128]{3,2,1,0:T(4,128)(2,1)S(1)}, u32[]{:S(2)}, u32[]{:S(2)}) %collective-permute-start) | collective-permute-done | bytes 16416 | tf_op jit(solution)/shard_map/ppermute | solution.py:362
  11.2 2.0 %collective-permute-start.2 = (bf16[8,128,128]{2,1,0:T(8,128)(2,1)S(1)}, bf16[8,128,128]{2,1,0:T(8,128)(2,1)S(1)}, u32[]{:S(2)}, u32[]{:S(2)}) collective-permute-start(bf16[8,128,128]{2,1,0:T(8,128)(2,1)S(1)} %get-tuple-element.41.cot_own), channel_id=1, source_target_pairs={{0,1},{1,0},{2,3},{3,2},{4,5},{5,4},{6,7},{7,6},{8,9},{9,8},{10,11... | collective-permute-start | bytes 786440 | tf_op jit(solution)/shard_map/ppermute | solution.py:366
  13.1 2.3 %collective-permute-done.3.sides = bf16[2,2,8,4,128]{4,3,2,1,0:T(4,128)(2,1)S(1)} collective-permute-done((bf16[2,2,8,4,128]{4,3,2,1,0:T(4,128)(2,1)S(1)}, bf16[2,2,8,4,128]{4,3,2,1,0:T(4,128)(2,1)S(1)}, u32[]{:S(2)}, u32[]{:S(2)}) %collective-permute-start.3) | collective-permute-done | bytes 32800 | tf_op jit(solution)/shard_map/ppermute | solution.py:365
  15.4 3.9 %shard_map.68 = (f32[4,8,144,128]{3,2,1,0:T(8,128)S(1)}, bf16[10,128,256]{2,1,0:T(8,128)(2,1)S(1)}, bf16[1024,1152]{1,0:T(8,128)(2,1)S(1)}, f32[128,1152]{1,0:T(8,128)S(1)}) custom-call(bf16[8,128,128]{2,1,0:T(8,128)(2,1)S(1)} %get-tuple-element.45.own, bf16[41,32,128]{2,1,0:T(8,128)(2,1)S(1)} %collective-permute-done.4.packed, ...), custom_call_target="tpu_custom_call" | custom-call | flops 1660944384 | bytes 7479296 | tf_op jit(solution)/shard_map/pallas_call | solution.py:273
  19.9 0.6 %shard_map.70 = (f32[18,64,128]{2,1,0:T(8,128)S(1)}, bf16[18,64,128]{2,1,0:T(8,128)(2,1)S(1)}) custom-call(f32[128,1152]{1,0:T(8,128)S(1)} %get-tuple-element.50.sums_own, bf16[8,128,128]{2,1,0:T(8,128)(2,1)S(1)} %collective-permute-done.2.cot_oth, bf16[1024,1152]{1,0:T(8,128)(2,1)S(1)} %get-tuple-element.51.smooth), custom_call_target="tpu_custom_call" | custom-call | flops 301989888 | bytes 4096000 | tf_op jit(solution)/shard_map/pallas_call | solution.py:273
  20.5 0.6 collective-permute-start.7
  21.2 1.1 %shard_map.69.smooth_grad = bf16[8,144,128]{2,1,0:T(8,128)(2,1)S(1)} custom-call(bf16[8,128,128]{2,1,0:T(8,128)(2,1)S(1)} %get-tuple-element.41.cot_own, bf16[8,128,128]{2,1,0:T(8,128)(2,1)S(1)} %collective-permute-done.2.cot_oth, bf16[2,2,8,4,128]{4,3,2,1,0:T(4,128)(2,1)S(1)} %pad_maximum_fusion.6.both, ...), custom_call_target="tpu_custom_call" | custom-call | flops 2038431744 | bytes 1474560 | tf_op jit(solution)/shard_map/pallas_call | solution.py:273
  22.5 1.7 %collective-permute-start.16 = (bf16[18,32,128]{2,1,0:T(8,128)(2,1)S(1)}, bf16[18,32,128]{2,1,0:T(8,128)(2,1)S(1)}, u32[]{:S(2)}, u32[]{:S(2)}) collective-permute-start(bf16[18,32,128]{2,1,0:T(8,128)(2,1)S(1)} %select_convert_fusion.1), channel_id=1, source_target_pairs={{0,4},{2,6},{4,0},{6,2},{8,12},{10,14},{12,8},{14,10},{16,20},{18,... | collective-permute-start | bytes 442376 | tf_op jit(solution)/shard_map/ppermute | solution.py:423
  24.2 1.6 %shard_map.71 = (bf16[8,144,128]{2,1,0:T(8,128)(2,1)S(1)}, f32[9,64,256]{2,1,0:T(8,128)S(1)}, bf16[9,64,256]{2,1,0:T(8,128)(2,1)S(1)}) custom-call(bf16[8,144,128]{2,1,0:T(8,128)(2,1)S(1)} %shard_map.69.smooth_grad, f32[4,8,144,128]{3,2,1,0:T(8,128)S(1)} %get-tuple-element.56.slopes, bf16[10,128,256]{2,1,0:T(8,128)(2,1)S(1)} %get-tuple-element.57.right), custom_call_target="tpu_custom_call" | custom-call | flops 1283457024 | bytes 4489216 | tf_op jit(solution)/shard_map/pallas_call | solution.py:273
  25.9 1.4 %shard_map.72 = (f32[8,128,128]{2,1,0:T(8,128)S(1)}, bf16[8,128,128]{2,1,0:T(8,128)(2,1)S(1)}) custom-call(bf16[8,144,128]{2,1,0:T(8,128)(2,1)S(1)} %get-tuple-element.58.grad, bf16[9,128,256]{2,1,0:T(8,128)(2,1)S(1)} %bitcast.13), custom_call_target="tpu_custom_call" | custom-call | bytes 1671168 | tf_op jit(solution)/shard_map/pallas_call | solution.py:273
  27.3 0.9 %collective-permute-start.8 = (bf16[8,128,128]{2,1,0:T(8,128)(2,1)S(1)}, bf16[8,128,128]{2,1,0:T(8,128)(2,1)S(1)}, u32[]{:S(2)}, u32[]{:S(2)}) collective-permute-start(bf16[8,128,128]{2,1,0:T(8,128)(2,1)S(1)} %get-tuple-element.60), channel_id=1, source_target_pairs={{0,1},{1,0},{2,3},{3,2},{4,5},{5,4},{6,7},{7,6},{8,9},{9,8},{10,11... | collective-permute-start | bytes 786440 | tf_op jit(solution)/shard_map/ppermute | solution.py:427
  28.8 1.2 %collective-permute-start.10 = (bf16[9,32,256]{2,1,0:T(8,128)(2,1)S(1)}, bf16[9,32,256]{2,1,0:T(8,128)(2,1)S(1)}, u32[]{:S(2)}, u32[]{:S(2)}) collective-permute-start(bf16[9,32,256]{2,1,0:T(8,128)(2,1)S(1)} %select_convert_fusion), channel_id=1, source_target_pairs={{0,8},{2,10},{4,12},{6,14},{8,0},{10,2},{12,4},{14,6},{16,24},{18,... | collective-permute-start | bytes 442376 | tf_op jit(solution)/shard_map/ppermute | solution.py:298
  30.0 1.0 %collective-permute-start.17 = (bf16[18,16,128]{2,1,0:T(8,128)(2,1)S(1)}, bf16[18,16,128]{2,1,0:T(8,128)(2,1)S(1)}, u32[]{:S(2)}, u32[]{:S(2)}) collective-permute-start(bf16[18,16,128]{2,1,0:T(8,128)(2,1)S(1)} %select_convert_fusion.2), channel_id=1, source_target_pairs={{0,8},{2,10},{4,12},{6,14},{8,0},{10,2},{12,4},{14,6},{16,24},{18,... | collective-permute-start | bytes 221192 | tf_op jit(solution)/shard_map/ppermute | solution.py:298
  31.0 4.2 %collective-permute-done.10 = bf16[9,32,256]{2,1,0:T(8,128)(2,1)S(1)} collective-permute-done((bf16[9,32,256]{2,1,0:T(8,128)(2,1)S(1)}, bf16[9,32,256]{2,1,0:T(8,128)(2,1)S(1)}, u32[]{:S(2)}, u32[]{:S(2)}) %collective-permute-start.10) | collective-permute-done | bytes 147488 | tf_op jit(solution)/shard_map/ppermute | solution.py:298
  35.3 1.4 %collective-permute-start.11 = (bf16[9,16,256]{2,1,0:T(8,128)(2,1)S(1)}, bf16[9,16,256]{2,1,0:T(8,128)(2,1)S(1)}, u32[]{:S(2)}, u32[]{:S(2)}) collective-permute-start(bf16[9,16,256]{2,1,0:T(8,128)(2,1)S(1)} %select_convert_fusion.3), channel_id=1, source_target_pairs={{0,4},{2,6},{4,0},{6,2},{8,12},{10,14},{12,8},{14,10},{16,20},{18,... | collective-permute-start | bytes 221192 | tf_op jit(solution)/shard_map/ppermute | solution.py:298
  36.7 2.1 %collective-permute-start.18 = (bf16[18,16,128]{2,1,0:T(8,128)(2,1)S(1)}, bf16[18,16,128]{2,1,0:T(8,128)(2,1)S(1)}, u32[]{:S(2)}, u32[]{:S(2)}) collective-permute-start(bf16[18,16,128]{2,1,0:T(8,128)(2,1)S(1)} %add_convert_fusion.2), channel_id=1, source_target_pairs={{0,16},{2,18},{4,20},{6,22},{8,24},{10,26},{12,28},{14,30},{16,0},... | collective-permute-start | bytes 221192 | tf_op jit(solution)/shard_map/ppermute | solution.py:308
  38.8 0.9 %collective-permute-done.11 = bf16[9,16,256]{2,1,0:T(8,128)(2,1)S(1)} collective-permute-done((bf16[9,16,256]{2,1,0:T(8,128)(2,1)S(1)}, bf16[9,16,256]{2,1,0:T(8,128)(2,1)S(1)}, u32[]{:S(2)}, u32[]{:S(2)}) %collective-permute-start.11) | collective-permute-done | bytes 73760 | tf_op jit(solution)/shard_map/ppermute | solution.py:298
  39.7 2.6 %collective-permute-start.12 = (bf16[9,16,256]{2,1,0:T(8,128)(2,1)S(1)}, bf16[9,16,256]{2,1,0:T(8,128)(2,1)S(1)}, u32[]{:S(2)}, u32[]{:S(2)}) collective-permute-start(bf16[9,16,256]{2,1,0:T(8,128)(2,1)S(1)} %add_convert_fusion.4), channel_id=1, source_target_pairs={{0,16},{2,18},{4,20},{6,22},{8,24},{10,26},{12,28},{14,30},{16,0},... | collective-permute-start | bytes 221192 | tf_op jit(solution)/shard_map/ppermute | solution.py:308
  42.3 1.9 %collective-permute-done.18 = bf16[18,16,128]{2,1,0:T(8,128)(2,1)S(1)} collective-permute-done((bf16[18,16,128]{2,1,0:T(8,128)(2,1)S(1)}, bf16[18,16,128]{2,1,0:T(8,128)(2,1)S(1)}, u32[]{:S(2)}, u32[]{:S(2)}) %collective-permute-start.18) | collective-permute-done | bytes 73760 | tf_op jit(solution)/shard_map/ppermute | solution.py:308
  44.2 0.4 collective-permute-start.19
  44.8 0.9 %copy.7 = bf16[128,8,128]{2,1,0:T(8,128)(2,1)} copy(bf16[128,8,128]{0,2,1:T(8,128)(2,1)S(1)} %fusion) | data formatting | bytes 524288
  45.7 2.6 %collective-permute-done.19 = bf16[9,16,128]{2,1,0:T(8,128)(2,1)S(1)} collective-permute-done((bf16[9,16,128]{2,1,0:T(8,128)(2,1)S(1)}, bf16[9,16,128]{2,1,0:T(8,128)(2,1)S(1)}, u32[]{:S(2)}, u32[]{:S(2)}) %collective-permute-start.19) | collective-permute-done | bytes 36896 | tf_op jit(solution)/shard_map/ppermute | solution.py:435
  48.4 0.9 %collective-permute-start.13 = (bf16[9,16,256]{2,1,0:T(8,128)(2,1)S(1)}, bf16[9,16,256]{2,1,0:T(8,128)(2,1)S(1)}, u32[]{:S(2)}, u32[]{:S(2)}) collective-permute-start(bf16[9,16,256]{2,1,0:T(8,128)(2,1)S(1)} %add_convert_fusion.3), channel_id=1, source_target_pairs={{0,4},{2,6},{4,0},{6,2},{8,12},{10,14},{12,8},{14,10},{16,20},{18,... | collective-permute-start | bytes 221192 | tf_op jit(solution)/shard_map/ppermute | solution.py:314
  49.3 3.8 %collective-permute-done.20 = bf16[9,16,256]{2,1,0:T(8,128)(2,1)S(1)} collective-permute-done((bf16[9,16,256]{2,1,0:T(8,128)(2,1)S(1)}, bf16[9,16,256]{2,1,0:T(8,128)(2,1)S(1)}, u32[]{:S(2)}, u32[]{:S(2)}) %collective-permute-start.20) | collective-permute-done | bytes 73760 | tf_op jit(solution)/shard_map/ppermute | solution.py:314
  53.7 1.2 %collective-permute-start.14 = (bf16[9,32,256]{2,1,0:T(8,128)(2,1)S(1)}, bf16[9,32,256]{2,1,0:T(8,128)(2,1)S(1)}, u32[]{:S(2)}, u32[]{:S(2)}) collective-permute-start(bf16[9,32,256]{2,1,0:T(8,128)(2,1)S(1)} %pad_maximum_fusion.3), channel_id=1, source_target_pairs={{0,8},{2,10},{4,12},{6,14},{8,0},{10,2},{12,4},{14,6},{16,24},{18,... | collective-permute-start | bytes 442376 | tf_op jit(solution)/shard_map/ppermute | solution.py:314
  54.9 3.5 %collective-permute-done.21 = bf16[9,32,256]{2,1,0:T(8,128)(2,1)S(1)} collective-permute-done((bf16[9,32,256]{2,1,0:T(8,128)(2,1)S(1)}, bf16[9,32,256]{2,1,0:T(8,128)(2,1)S(1)}, u32[]{:S(2)}, u32[]{:S(2)}) %collective-permute-start.21) | collective-permute-done | bytes 147488 | tf_op jit(solution)/shard_map/ppermute | solution.py:314
  59.3 0.9 %collective-permute-done.22 = bf16[9,64,256]{2,1,0:T(8,128)(2,1)S(1)} collective-permute-done((bf16[9,64,256]{2,1,0:T(8,128)(2,1)S(1)}, bf16[9,64,256]{2,1,0:T(8,128)(2,1)S(1)}, u32[]{:S(2)}, u32[]{:S(2)}) %collective-permute-start.22) | collective-permute-done | bytes 294944 | tf_op jit(solution)/shard_map/ppermute | solution.py:314
  60.3 1.1 %convert_bitcast_fusion = f32[128,9,256]{2,0,1:T(8,128)} fusion(bf16[9,64,256]{2,1,0:T(8,128)(2,1)S(1)} %get-tuple-element.75, bf16[9,64,256]{2,1,0:T(8,128)(2,1)S(1)} %get-tuple-element.74), kind=kLoop, calls=%fused_computation | loop fusion | flops 1179648 | bytes 1769472 | tf_op jit(solution)/shard_map/transpose | solution.py:322
  61.6 1.1 %convert_bitcast_fusion.1 = f32[128,9,256]{2,0,1:T(8,128)} fusion(bf16[9,64,256]{2,1,0:T(8,128)(2,1)S(1)} %get-tuple-element.77, bf16[9,64,256]{2,1,0:T(8,128)(2,1)S(1)} %get-tuple-element.76), kind=kLoop, calls=%fused_computation.1 | loop fusion | flops 1179648 | bytes 1769472 | tf_op jit(solution)/shard_map/transpose | solution.py:322
  (54 shorter events, 3.6 us)
Async XLA Ops:
  0.6 14.8 %copy-start = (bf16[128,9,256]{2,0,1:T(8,128)(2,1)S(1)}, bf16[128,9,256]{2,0,1:T(8,128)(2,1)}, u32[]{:S(2)}) copy-start(bf16[128,9,256]{2,0,1:T(8,128)(2,1)} %param.5) | copy-start | bytes 1769476
  2.1 11.0 %collective-permute-start.4 = (bf16[41,32,128]{2,1,0:T(8,128)(2,1)S(1)}, bf16[41,32,128]{2,1,0:T(8,128)(2,1)S(1)}, u32[]{:S(2)}, u32[]{:S(2)}) collective-permute-start(bf16[41,32,128]{2,1,0:T(8,128)(2,1)S(1)} %get-tuple-element.43), channel_id=1, source_target_pairs={{0,1},{1,0},{2,3},{3,2},{4,5},{5,4},{6,7},{7,6},{8,9},{9,8},{10,11... | collective-permute-start | bytes 1007624 | tf_op jit(solution)/shard_map/ppermute | solution.py:361
  5.1 5.9 %collective-permute-start = (bf16[2,8,4,128]{3,2,1,0:T(4,128)(2,1)S(1)}, bf16[2,8,4,128]{3,2,1,0:T(4,128)(2,1)S(1)}, u32[]{:S(2)}, u32[]{:S(2)}) collective-permute-start(bf16[2,8,4,128]{3,2,1,0:T(4,128)(2,1)S(1)} %get-tuple-element.39), channel_id=1, source_target_pairs={{0,2},{2,4},{4,6},{6,8},{8,10},{10,12},{12,14},{14,16},{16,18},{18... | collective-permute-start | bytes 49160 | tf_op jit(solution)/shard_map/ppermute | solution.py:362
  5.1 5.9 %collective-permute-start.1 = (bf16[2,8,4,128]{3,2,1,0:T(4,128)(2,1)S(1)}, bf16[2,8,4,128]{3,2,1,0:T(4,128)(2,1)S(1)}, u32[]{:S(2)}, u32[]{:S(2)}) collective-permute-start(bf16[2,8,4,128]{3,2,1,0:T(4,128)(2,1)S(1)} %get-tuple-element.40), channel_id=1, source_target_pairs={{2,0},{4,2},{6,4},{8,6},{10,8},{12,10},{14,12},{16,14},{18,16},{20... | collective-permute-start | bytes 49160 | tf_op jit(solution)/shard_map/ppermute | solution.py:363
  11.0 4.4 %collective-permute-start.3 = (bf16[2,2,8,4,128]{4,3,2,1,0:T(4,128)(2,1)S(1)}, bf16[2,2,8,4,128]{4,3,2,1,0:T(4,128)(2,1)S(1)}, u32[]{:S(2)}, u32[]{:S(2)}) collective-permute-start(bf16[2,2,8,4,128]{4,3,2,1,0:T(4,128)(2,1)S(1)} %pad_maximum_fusion.6.both), channel_id=1, source_target_pairs={{0,1},{1,0},{2,3},{3,2},{4,5},{5,4},{6,7},{7,6},{8,9},{9,8},{10,11... | collective-permute-start | bytes 98312 | tf_op jit(solution)/shard_map/ppermute | solution.py:365
  11.2 8.7 %collective-permute-start.2 = (bf16[8,128,128]{2,1,0:T(8,128)(2,1)S(1)}, bf16[8,128,128]{2,1,0:T(8,128)(2,1)S(1)}, u32[]{:S(2)}, u32[]{:S(2)}) collective-permute-start(bf16[8,128,128]{2,1,0:T(8,128)(2,1)S(1)} %get-tuple-element.41.cot_own), channel_id=1, source_target_pairs={{0,1},{1,0},{2,3},{3,2},{4,5},{5,4},{6,7},{7,6},{8,9},{9,8},{10,11... | collective-permute-start | bytes 786440 | tf_op jit(solution)/shard_map/ppermute | solution.py:366
  15.4 4.4 %collective-permute-start.5 = (bf16[9,32,128]{2,1,0:T(8,128)(2,1)S(1)}, bf16[9,32,128]{2,1,0:T(8,128)(2,1)S(1)}, u32[]{:S(2)}, u32[]{:S(2)}) collective-permute-start(bf16[9,32,128]{2,1,0:T(8,128)(2,1)S(1)} %slice.44), channel_id=1, source_target_pairs={{0,4},{2,6},{4,0},{6,2},{8,12},{10,14},{12,8},{14,10},{16,20},{18,... | collective-permute-start | bytes 221192 | tf_op jit(solution)/shard_map/ppermute | solution.py:368
  19.8 1.4 %collective-permute-start.6 = (bf16[2,9,32,128]{3,2,1,0:T(8,128)(2,1)S(1)}, bf16[2,9,32,128]{3,2,1,0:T(8,128)(2,1)S(1)}, u32[]{:S(2)}, u32[]{:S(2)}) collective-permute-start(bf16[2,9,32,128]{3,2,1,0:T(8,128)(2,1)S(1)} %pad_maximum_fusion.2.weight_pair), channel_id=1, source_target_pairs={{0,2},{2,0},{4,6},{6,4},{8,10},{10,8},{12,14},{14,12},{16,18},{18,... | collective-permute-start | bytes 442376 | tf_op jit(solution)/shard_map/ppermute | solution.py:385
  20.5 1.9 %collective-permute-start.7 = (bf16[18,64,128]{2,1,0:T(8,128)(2,1)S(1)}, bf16[18,64,128]{2,1,0:T(8,128)(2,1)S(1)}, u32[]{:S(2)}, u32[]{:S(2)}) collective-permute-start(bf16[18,64,128]{2,1,0:T(8,128)(2,1)S(1)} %get-tuple-element.53), channel_id=1, source_target_pairs={{0,2},{2,0},{4,6},{6,4},{8,10},{10,8},{12,14},{14,12},{16,18},{18,... | collective-permute-start | bytes 884744 | tf_op jit(solution)/shard_map/ppermute | solution.py:401
  22.5 6.1 %collective-permute-start.16 = (bf16[18,32,128]{2,1,0:T(8,128)(2,1)S(1)}, bf16[18,32,128]{2,1,0:T(8,128)(2,1)S(1)}, u32[]{:S(2)}, u32[]{:S(2)}) collective-permute-start(bf16[18,32,128]{2,1,0:T(8,128)(2,1)S(1)} %select_convert_fusion.1), channel_id=1, source_target_pairs={{0,4},{2,6},{4,0},{6,2},{8,12},{10,14},{12,8},{14,10},{16,20},{18,... | collective-permute-start | bytes 442376 | tf_op jit(solution)/shard_map/ppermute | solution.py:423
  25.8 2.9 %collective-permute-start.9 = (bf16[9,64,256]{2,1,0:T(8,128)(2,1)S(1)}, bf16[9,64,256]{2,1,0:T(8,128)(2,1)S(1)}, u32[]{:S(2)}, u32[]{:S(2)}) collective-permute-start(bf16[9,64,256]{2,1,0:T(8,128)(2,1)S(1)} %get-tuple-element.63), channel_id=1, source_target_pairs={{0,2},{2,0},{4,6},{6,4},{8,10},{10,8},{12,14},{14,12},{16,18},{18,... | collective-permute-start | bytes 884744 | tf_op jit(solution)/shard_map/ppermute | solution.py:298
  27.3 15.0 %collective-permute-start.8 = (bf16[8,128,128]{2,1,0:T(8,128)(2,1)S(1)}, bf16[8,128,128]{2,1,0:T(8,128)(2,1)S(1)}, u32[]{:S(2)}, u32[]{:S(2)}) collective-permute-start(bf16[8,128,128]{2,1,0:T(8,128)(2,1)S(1)} %get-tuple-element.60), channel_id=1, source_target_pairs={{0,1},{1,0},{2,3},{3,2},{4,5},{5,4},{6,7},{7,6},{8,9},{9,8},{10,11... | collective-permute-start | bytes 786440 | tf_op jit(solution)/shard_map/ppermute | solution.py:427
  28.8 6.4 %collective-permute-start.10 = (bf16[9,32,256]{2,1,0:T(8,128)(2,1)S(1)}, bf16[9,32,256]{2,1,0:T(8,128)(2,1)S(1)}, u32[]{:S(2)}, u32[]{:S(2)}) collective-permute-start(bf16[9,32,256]{2,1,0:T(8,128)(2,1)S(1)} %select_convert_fusion), channel_id=1, source_target_pairs={{0,8},{2,10},{4,12},{6,14},{8,0},{10,2},{12,4},{14,6},{16,24},{18,... | collective-permute-start | bytes 442376 | tf_op jit(solution)/shard_map/ppermute | solution.py:298
  30.0 6.6 %collective-permute-start.17 = (bf16[18,16,128]{2,1,0:T(8,128)(2,1)S(1)}, bf16[18,16,128]{2,1,0:T(8,128)(2,1)S(1)}, u32[]{:S(2)}, u32[]{:S(2)}) collective-permute-start(bf16[18,16,128]{2,1,0:T(8,128)(2,1)S(1)} %select_convert_fusion.2), channel_id=1, source_target_pairs={{0,8},{2,10},{4,12},{6,14},{8,0},{10,2},{12,4},{14,6},{16,24},{18,... | collective-permute-start | bytes 221192 | tf_op jit(solution)/shard_map/ppermute | solution.py:298
  35.3 4.4 %collective-permute-start.11 = (bf16[9,16,256]{2,1,0:T(8,128)(2,1)S(1)}, bf16[9,16,256]{2,1,0:T(8,128)(2,1)S(1)}, u32[]{:S(2)}, u32[]{:S(2)}) collective-permute-start(bf16[9,16,256]{2,1,0:T(8,128)(2,1)S(1)} %select_convert_fusion.3), channel_id=1, source_target_pairs={{0,4},{2,6},{4,0},{6,2},{8,12},{10,14},{12,8},{14,10},{16,20},{18,... | collective-permute-start | bytes 221192 | tf_op jit(solution)/shard_map/ppermute | solution.py:298
  36.7 7.5 %collective-permute-start.18 = (bf16[18,16,128]{2,1,0:T(8,128)(2,1)S(1)}, bf16[18,16,128]{2,1,0:T(8,128)(2,1)S(1)}, u32[]{:S(2)}, u32[]{:S(2)}) collective-permute-start(bf16[18,16,128]{2,1,0:T(8,128)(2,1)S(1)} %add_convert_fusion.2), channel_id=1, source_target_pairs={{0,16},{2,18},{4,20},{6,22},{8,24},{10,26},{12,28},{14,30},{16,0},... | collective-permute-start | bytes 221192 | tf_op jit(solution)/shard_map/ppermute | solution.py:308
  39.7 8.7 %collective-permute-start.12 = (bf16[9,16,256]{2,1,0:T(8,128)(2,1)S(1)}, bf16[9,16,256]{2,1,0:T(8,128)(2,1)S(1)}, u32[]{:S(2)}, u32[]{:S(2)}) collective-permute-start(bf16[9,16,256]{2,1,0:T(8,128)(2,1)S(1)} %add_convert_fusion.4), channel_id=1, source_target_pairs={{0,16},{2,18},{4,20},{6,22},{8,24},{10,26},{12,28},{14,30},{16,0},... | collective-permute-start | bytes 221192 | tf_op jit(solution)/shard_map/ppermute | solution.py:308
  44.2 4.0 %collective-permute-start.19 = (bf16[9,16,128]{2,1,0:T(8,128)(2,1)S(1)}, bf16[9,16,128]{2,1,0:T(8,128)(2,1)S(1)}, u32[]{:S(2)}, u32[]{:S(2)}) collective-permute-start(bf16[9,16,128]{2,1,0:T(8,128)(2,1)S(1)} %slice.53), channel_id=1, source_target_pairs={{0,1},{1,0},{2,3},{3,2},{4,5},{5,4},{6,7},{7,6},{8,9},{9,8},{10,11... | collective-permute-start | bytes 110600 | tf_op jit(solution)/shard_map/ppermute | solution.py:435
  48.3 4.9 %collective-permute-start.20 = (bf16[9,16,256]{2,1,0:T(8,128)(2,1)S(1)}, bf16[9,16,256]{2,1,0:T(8,128)(2,1)S(1)}, u32[]{:S(2)}, u32[]{:S(2)}) collective-permute-start(bf16[9,16,256]{2,1,0:T(8,128)(2,1)S(1)} %pad_maximum_fusion.5), channel_id=1, source_target_pairs={{0,8},{2,10},{4,12},{6,14},{8,0},{10,2},{12,4},{14,6},{16,24},{18,... | collective-permute-start | bytes 221192 | tf_op jit(solution)/shard_map/ppermute | solution.py:314
  48.4 5.2 %collective-permute-start.13 = (bf16[9,16,256]{2,1,0:T(8,128)(2,1)S(1)}, bf16[9,16,256]{2,1,0:T(8,128)(2,1)S(1)}, u32[]{:S(2)}, u32[]{:S(2)}) collective-permute-start(bf16[9,16,256]{2,1,0:T(8,128)(2,1)S(1)} %add_convert_fusion.3), channel_id=1, source_target_pairs={{0,4},{2,6},{4,0},{6,2},{8,12},{10,14},{12,8},{14,10},{16,20},{18,... | collective-permute-start | bytes 221192 | tf_op jit(solution)/shard_map/ppermute | solution.py:314
  53.2 5.2 %collective-permute-start.21 = (bf16[9,32,256]{2,1,0:T(8,128)(2,1)S(1)}, bf16[9,32,256]{2,1,0:T(8,128)(2,1)S(1)}, u32[]{:S(2)}, u32[]{:S(2)}) collective-permute-start(bf16[9,32,256]{2,1,0:T(8,128)(2,1)S(1)} %pad_maximum_fusion.4), channel_id=1, source_target_pairs={{0,4},{2,6},{4,0},{6,2},{8,12},{10,14},{12,8},{14,10},{16,20},{18,... | collective-permute-start | bytes 442376 | tf_op jit(solution)/shard_map/ppermute | solution.py:314
  53.7 5.2 %collective-permute-start.14 = (bf16[9,32,256]{2,1,0:T(8,128)(2,1)S(1)}, bf16[9,32,256]{2,1,0:T(8,128)(2,1)S(1)}, u32[]{:S(2)}, u32[]{:S(2)}) collective-permute-start(bf16[9,32,256]{2,1,0:T(8,128)(2,1)S(1)} %pad_maximum_fusion.3), channel_id=1, source_target_pairs={{0,8},{2,10},{4,12},{6,14},{8,0},{10,2},{12,4},{14,6},{16,24},{18,... | collective-permute-start | bytes 442376 | tf_op jit(solution)/shard_map/ppermute | solution.py:314
  58.5 1.6 %collective-permute-start.22 = (bf16[9,64,256]{2,1,0:T(8,128)(2,1)S(1)}, bf16[9,64,256]{2,1,0:T(8,128)(2,1)S(1)}, u32[]{:S(2)}, u32[]{:S(2)}) collective-permute-start(bf16[9,64,256]{2,1,0:T(8,128)(2,1)S(1)} %pad_maximum_fusion.1), channel_id=1, source_target_pairs={{0,2},{2,0},{4,6},{6,4},{8,10},{10,8},{12,14},{14,12},{16,18},{18,... | collective-permute-start | bytes 884744 | tf_op jit(solution)/shard_map/ppermute | solution.py:314
  59.0 2.4 %collective-permute-start.15 = (bf16[9,64,256]{2,1,0:T(8,128)(2,1)S(1)}, bf16[9,64,256]{2,1,0:T(8,128)(2,1)S(1)}, u32[]{:S(2)}, u32[]{:S(2)}) collective-permute-start(bf16[9,64,256]{2,1,0:T(8,128)(2,1)S(1)} %pad_maximum_fusion), channel_id=1, source_target_pairs={{0,2},{2,0},{4,6},{6,4},{8,10},{10,8},{12,14},{14,12},{16,18},{18,... | collective-permute-start | bytes 884744 | tf_op jit(solution)/shard_map/ppermute | solution.py:314

commit v3 on v2

--- a/solution.py
+++ b/solution.py
@@ -397,7 +397,6 @@
         3 * conv_flops,
         cot_own, cot_oth, both, sides, weight_own, weight_pair, weight_rest,
     )
-    first_steps = steps[:1] + steps[2:-1] + steps[1:2] + steps[-1:] if count >= 8 else steps
     second_got = lax.ppermute(second_send, "space", swap_pairs(count, steps[0]))
     second_sum = second_keep + after(second_got, smooth_grad).astype(F32)
     second_keep, second_send = split_half(second_sum, upper[steps[1]])
@@ -412,29 +411,26 @@
         conv_flops + sums_flops,
         after(smooth_grad, second_send), slopes, field_rows,
     )
-    first_piece, sent = reduce_space(first_keep, first_send, count, first_steps, upper)
+    first_piece, sent = reduce_space(first_keep, first_send, count, steps, upper)
+
     field_keep, field_send = run_kernel(
         spread_kernel,
         [((rows, length, width), F32), ((rows, length, width), BF16)],
         [((rows + 2, wide, width), BF16), ((rows, wide, 2 * width), F32)],
-        0,
-        hidden_grad, first_taps,
-    )
-    second_got = lax.ppermute(second_send, "space", swap_pairs(count, steps[1]))
-    second_sum = second_keep + after(second_got, field_send).astype(F32)
-    second_keep, second_send = split_half(second_sum, upper[steps[2]])
-
+        conv_flops,
+        after(hidden_grad, sent[1]), first_taps,
+    )
     field_got = lax.ppermute(field_send, "chan", chan_swap)
     field_sum = field_keep + after(field_got, first_piece).astype(F32)
     field_grad = (cot_own.astype(F32) + field_sum).astype(BF16).transpose(2, 0, 1)
 
-    others = [(sent[2],)] + [(value,) for value in sent[2:]]
-    second_piece, _ = reduce_space(second_keep, second_send, count, steps[2:], upper, others)
+    others = [(sent[0],), (sent[1], field_send)] + [(value,) for value in sent[2:]]
+    second_piece, _ = reduce_space(second_keep, second_send, count, steps[1:], upper, others)
     second_piece = swap_pieces(second_piece, count, steps[-1], sent[-1])
     first_piece = swap_pieces(first_piece, count, steps[-1])
     second_got = after(lax.ppermute(second_piece[9:], "chan", chan_swap), field_grad)
     second_piece = in_order(second_part, second_piece[:9], second_got, 2)
-    first_grad = gather_space(first_piece, count, first_steps, upper)
+    first_grad = gather_space(first_piece, count, steps, upper)
     second_grad = gather_space(second_piece, count, steps, upper)
     return (field_grad, first_grad, second_grad)
 

time: 62.8 us -> 60.6 us (0.965)
  waiting for transfers between devices: 22.9 us -> 21.4 us
  starting transfers between devices: 24.5 us -> 23.8 us
    ppermute x2, waiting for transfers between devices: 1.91 us -> 4.63 us  [swap_pieces(): got = after(lax.ppermute(piece, 'space', swap_pairs(count, step)), *others)]
    ppermute x1, waiting for transfers between devices: 2.59 us -> 0.66 us  [on_device(): lax.ppermute(second_piece[9:], 'chan', chan_swap)]
    ppermute x1 -> x0, starting transfers between devices: 1.67 us -> none  [on_device(): second_got = lax.ppermute(second_send, 'space', swap_pairs(count, steps[1]))]
    ppermute x4 -> x5, waiting for transfers between devices: 5.11 us -> 3.82 us  [reduce_space(): got = lax.ppermute(send, 'space', swap_pairs(count, step))]
    ppermute x1, starting transfers between devices: 0.91 us -> 1.98 us  [on_device(): field_got = lax.ppermute(field_send, 'chan', chan_swap)]
    ppermute x4 -> x5, starting transfers between devices: 3.59 us -> 4.41 us  [reduce_space(): got = lax.ppermute(send, 'space', swap_pairs(count, step))]
    ppermute x2, starting transfers between devices: 4.68 us -> 3.89 us  [swap_pieces(): got = after(lax.ppermute(piece, 'space', swap_pairs(count, step)), *others)]
  transfers between devices with their start and end apart: 23 -> 23, of which waited for: 13 -> 14; matrix products, arithmetic and copies ran while one was open for 5% -> 5% of each run, Pallas kernels for 14% -> 14%
where the time goes in v3:
time: 60.6 us; the launch traced here: 60.5 us
  starting transfers between devices  23.8 us (39%)
  waiting for transfers between devices  21.4 us (35%)
  Pallas kernels  10 us (17%)
  other arithmetic  3.34 us (6%)
  between operations  0.94 us (2%)
  local copies, waits for them, and re-layouts  0.9 us (1%)
    pallas_call x6, Pallas kernels, run_kernel(): pl.pallas_call(kernel, cost_estimate=pl.CostEstimate(flops=flops, transce...  10 us
    ppermute x6, waiting for transfers between devices, gather_space(): got = lax.ppermute(values, 'space', swap_pairs(count, step))  7.98 us
    ppermute x2, waiting for transfers between devices, swap_pieces(): got = after(lax.ppermute(piece, 'space', swap_pairs(count, step)), *others)  4.63 us
    ppermute x1, starting transfers between devices, on_device(): high = lax.ppermute(first, 'space', backward)  4.44 us
    ppermute x5, starting transfers between devices, reduce_space(): got = lax.ppermute(send, 'space', swap_pairs(count, step))  4.41 us
    ppermute x2, starting transfers between devices, swap_pieces(): got = after(lax.ppermute(piece, 'space', swap_pairs(count, step)), *others)  3.89 us
    ppermute x5, waiting for transfers between devices, reduce_space(): got = lax.ppermute(send, 'space', swap_pairs(count, step))  3.82 us
    ppermute x6, starting transfers between devices, gather_space(): got = lax.ppermute(values, 'space', swap_pairs(count, step))  3.28 us
  transfers between devices with their start and end apart: 23, of which 14 were waited for; matrix products, arithmetic and copies ran while one was open for 5% of the time, Pallas kernels for 14%

profile of v3, /device:TPU:0, one launch (start us, length us, event | category | flops | bytes accessed | tf_op | source)
XLA Modules:
  0.0 60.5 jit_solution(2749151929848079632)
XLA Ops:
  0.7 1.4 %shard_map.67 = (bf16[41,32,128]{2,1,0:T(8,128)(2,1)S(1)}, bf16[8,128,128]{2,1,0:T(8,128)(2,1)S(1)}, bf16[8,128,128]{2,1,0:T(8,128)(2,1)S(1)}, bf16[128,1024]{1,...) custom-call(bf16[128,8,128]{2,1,0:T(8,128)(2,1)} %field, ...), custom_call_target="tpu_custom_call" | custom-call | bytes 2564096 | tf_op jit(solution)/shard_map/pallas_call | solution.py:273
  2.1 3.0 %collective-permute-start.4 = (bf16[41,32,128]{2,1,0:T(8,128)(2,1)S(1)}, bf16[41,32,128]{2,1,0:T(8,128)(2,1)S(1)}, u32[]{:S(2)}, u32[]{:S(2)}) collective-permute-start(bf16[41,32,128]{2,1,0:T(8,128)(2,1)S(1)} %get-tuple-element.44), channel_id=1, source_target_pairs={{0,1},{1,0},{2,3},{3,2},{4,5},{5,4},{6,7},{7,6},{8,9},{9,8},{10,11... | collective-permute-start | bytes 1007624 | tf_op jit(solution)/shard_map/ppermute | solution.py:361
  5.1 4.4 %collective-permute-start.1 = (bf16[2,8,4,128]{3,2,1,0:T(4,128)(2,1)S(1)}, bf16[2,8,4,128]{3,2,1,0:T(4,128)(2,1)S(1)}, u32[]{:S(2)}, u32[]{:S(2)}) collective-permute-start(bf16[2,8,4,128]{3,2,1,0:T(4,128)(2,1)S(1)} %get-tuple-element.41), channel_id=1, source_target_pairs={{2,0},{4,2},{6,4},{8,6},{10,8},{12,10},{14,12},{16,14},{18,16},{20... | collective-permute-start | bytes 49160 | tf_op jit(solution)/shard_map/ppermute | solution.py:363
  9.6 1.4 %collective-permute-done = bf16[2,8,4,128]{3,2,1,0:T(4,128)(2,1)S(1)} collective-permute-done((bf16[2,8,4,128]{3,2,1,0:T(4,128)(2,1)S(1)}, bf16[2,8,4,128]{3,2,1,0:T(4,128)(2,1)S(1)}, u32[]{:S(2)}, u32[]{:S(2)}) %collective-permute-start) | collective-permute-done | bytes 16416 | tf_op jit(solution)/shard_map/ppermute | solution.py:362
  11.2 2.0 %collective-permute-start.2 = (bf16[8,128,128]{2,1,0:T(8,128)(2,1)S(1)}, bf16[8,128,128]{2,1,0:T(8,128)(2,1)S(1)}, u32[]{:S(2)}, u32[]{:S(2)}) collective-permute-start(bf16[8,128,128]{2,1,0:T(8,128)(2,1)S(1)} %get-tuple-element.42.cot_own), channel_id=1, source_target_pairs={{0,1},{1,0},{2,3},{3,2},{4,5},{5,4},{6,7},{7,6},{8,9},{9,8},{10,11... | collective-permute-start | bytes 786440 | tf_op jit(solution)/shard_map/ppermute | solution.py:366
  13.1 2.3 %collective-permute-done.3.sides = bf16[2,2,8,4,128]{4,3,2,1,0:T(4,128)(2,1)S(1)} collective-permute-done((bf16[2,2,8,4,128]{4,3,2,1,0:T(4,128)(2,1)S(1)}, bf16[2,2,8,4,128]{4,3,2,1,0:T(4,128)(2,1)S(1)}, u32[]{:S(2)}, u32[]{:S(2)}) %collective-permute-start.3) | collective-permute-done | bytes 32800 | tf_op jit(solution)/shard_map/ppermute | solution.py:365
  15.4 3.9 %shard_map.68 = (f32[4,8,144,128]{3,2,1,0:T(8,128)S(1)}, bf16[10,128,256]{2,1,0:T(8,128)(2,1)S(1)}, bf16[1024,1152]{1,0:T(8,128)(2,1)S(1)}, f32[128,1152]{1,0:T(8,128)S(1)}) custom-call(bf16[8,128,128]{2,1,0:T(8,128)(2,1)S(1)} %get-tuple-element.46.own, bf16[41,32,128]{2,1,0:T(8,128)(2,1)S(1)} %collective-permute-done.4.packed, ...), custom_call_target="tpu_custom_call" | custom-call | flops 1660944384 | bytes 7479296 | tf_op jit(solution)/shard_map/pallas_call | solution.py:273
  19.9 0.6 %shard_map.70 = (f32[18,64,128]{2,1,0:T(8,128)S(1)}, bf16[18,64,128]{2,1,0:T(8,128)(2,1)S(1)}) custom-call(f32[128,1152]{1,0:T(8,128)S(1)} %get-tuple-element.51.sums_own, bf16[8,128,128]{2,1,0:T(8,128)(2,1)S(1)} %collective-permute-done.2.cot_oth, bf16[1024,1152]{1,0:T(8,128)(2,1)S(1)} %get-tuple-element.52.smooth), custom_call_target="tpu_custom_call" | custom-call | flops 301989888 | bytes 4096000 | tf_op jit(solution)/shard_map/pallas_call | solution.py:273
  21.2 1.1 %shard_map.69.smooth_grad = bf16[8,144,128]{2,1,0:T(8,128)(2,1)S(1)} custom-call(bf16[8,128,128]{2,1,0:T(8,128)(2,1)S(1)} %get-tuple-element.42.cot_own, bf16[8,128,128]{2,1,0:T(8,128)(2,1)S(1)} %collective-permute-done.2.cot_oth, bf16[2,2,8,4,128]{4,3,2,1,0:T(4,128)(2,1)S(1)} %pad_maximum_fusion.6.both, ...), custom_call_target="tpu_custom_call" | custom-call | flops 2038431744 | bytes 1474560 | tf_op jit(solution)/shard_map/pallas_call | solution.py:273
  22.5 1.7 %collective-permute-start.16 = (bf16[18,32,128]{2,1,0:T(8,128)(2,1)S(1)}, bf16[18,32,128]{2,1,0:T(8,128)(2,1)S(1)}, u32[]{:S(2)}, u32[]{:S(2)}) collective-permute-start(bf16[18,32,128]{2,1,0:T(8,128)(2,1)S(1)} %select_convert_fusion.1), channel_id=1, source_target_pairs={{0,4},{2,6},{4,0},{6,2},{8,12},{10,14},{12,8},{14,10},{16,20},{18,... | collective-permute-start | bytes 442376 | tf_op jit(solution)/shard_map/ppermute | solution.py:298
  24.2 1.6 %shard_map.71 = (bf16[8,144,128]{2,1,0:T(8,128)(2,1)S(1)}, f32[9,64,256]{2,1,0:T(8,128)S(1)}, bf16[9,64,256]{2,1,0:T(8,128)(2,1)S(1)}) custom-call(bf16[8,144,128]{2,1,0:T(8,128)(2,1)S(1)} %shard_map.69.smooth_grad, f32[4,8,144,128]{3,2,1,0:T(8,128)S(1)} %get-tuple-element.57.slopes, bf16[10,128,256]{2,1,0:T(8,128)(2,1)S(1)} %get-tuple-element.58.right), custom_call_target="tpu_custom_call" | custom-call | flops 1283457024 | bytes 4489216 | tf_op jit(solution)/shard_map/pallas_call | solution.py:273
  25.8 2.8 %collective-permute-done.16 = bf16[18,32,128]{2,1,0:T(8,128)(2,1)S(1)} collective-permute-done((bf16[18,32,128]{2,1,0:T(8,128)(2,1)S(1)}, bf16[18,32,128]{2,1,0:T(8,128)(2,1)S(1)}, u32[]{:S(2)}, u32[]{:S(2)}) %collective-permute-start.16) | collective-permute-done | bytes 147488 | tf_op jit(solution)/shard_map/ppermute | solution.py:298
  28.7 1.1 %collective-permute-start.17 = (bf16[18,16,128]{2,1,0:T(8,128)(2,1)S(1)}, bf16[18,16,128]{2,1,0:T(8,128)(2,1)S(1)}, u32[]{:S(2)}, u32[]{:S(2)}) collective-permute-start(bf16[18,16,128]{2,1,0:T(8,128)(2,1)S(1)} %select_convert_fusion.2), channel_id=1, source_target_pairs={{0,8},{2,10},{4,12},{6,14},{8,0},{10,2},{12,4},{14,6},{16,24},{18,... | collective-permute-start | bytes 221192 | tf_op jit(solution)/shard_map/ppermute | solution.py:298
  29.9 1.0 %collective-permute-start.10 = (bf16[9,32,256]{2,1,0:T(8,128)(2,1)S(1)}, bf16[9,32,256]{2,1,0:T(8,128)(2,1)S(1)}, u32[]{:S(2)}, u32[]{:S(2)}) collective-permute-start(bf16[9,32,256]{2,1,0:T(8,128)(2,1)S(1)} %select_convert_fusion), channel_id=1, source_target_pairs={{0,4},{2,6},{4,0},{6,2},{8,12},{10,14},{12,8},{14,10},{16,20},{18,... | collective-permute-start | bytes 442376 | tf_op jit(solution)/shard_map/ppermute | solution.py:298
  31.0 1.4 %shard_map.72 = (f32[8,128,128]{2,1,0:T(8,128)S(1)}, bf16[8,128,128]{2,1,0:T(8,128)(2,1)S(1)}) custom-call(bf16[8,144,128]{2,1,0:T(8,128)(2,1)S(1)} %get-tuple-element.62.grad, bf16[9,128,256]{2,1,0:T(8,128)(2,1)S(1)} %bitcast.13), custom_call_target="tpu_custom_call" | custom-call | flops 679477248 | bytes 1671168 | tf_op jit(solution)/shard_map/pallas_call | solution.py:273
  32.3 2.0 %collective-permute-start.9 = (bf16[8,128,128]{2,1,0:T(8,128)(2,1)S(1)}, bf16[8,128,128]{2,1,0:T(8,128)(2,1)S(1)}, u32[]{:S(2)}, u32[]{:S(2)}) collective-permute-start(bf16[8,128,128]{2,1,0:T(8,128)(2,1)S(1)} %get-tuple-element.64), channel_id=1, source_target_pairs={{0,1},{1,0},{2,3},{3,2},{4,5},{5,4},{6,7},{7,6},{8,9},{9,8},{10,11... | collective-permute-start | bytes 786440 | tf_op jit(solution)/shard_map/ppermute | solution.py:423
  34.4 2.7 %collective-permute-start.18 = (bf16[18,16,128]{2,1,0:T(8,128)(2,1)S(1)}, bf16[18,16,128]{2,1,0:T(8,128)(2,1)S(1)}, u32[]{:S(2)}, u32[]{:S(2)}) collective-permute-start(bf16[18,16,128]{2,1,0:T(8,128)(2,1)S(1)} %add_convert_fusion.2), channel_id=1, source_target_pairs={{0,16},{2,18},{4,20},{6,22},{8,24},{10,26},{12,28},{14,30},{16,0},... | collective-permute-start | bytes 221192 | tf_op jit(solution)/shard_map/ppermute | solution.py:308
  37.6 2.8 %collective-permute-done.18 = bf16[18,16,128]{2,1,0:T(8,128)(2,1)S(1)} collective-permute-done((bf16[18,16,128]{2,1,0:T(8,128)(2,1)S(1)}, bf16[18,16,128]{2,1,0:T(8,128)(2,1)S(1)}, u32[]{:S(2)}, u32[]{:S(2)}) %collective-permute-start.18) | collective-permute-done | bytes 73760 | tf_op jit(solution)/shard_map/ppermute | solution.py:308
  40.5 1.0 %collective-permute-done.11 = bf16[9,16,256]{2,1,0:T(8,128)(2,1)S(1)} collective-permute-done((bf16[9,16,256]{2,1,0:T(8,128)(2,1)S(1)}, bf16[9,16,256]{2,1,0:T(8,128)(2,1)S(1)}, u32[]{:S(2)}, u32[]{:S(2)}) %collective-permute-start.11) | collective-permute-done | bytes 73760 | tf_op jit(solution)/shard_map/ppermute | solution.py:298
  41.6 1.2 %collective-permute-start.12 = (bf16[9,16,256]{2,1,0:T(8,128)(2,1)S(1)}, bf16[9,16,256]{2,1,0:T(8,128)(2,1)S(1)}, u32[]{:S(2)}, u32[]{:S(2)}) collective-permute-start(bf16[9,16,256]{2,1,0:T(8,128)(2,1)S(1)} %add_convert_fusion.4), channel_id=1, source_target_pairs={{0,16},{2,18},{4,20},{6,22},{8,24},{10,26},{12,28},{14,30},{16,0},... | collective-permute-start | bytes 221192 | tf_op jit(solution)/shard_map/ppermute | solution.py:308
  42.9 0.9 %copy.7 = bf16[128,8,128]{2,1,0:T(8,128)(2,1)} copy(bf16[128,8,128]{0,2,1:T(8,128)(2,1)S(1)} %fusion) | data formatting | bytes 524288
  43.8 0.7 %collective-permute-done.19 = bf16[9,16,128]{2,1,0:T(8,128)(2,1)S(1)} collective-permute-done((bf16[9,16,128]{2,1,0:T(8,128)(2,1)S(1)}, bf16[9,16,128]{2,1,0:T(8,128)(2,1)S(1)}, u32[]{:S(2)}, u32[]{:S(2)}) %collective-permute-start.19) | collective-permute-done | bytes 36896 | tf_op jit(solution)/shard_map/ppermute | solution.py:431
  44.5 1.4 %collective-permute-start.20 = (bf16[9,16,256]{2,1,0:T(8,128)(2,1)S(1)}, bf16[9,16,256]{2,1,0:T(8,128)(2,1)S(1)}, u32[]{:S(2)}, u32[]{:S(2)}) collective-permute-start(bf16[9,16,256]{2,1,0:T(8,128)(2,1)S(1)} %pad_maximum_fusion.5), channel_id=1, source_target_pairs={{0,8},{2,10},{4,12},{6,14},{8,0},{10,2},{12,4},{14,6},{16,24},{18,... | collective-permute-start | bytes 221192 | tf_op jit(solution)/shard_map/ppermute | solution.py:314
  45.9 1.9 %collective-permute-done.12 = bf16[9,16,256]{2,1,0:T(8,128)(2,1)S(1)} collective-permute-done((bf16[9,16,256]{2,1,0:T(8,128)(2,1)S(1)}, bf16[9,16,256]{2,1,0:T(8,128)(2,1)S(1)}, u32[]{:S(2)}, u32[]{:S(2)}) %collective-permute-start.12) | collective-permute-done | bytes 73760 | tf_op jit(solution)/shard_map/ppermute | solution.py:308
  47.9 1.1 %collective-permute-done.20 = bf16[9,16,256]{2,1,0:T(8,128)(2,1)S(1)} collective-permute-done((bf16[9,16,256]{2,1,0:T(8,128)(2,1)S(1)}, bf16[9,16,256]{2,1,0:T(8,128)(2,1)S(1)}, u32[]{:S(2)}, u32[]{:S(2)}) %collective-permute-start.20) | collective-permute-done | bytes 73760 | tf_op jit(solution)/shard_map/ppermute | solution.py:314
  49.0 0.8 %collective-permute-start.21 = (bf16[9,32,256]{2,1,0:T(8,128)(2,1)S(1)}, bf16[9,32,256]{2,1,0:T(8,128)(2,1)S(1)}, u32[]{:S(2)}, u32[]{:S(2)}) collective-permute-start(bf16[9,32,256]{2,1,0:T(8,128)(2,1)S(1)} %pad_maximum_fusion.4), channel_id=1, source_target_pairs={{0,4},{2,6},{4,0},{6,2},{8,12},{10,14},{12,8},{14,10},{16,20},{18,... | collective-permute-start | bytes 442376 | tf_op jit(solution)/shard_map/ppermute | solution.py:314
  49.9 2.4 %collective-permute-done.13 = bf16[9,16,256]{2,1,0:T(8,128)(2,1)S(1)} collective-permute-done((bf16[9,16,256]{2,1,0:T(8,128)(2,1)S(1)}, bf16[9,16,256]{2,1,0:T(8,128)(2,1)S(1)}, u32[]{:S(2)}, u32[]{:S(2)}) %collective-permute-start.13) | collective-permute-done | bytes 73760 | tf_op jit(solution)/shard_map/ppermute | solution.py:314
  52.3 0.8 %collective-permute-start.14 = (bf16[9,32,256]{2,1,0:T(8,128)(2,1)S(1)}, bf16[9,32,256]{2,1,0:T(8,128)(2,1)S(1)}, u32[]{:S(2)}, u32[]{:S(2)}) collective-permute-start(bf16[9,32,256]{2,1,0:T(8,128)(2,1)S(1)} %pad_maximum_fusion.3), channel_id=1, source_target_pairs={{0,4},{2,6},{4,0},{6,2},{8,12},{10,14},{12,8},{14,10},{16,20},{18,... | collective-permute-start | bytes 442376 | tf_op jit(solution)/shard_map/ppermute | solution.py:314
  53.1 1.2 %collective-permute-done.21 = bf16[9,32,256]{2,1,0:T(8,128)(2,1)S(1)} collective-permute-done((bf16[9,32,256]{2,1,0:T(8,128)(2,1)S(1)}, bf16[9,32,256]{2,1,0:T(8,128)(2,1)S(1)}, u32[]{:S(2)}, u32[]{:S(2)}) %collective-permute-start.21) | collective-permute-done | bytes 147488 | tf_op jit(solution)/shard_map/ppermute | solution.py:314
  54.4 3.0 %collective-permute-done.14 = bf16[9,32,256]{2,1,0:T(8,128)(2,1)S(1)} collective-permute-done((bf16[9,32,256]{2,1,0:T(8,128)(2,1)S(1)}, bf16[9,32,256]{2,1,0:T(8,128)(2,1)S(1)}, u32[]{:S(2)}, u32[]{:S(2)}) %collective-permute-start.14) | collective-permute-done | bytes 147488 | tf_op jit(solution)/shard_map/ppermute | solution.py:314
  57.8 1.1 %convert_bitcast_fusion = f32[128,9,256]{2,0,1:T(8,128)} fusion(bf16[9,64,256]{2,1,0:T(8,128)(2,1)S(1)} %get-tuple-element.77, bf16[9,64,256]{2,1,0:T(8,128)(2,1)S(1)} %get-tuple-element.76), kind=kLoop, calls=%fused_computation | loop fusion | flops 1179648 | bytes 1769472 | tf_op jit(solution)/shard_map/transpose | solution.py:322
  59.3 1.1 %convert_bitcast_fusion.1 = f32[128,9,256]{2,0,1:T(8,128)} fusion(bf16[9,64,256]{2,1,0:T(8,128)(2,1)S(1)} %get-tuple-element.79, bf16[9,64,256]{2,1,0:T(8,128)(2,1)S(1)} %get-tuple-element.78), kind=kLoop, calls=%fused_computation.1 | loop fusion | flops 1179648 | bytes 1769472 | tf_op jit(solution)/shard_map/transpose | solution.py:322
  (54 shorter events, 3.7 us)
Async XLA Ops:
  0.6 14.8 %copy-start = (bf16[128,9,256]{2,0,1:T(8,128)(2,1)S(1)}, bf16[128,9,256]{2,0,1:T(8,128)(2,1)}, u32[]{:S(2)}) copy-start(bf16[128,9,256]{2,0,1:T(8,128)(2,1)} %param.5) | copy-start | bytes 1769476
  2.1 11.0 %collective-permute-start.4 = (bf16[41,32,128]{2,1,0:T(8,128)(2,1)S(1)}, bf16[41,32,128]{2,1,0:T(8,128)(2,1)S(1)}, u32[]{:S(2)}, u32[]{:S(2)}) collective-permute-start(bf16[41,32,128]{2,1,0:T(8,128)(2,1)S(1)} %get-tuple-element.44), channel_id=1, source_target_pairs={{0,1},{1,0},{2,3},{3,2},{4,5},{5,4},{6,7},{7,6},{8,9},{9,8},{10,11... | collective-permute-start | bytes 1007624 | tf_op jit(solution)/shard_map/ppermute | solution.py:361
  5.1 5.9 %collective-permute-start = (bf16[2,8,4,128]{3,2,1,0:T(4,128)(2,1)S(1)}, bf16[2,8,4,128]{3,2,1,0:T(4,128)(2,1)S(1)}, u32[]{:S(2)}, u32[]{:S(2)}) collective-permute-start(bf16[2,8,4,128]{3,2,1,0:T(4,128)(2,1)S(1)} %get-tuple-element.40), channel_id=1, source_target_pairs={{0,2},{2,4},{4,6},{6,8},{8,10},{10,12},{12,14},{14,16},{16,18},{18... | collective-permute-start | bytes 49160 | tf_op jit(solution)/shard_map/ppermute | solution.py:362
  5.1 5.9 %collective-permute-start.1 = (bf16[2,8,4,128]{3,2,1,0:T(4,128)(2,1)S(1)}, bf16[2,8,4,128]{3,2,1,0:T(4,128)(2,1)S(1)}, u32[]{:S(2)}, u32[]{:S(2)}) collective-permute-start(bf16[2,8,4,128]{3,2,1,0:T(4,128)(2,1)S(1)} %get-tuple-element.41), channel_id=1, source_target_pairs={{2,0},{4,2},{6,4},{8,6},{10,8},{12,10},{14,12},{16,14},{18,16},{20... | collective-permute-start | bytes 49160 | tf_op jit(solution)/shard_map/ppermute | solution.py:363
  11.0 4.4 %collective-permute-start.3 = (bf16[2,2,8,4,128]{4,3,2,1,0:T(4,128)(2,1)S(1)}, bf16[2,2,8,4,128]{4,3,2,1,0:T(4,128)(2,1)S(1)}, u32[]{:S(2)}, u32[]{:S(2)}) collective-permute-start(bf16[2,2,8,4,128]{4,3,2,1,0:T(4,128)(2,1)S(1)} %pad_maximum_fusion.6.both), channel_id=1, source_target_pairs={{0,1},{1,0},{2,3},{3,2},{4,5},{5,4},{6,7},{7,6},{8,9},{9,8},{10,11... | collective-permute-start | bytes 98312 | tf_op jit(solution)/shard_map/ppermute | solution.py:365
  11.2 8.7 %collective-permute-start.2 = (bf16[8,128,128]{2,1,0:T(8,128)(2,1)S(1)}, bf16[8,128,128]{2,1,0:T(8,128)(2,1)S(1)}, u32[]{:S(2)}, u32[]{:S(2)}) collective-permute-start(bf16[8,128,128]{2,1,0:T(8,128)(2,1)S(1)} %get-tuple-element.42.cot_own), channel_id=1, source_target_pairs={{0,1},{1,0},{2,3},{3,2},{4,5},{5,4},{6,7},{7,6},{8,9},{9,8},{10,11... | collective-permute-start | bytes 786440 | tf_op jit(solution)/shard_map/ppermute | solution.py:366
  15.4 4.4 %collective-permute-start.5 = (bf16[9,32,128]{2,1,0:T(8,128)(2,1)S(1)}, bf16[9,32,128]{2,1,0:T(8,128)(2,1)S(1)}, u32[]{:S(2)}, u32[]{:S(2)}) collective-permute-start(bf16[9,32,128]{2,1,0:T(8,128)(2,1)S(1)} %slice.44), channel_id=1, source_target_pairs={{0,4},{2,6},{4,0},{6,2},{8,12},{10,14},{12,8},{14,10},{16,20},{18,... | collective-permute-start | bytes 221192 | tf_op jit(solution)/shard_map/ppermute | solution.py:368
  19.8 1.4 %collective-permute-start.6 = (bf16[2,9,32,128]{3,2,1,0:T(8,128)(2,1)S(1)}, bf16[2,9,32,128]{3,2,1,0:T(8,128)(2,1)S(1)}, u32[]{:S(2)}, u32[]{:S(2)}) collective-permute-start(bf16[2,9,32,128]{3,2,1,0:T(8,128)(2,1)S(1)} %pad_maximum_fusion.2.weight_pair), channel_id=1, source_target_pairs={{0,2},{2,0},{4,6},{6,4},{8,10},{10,8},{12,14},{14,12},{16,18},{18,... | collective-permute-start | bytes 442376 | tf_op jit(solution)/shard_map/ppermute | solution.py:385
  20.5 1.9 %collective-permute-start.7 = (bf16[18,64,128]{2,1,0:T(8,128)(2,1)S(1)}, bf16[18,64,128]{2,1,0:T(8,128)(2,1)S(1)}, u32[]{:S(2)}, u32[]{:S(2)}) collective-permute-start(bf16[18,64,128]{2,1,0:T(8,128)(2,1)S(1)} %get-tuple-element.54), channel_id=1, source_target_pairs={{0,2},{2,0},{4,6},{6,4},{8,10},{10,8},{12,14},{14,12},{16,18},{18,... | collective-permute-start | bytes 884744 | tf_op jit(solution)/shard_map/ppermute | solution.py:400
  22.5 6.1 %collective-permute-start.16 = (bf16[18,32,128]{2,1,0:T(8,128)(2,1)S(1)}, bf16[18,32,128]{2,1,0:T(8,128)(2,1)S(1)}, u32[]{:S(2)}, u32[]{:S(2)}) collective-permute-start(bf16[18,32,128]{2,1,0:T(8,128)(2,1)S(1)} %select_convert_fusion.1), channel_id=1, source_target_pairs={{0,4},{2,6},{4,0},{6,2},{8,12},{10,14},{12,8},{14,10},{16,20},{18,... | collective-permute-start | bytes 442376 | tf_op jit(solution)/shard_map/ppermute | solution.py:298
  25.7 4.1 %collective-permute-start.8 = (bf16[9,64,256]{2,1,0:T(8,128)(2,1)S(1)}, bf16[9,64,256]{2,1,0:T(8,128)(2,1)S(1)}, u32[]{:S(2)}, u32[]{:S(2)}) collective-permute-start(bf16[9,64,256]{2,1,0:T(8,128)(2,1)S(1)} %get-tuple-element.61), channel_id=1, source_target_pairs={{0,2},{2,0},{4,6},{6,4},{8,10},{10,8},{12,14},{14,12},{16,18},{18,... | collective-permute-start | bytes 884744 | tf_op jit(solution)/shard_map/ppermute | solution.py:298
  28.7 5.6 %collective-permute-start.17 = (bf16[18,16,128]{2,1,0:T(8,128)(2,1)S(1)}, bf16[18,16,128]{2,1,0:T(8,128)(2,1)S(1)}, u32[]{:S(2)}, u32[]{:S(2)}) collective-permute-start(bf16[18,16,128]{2,1,0:T(8,128)(2,1)S(1)} %select_convert_fusion.2), channel_id=1, source_target_pairs={{0,8},{2,10},{4,12},{6,14},{8,0},{10,2},{12,4},{14,6},{16,24},{18,... | collective-permute-start | bytes 221192 | tf_op jit(solution)/shard_map/ppermute | solution.py:298
  29.9 7.1 %collective-permute-start.10 = (bf16[9,32,256]{2,1,0:T(8,128)(2,1)S(1)}, bf16[9,32,256]{2,1,0:T(8,128)(2,1)S(1)}, u32[]{:S(2)}, u32[]{:S(2)}) collective-permute-start(bf16[9,32,256]{2,1,0:T(8,128)(2,1)S(1)} %select_convert_fusion), channel_id=1, source_target_pairs={{0,4},{2,6},{4,0},{6,2},{8,12},{10,14},{12,8},{14,10},{16,20},{18,... | collective-permute-start | bytes 442376 | tf_op jit(solution)/shard_map/ppermute | solution.py:298
  32.3 10.4 %collective-permute-start.9 = (bf16[8,128,128]{2,1,0:T(8,128)(2,1)S(1)}, bf16[8,128,128]{2,1,0:T(8,128)(2,1)S(1)}, u32[]{:S(2)}, u32[]{:S(2)}) collective-permute-start(bf16[8,128,128]{2,1,0:T(8,128)(2,1)S(1)} %get-tuple-element.64), channel_id=1, source_target_pairs={{0,1},{1,0},{2,3},{3,2},{4,5},{5,4},{6,7},{7,6},{8,9},{9,8},{10,11... | collective-permute-start | bytes 786440 | tf_op jit(solution)/shard_map/ppermute | solution.py:423
  34.4 6.0 %collective-permute-start.18 = (bf16[18,16,128]{2,1,0:T(8,128)(2,1)S(1)}, bf16[18,16,128]{2,1,0:T(8,128)(2,1)S(1)}, u32[]{:S(2)}, u32[]{:S(2)}) collective-permute-start(bf16[18,16,128]{2,1,0:T(8,128)(2,1)S(1)} %add_convert_fusion.2), channel_id=1, source_target_pairs={{0,16},{2,18},{4,20},{6,22},{8,24},{10,26},{12,28},{14,30},{16,0},... | collective-permute-start | bytes 221192 | tf_op jit(solution)/shard_map/ppermute | solution.py:308
  37.1 4.4 %collective-permute-start.11 = (bf16[9,16,256]{2,1,0:T(8,128)(2,1)S(1)}, bf16[9,16,256]{2,1,0:T(8,128)(2,1)S(1)}, u32[]{:S(2)}, u32[]{:S(2)}) collective-permute-start(bf16[9,16,256]{2,1,0:T(8,128)(2,1)S(1)} %select_convert_fusion.3), channel_id=1, source_target_pairs={{0,8},{2,10},{4,12},{6,14},{8,0},{10,2},{12,4},{14,6},{16,24},{18,... | collective-permute-start | bytes 221192 | tf_op jit(solution)/shard_map/ppermute | solution.py:298
  40.4 4.0 %collective-permute-start.19 = (bf16[9,16,128]{2,1,0:T(8,128)(2,1)S(1)}, bf16[9,16,128]{2,1,0:T(8,128)(2,1)S(1)}, u32[]{:S(2)}, u32[]{:S(2)}) collective-permute-start(bf16[9,16,128]{2,1,0:T(8,128)(2,1)S(1)} %slice.53), channel_id=1, source_target_pairs={{0,1},{1,0},{2,3},{3,2},{4,5},{5,4},{6,7},{7,6},{8,9},{9,8},{10,11... | collective-permute-start | bytes 110600 | tf_op jit(solution)/shard_map/ppermute | solution.py:431
  41.6 6.2 %collective-permute-start.12 = (bf16[9,16,256]{2,1,0:T(8,128)(2,1)S(1)}, bf16[9,16,256]{2,1,0:T(8,128)(2,1)S(1)}, u32[]{:S(2)}, u32[]{:S(2)}) collective-permute-start(bf16[9,16,256]{2,1,0:T(8,128)(2,1)S(1)} %add_convert_fusion.4), channel_id=1, source_target_pairs={{0,16},{2,18},{4,20},{6,22},{8,24},{10,26},{12,28},{14,30},{16,0},... | collective-permute-start | bytes 221192 | tf_op jit(solution)/shard_map/ppermute | solution.py:308
  44.5 4.5 %collective-permute-start.20 = (bf16[9,16,256]{2,1,0:T(8,128)(2,1)S(1)}, bf16[9,16,256]{2,1,0:T(8,128)(2,1)S(1)}, u32[]{:S(2)}, u32[]{:S(2)}) collective-permute-start(bf16[9,16,256]{2,1,0:T(8,128)(2,1)S(1)} %pad_maximum_fusion.5), channel_id=1, source_target_pairs={{0,8},{2,10},{4,12},{6,14},{8,0},{10,2},{12,4},{14,6},{16,24},{18,... | collective-permute-start | bytes 221192 | tf_op jit(solution)/shard_map/ppermute | solution.py:314
  47.8 4.4 %collective-permute-start.13 = (bf16[9,16,256]{2,1,0:T(8,128)(2,1)S(1)}, bf16[9,16,256]{2,1,0:T(8,128)(2,1)S(1)}, u32[]{:S(2)}, u32[]{:S(2)}) collective-permute-start(bf16[9,16,256]{2,1,0:T(8,128)(2,1)S(1)} %add_convert_fusion.3), channel_id=1, source_target_pairs={{0,8},{2,10},{4,12},{6,14},{8,0},{10,2},{12,4},{14,6},{16,24},{18,... | collective-permute-start | bytes 221192 | tf_op jit(solution)/shard_map/ppermute | solution.py:314
  49.0 5.2 %collective-permute-start.21 = (bf16[9,32,256]{2,1,0:T(8,128)(2,1)S(1)}, bf16[9,32,256]{2,1,0:T(8,128)(2,1)S(1)}, u32[]{:S(2)}, u32[]{:S(2)}) collective-permute-start(bf16[9,32,256]{2,1,0:T(8,128)(2,1)S(1)} %pad_maximum_fusion.4), channel_id=1, source_target_pairs={{0,4},{2,6},{4,0},{6,2},{8,12},{10,14},{12,8},{14,10},{16,20},{18,... | collective-permute-start | bytes 442376 | tf_op jit(solution)/shard_map/ppermute | solution.py:314
  52.3 5.2 %collective-permute-start.14 = (bf16[9,32,256]{2,1,0:T(8,128)(2,1)S(1)}, bf16[9,32,256]{2,1,0:T(8,128)(2,1)S(1)}, u32[]{:S(2)}, u32[]{:S(2)}) collective-permute-start(bf16[9,32,256]{2,1,0:T(8,128)(2,1)S(1)} %pad_maximum_fusion.3), channel_id=1, source_target_pairs={{0,4},{2,6},{4,0},{6,2},{8,12},{10,14},{12,8},{14,10},{16,20},{18,... | collective-permute-start | bytes 442376 | tf_op jit(solution)/shard_map/ppermute | solution.py:314
  54.3 3.3 %collective-permute-start.22 = (bf16[9,64,256]{2,1,0:T(8,128)(2,1)S(1)}, bf16[9,64,256]{2,1,0:T(8,128)(2,1)S(1)}, u32[]{:S(2)}, u32[]{:S(2)}) collective-permute-start(bf16[9,64,256]{2,1,0:T(8,128)(2,1)S(1)} %pad_maximum_fusion.1), channel_id=1, source_target_pairs={{0,2},{2,0},{4,6},{6,4},{8,10},{10,8},{12,14},{14,12},{16,18},{18,... | collective-permute-start | bytes 884744 | tf_op jit(solution)/shard_map/ppermute | solution.py:314
  57.6 1.6 %collective-permute-start.15 = (bf16[9,64,256]{2,1,0:T(8,128)(2,1)S(1)}, bf16[9,64,256]{2,1,0:T(8,128)(2,1)S(1)}, u32[]{:S(2)}, u32[]{:S(2)}) collective-permute-start(bf16[9,64,256]{2,1,0:T(8,128)(2,1)S(1)} %pad_maximum_fusion), channel_id=1, source_target_pairs={{0,2},{2,0},{4,6},{6,4},{8,10},{10,8},{12,14},{14,12},{16,18},{18,... | collective-permute-start | bytes 884744 | tf_op jit(solution)/shard_map/ppermute | solution.py:314

commit v4 on v3

--- a/solution.py
+++ b/solution.py
@@ -22,6 +22,10 @@
     return [(i, i ^ distance) for i in range(count)]
 
 
+def step_pairs(count, step):
+    return [(i, i ^ step[i % 2]) for i in range(count)]
+
+
 def shift(values, by):
     if by == 0:
         return values
@@ -38,10 +42,10 @@
 
 def gelu_pair(values):
     square = values * values
-    bent = jnp.tanh(GELU_RATE * (values + GELU_CUBE * (square * values)))
-    inner_slope = GELU_RATE * (1.0 + 3.0 * GELU_CUBE * square)
-    lifted = 0.5 * (1.0 + bent)
-    return values * lifted, lifted + 0.5 * values * (1.0 - bent * bent) * inner_slope
+    gate = 0.5 + 0.5 * jnp.tanh(values * (GELU_RATE + GELU_RATE * GELU_CUBE * square))
+    result = values * gate
+    rise = 2.0 * GELU_RATE + 6.0 * GELU_RATE * GELU_CUBE * square
+    return result, gate + result * (1.0 - gate) * rise
 
 
 def fill_block(scratch, lane, body, low, high):
@@ -295,7 +299,7 @@
     sent = []
     for number, step in enumerate(steps[:-1]):
         sent.append(send)
-        got = lax.ppermute(send, "space", swap_pairs(count, step))
+        got = lax.ppermute(send, "space", step_pairs(count, step))
         if others is not None:
             got = after(got, *others[number])
         values = keep + got.astype(F32)
@@ -305,13 +309,13 @@
 
 
 def swap_pieces(piece, count, step, *others):
-    got = after(lax.ppermute(piece, "space", swap_pairs(count, step)), *others)
+    got = after(lax.ppermute(piece, "space", step_pairs(count, step)), *others)
     return (piece.astype(F32) + got.astype(F32)).astype(BF16)
 
 
 def gather_space(values, count, steps, upper):
     for step in reversed(steps[:-1]):
-        got = lax.ppermute(values, "space", swap_pairs(count, step))
+        got = lax.ppermute(values, "space", step_pairs(count, step))
         values = jnp.concatenate(
             [
                 jnp.where(upper[step], got, values),
@@ -333,8 +337,13 @@
     wide = length + 2 * EDGE
     count = lax.axis_size("space")
     scale = 1.0 / math.sqrt(rows * length * count)
-    steps = [1 << b for b in range(count.bit_length() - 1)]
-    bits = [(lax.axis_index("space") & step) != 0 for step in steps]
+    steps = [(1, 1), (2, 4), (4, 2), (8, 8)]
+    place = lax.axis_index("space")
+    odd = (place & 1) != 0
+    bits = [
+        (odd & ((place & second) != 0)) | (~odd & ((place & first) != 0))
+        for first, second in steps[:-1]
+    ]
     field, second_part, *bits = lax.optimization_barrier(
         (field, lax.axis_index("chan") != 0, *bits)
     )
@@ -397,7 +406,8 @@
         3 * conv_flops,
         cot_own, cot_oth, both, sides, weight_own, weight_pair, weight_rest,
     )
-    second_got = lax.ppermute(second_send, "space", swap_pairs(count, steps[0]))
+    first_steps = [steps[0], steps[2], steps[1], steps[3]]
+    second_got = lax.ppermute(second_send, "space", step_pairs(count, steps[0]))
     second_sum = second_keep + after(second_got, smooth_grad).astype(F32)
     second_keep, second_send = split_half(second_sum, upper[steps[1]])
     hidden_grad, first_keep, first_send = run_kernel(
@@ -411,7 +421,7 @@
         conv_flops + sums_flops,
         after(smooth_grad, second_send), slopes, field_rows,
     )
-    first_piece, sent = reduce_space(first_keep, first_send, count, steps, upper)
+    first_piece, sent = reduce_space(first_keep, first_send, count, first_steps, upper)
 
     field_keep, field_send = run_kernel(
         spread_kernel,
@@ -430,7 +440,7 @@
     first_piece = swap_pieces(first_piece, count, steps[-1])
     second_got = after(lax.ppermute(second_piece[9:], "chan", chan_swap), field_grad)
     second_piece = in_order(second_part, second_piece[:9], second_got, 2)
-    first_grad = gather_space(first_piece, count, steps, upper)
+    first_grad = gather_space(first_piece, count, first_steps, upper)
     second_grad = gather_space(second_piece, count, steps, upper)
     return (field_grad, first_grad, second_grad)
 

time: 60.6 us -> 58.7 us (0.969)
  waiting for transfers between devices: 21.4 us -> 15.2 us
  starting transfers between devices: 23.8 us -> 28.6 us
    ppermute x14, waiting for transfers between devices: 16.4 us -> 10.5 us  [the longest x6 6.19 us: gather_space(): got = lax.ppermute(values, 'space', step_pairs(count, step))]
    ppermute x14, starting transfers between devices: 12.1 us -> 16.7 us  [the longest x6 5.58 us: gather_space(): got = lax.ppermute(values, 'space', step_pairs(count, step))]
    ppermute x1, starting transfers between devices: 0.07 us -> 1.26 us  [on_device(): lax.ppermute(second_piece[9:], 'chan', chan_swap)]
    ppermute x1, starting transfers between devices: 1.98 us -> 1.03 us  [on_device(): field_got = lax.ppermute(field_send, 'chan', chan_swap)]
    ppermute x1, waiting for transfers between devices: 0.66 us -> 0.01 us  [on_device(): lax.ppermute(second_piece[9:], 'chan', chan_swap)]
  transfers between devices with their start and end apart: 23 -> 23, of which waited for: 14 -> 13; matrix products, arithmetic and copies ran while one was open for 5% -> 5% of each run, Pallas kernels for 14% -> 14%
where the time goes in v4:
time: 58.7 us; the launch traced here: 58.6 us
  starting transfers between devices  28.6 us (49%)
  waiting for transfers between devices  15.2 us (26%)
  Pallas kernels  9.66 us (16%)
  other arithmetic  3.33 us (6%)
  between operations  0.94 us (2%)
  local copies, waits for them, and re-layouts  0.9 us (2%)
    pallas_call x6, Pallas kernels, run_kernel(): pl.pallas_call(kernel, cost_estimate=pl.CostEstimate(flops=flops, transce...  9.66 us
    ppermute x6, waiting for transfers between devices, gather_space(): got = lax.ppermute(values, 'space', step_pairs(count, step))  6.19 us
    ppermute x6, starting transfers between devices, gather_space(): got = lax.ppermute(values, 'space', step_pairs(count, step))  5.58 us
    ppermute x2, starting transfers between devices, swap_pieces(): got = after(lax.ppermute(piece, 'space', step_pairs(count, step)), *others)  5.41 us
    ppermute x5, starting transfers between devices, reduce_space(): got = lax.ppermute(send, 'space', step_pairs(count, step))  5.1 us
    ppermute x1, starting transfers between devices, on_device(): high = lax.ppermute(first, 'space', backward)  4.44 us
    ppermute x1, starting transfers between devices, on_device(): packed = lax.ppermute(packed, 'chan', chan_swap)  3.03 us
    ppermute x5, waiting for transfers between devices, reduce_space(): got = lax.ppermute(send, 'space', step_pairs(count, step))  2.79 us
  transfers between devices with their start and end apart: 23, of which 13 were waited for; matrix products, arithmetic and copies ran while one was open for 5% of the time, Pallas kernels for 14%

profile of v4, /device:TPU:0, one launch (start us, length us, event | category | flops | bytes accessed | tf_op | source)
XLA Modules:
  0.0 58.6 jit_solution(16898411324772548362)
XLA Ops:
  0.7 1.4 %shard_map.67 = (bf16[41,32,128]{2,1,0:T(8,128)(2,1)S(1)}, bf16[8,128,128]{2,1,0:T(8,128)(2,1)S(1)}, bf16[8,128,128]{2,1,0:T(8,128)(2,1)S(1)}, bf16[128,1024]{1,...) custom-call(bf16[128,8,128]{2,1,0:T(8,128)(2,1)} %field, ...), custom_call_target="tpu_custom_call" | custom-call | bytes 2564096 | tf_op jit(solution)/shard_map/pallas_call | solution.py:277
  2.1 3.0 %collective-permute-start.4 = (bf16[41,32,128]{2,1,0:T(8,128)(2,1)S(1)}, bf16[41,32,128]{2,1,0:T(8,128)(2,1)S(1)}, u32[]{:S(2)}, u32[]{:S(2)}) collective-permute-start(bf16[41,32,128]{2,1,0:T(8,128)(2,1)S(1)} %get-tuple-element.44), channel_id=1, source_target_pairs={{0,1},{1,0},{2,3},{3,2},{4,5},{5,4},{6,7},{7,6},{8,9},{9,8},{10,11... | collective-permute-start | bytes 1007624 | tf_op jit(solution)/shard_map/ppermute | solution.py:370
  5.1 4.4 %collective-permute-start.1 = (bf16[2,8,4,128]{3,2,1,0:T(4,128)(2,1)S(1)}, bf16[2,8,4,128]{3,2,1,0:T(4,128)(2,1)S(1)}, u32[]{:S(2)}, u32[]{:S(2)}) collective-permute-start(bf16[2,8,4,128]{3,2,1,0:T(4,128)(2,1)S(1)} %get-tuple-element.41), channel_id=1, source_target_pairs={{2,0},{4,2},{6,4},{8,6},{10,8},{12,10},{14,12},{16,14},{18,16},{20... | collective-permute-start | bytes 49160 | tf_op jit(solution)/shard_map/ppermute | solution.py:372
  9.6 1.4 %collective-permute-done = bf16[2,8,4,128]{3,2,1,0:T(4,128)(2,1)S(1)} collective-permute-done((bf16[2,8,4,128]{3,2,1,0:T(4,128)(2,1)S(1)}, bf16[2,8,4,128]{3,2,1,0:T(4,128)(2,1)S(1)}, u32[]{:S(2)}, u32[]{:S(2)}) %collective-permute-start) | collective-permute-done | bytes 16416 | tf_op jit(solution)/shard_map/ppermute | solution.py:371
  11.2 2.0 %collective-permute-start.2 = (bf16[8,128,128]{2,1,0:T(8,128)(2,1)S(1)}, bf16[8,128,128]{2,1,0:T(8,128)(2,1)S(1)}, u32[]{:S(2)}, u32[]{:S(2)}) collective-permute-start(bf16[8,128,128]{2,1,0:T(8,128)(2,1)S(1)} %get-tuple-element.42.cot_own), channel_id=1, source_target_pairs={{0,1},{1,0},{2,3},{3,2},{4,5},{5,4},{6,7},{7,6},{8,9},{9,8},{10,11... | collective-permute-start | bytes 786440 | tf_op jit(solution)/shard_map/ppermute | solution.py:375
  13.2 2.3 %collective-permute-done.3.sides = bf16[2,2,8,4,128]{4,3,2,1,0:T(4,128)(2,1)S(1)} collective-permute-done((bf16[2,2,8,4,128]{4,3,2,1,0:T(4,128)(2,1)S(1)}, bf16[2,2,8,4,128]{4,3,2,1,0:T(4,128)(2,1)S(1)}, u32[]{:S(2)}, u32[]{:S(2)}) %collective-permute-start.3) | collective-permute-done | bytes 32800 | tf_op jit(solution)/shard_map/ppermute | solution.py:374
  15.4 3.5 %shard_map.68 = (f32[4,8,144,128]{3,2,1,0:T(8,128)S(1)}, bf16[10,128,256]{2,1,0:T(8,128)(2,1)S(1)}, bf16[1024,1152]{1,0:T(8,128)(2,1)S(1)}, f32[128,1152]{1,0:T(8,128)S(1)}) custom-call(bf16[8,128,128]{2,1,0:T(8,128)(2,1)S(1)} %get-tuple-element.46.own, bf16[41,32,128]{2,1,0:T(8,128)(2,1)S(1)} %collective-permute-done.4.packed, ...), custom_call_target="tpu_custom_call" | custom-call | flops 1660944384 | bytes 7479296 | tf_op jit(solution)/shard_map/pallas_call | solution.py:277
  19.0 0.8 %collective-permute-done.5 = bf16[9,32,128]{2,1,0:T(8,128)(2,1)S(1)} collective-permute-done((bf16[9,32,128]{2,1,0:T(8,128)(2,1)S(1)}, bf16[9,32,128]{2,1,0:T(8,128)(2,1)S(1)}, u32[]{:S(2)}, u32[]{:S(2)}) %collective-permute-start.5) | collective-permute-done | bytes 73760 | tf_op jit(solution)/shard_map/ppermute | solution.py:377
  21.3 1.1 %shard_map.69.smooth_grad = bf16[8,144,128]{2,1,0:T(8,128)(2,1)S(1)} custom-call(bf16[8,128,128]{2,1,0:T(8,128)(2,1)S(1)} %get-tuple-element.42.cot_own, bf16[8,128,128]{2,1,0:T(8,128)(2,1)S(1)} %collective-permute-done.2.cot_oth, bf16[2,2,8,4,128]{4,3,2,1,0:T(4,128)(2,1)S(1)} %pad_maximum_fusion.6.both, ...), custom_call_target="tpu_custom_call" | custom-call | flops 2038431744 | bytes 1474560 | tf_op jit(solution)/shard_map/pallas_call | solution.py:277
  22.5 1.3 %collective-permute-start.16 = (bf16[18,32,128]{2,1,0:T(8,128)(2,1)S(1)}, bf16[18,32,128]{2,1,0:T(8,128)(2,1)S(1)}, u32[]{:S(2)}, u32[]{:S(2)}) collective-permute-start(bf16[18,32,128]{2,1,0:T(8,128)(2,1)S(1)} %select_convert_fusion.1), channel_id=1, source_target_pairs={{0,4},{2,10},{4,0},{6,14},{8,12},{10,2},{12,8},{14,6},{16,20},{18,... | collective-permute-start | bytes 442376 | tf_op jit(solution)/shard_map/ppermute | solution.py:302
  23.8 1.6 %shard_map.71 = (bf16[8,144,128]{2,1,0:T(8,128)(2,1)S(1)}, f32[9,64,256]{2,1,0:T(8,128)S(1)}, bf16[9,64,256]{2,1,0:T(8,128)(2,1)S(1)}) custom-call(bf16[8,144,128]{2,1,0:T(8,128)(2,1)S(1)} %shard_map.69.smooth_grad, f32[4,8,144,128]{3,2,1,0:T(8,128)S(1)} %get-tuple-element.57.slopes, bf16[10,128,256]{2,1,0:T(8,128)(2,1)S(1)} %get-tuple-element.58.right), custom_call_target="tpu_custom_call" | custom-call | flops 1283457024 | bytes 4489216 | tf_op jit(solution)/shard_map/pallas_call | solution.py:277
  25.5 2.3 %collective-permute-done.16 = bf16[18,32,128]{2,1,0:T(8,128)(2,1)S(1)} collective-permute-done((bf16[18,32,128]{2,1,0:T(8,128)(2,1)S(1)}, bf16[18,32,128]{2,1,0:T(8,128)(2,1)S(1)}, u32[]{:S(2)}, u32[]{:S(2)}) %collective-permute-start.16) | collective-permute-done | bytes 147488 | tf_op jit(solution)/shard_map/ppermute | solution.py:302
  27.8 1.1 %collective-permute-start.17 = (bf16[18,16,128]{2,1,0:T(8,128)(2,1)S(1)}, bf16[18,16,128]{2,1,0:T(8,128)(2,1)S(1)}, u32[]{:S(2)}, u32[]{:S(2)}) collective-permute-start(bf16[18,16,128]{2,1,0:T(8,128)(2,1)S(1)} %select_convert_fusion.2), channel_id=1, source_target_pairs={{0,8},{2,6},{4,12},{6,2},{8,0},{10,14},{12,4},{14,10},{16,24},{18,... | collective-permute-start | bytes 221192 | tf_op jit(solution)/shard_map/ppermute | solution.py:302
  29.0 1.1 %collective-permute-start.10 = (bf16[9,32,256]{2,1,0:T(8,128)(2,1)S(1)}, bf16[9,32,256]{2,1,0:T(8,128)(2,1)S(1)}, u32[]{:S(2)}, u32[]{:S(2)}) collective-permute-start(bf16[9,32,256]{2,1,0:T(8,128)(2,1)S(1)} %select_convert_fusion), channel_id=1, source_target_pairs={{0,8},{2,6},{4,12},{6,2},{8,0},{10,14},{12,4},{14,10},{16,24},{18,... | collective-permute-start | bytes 442376 | tf_op jit(solution)/shard_map/ppermute | solution.py:302
  30.1 1.4 %shard_map.72 = (f32[8,128,128]{2,1,0:T(8,128)S(1)}, bf16[8,128,128]{2,1,0:T(8,128)(2,1)S(1)}) custom-call(bf16[8,144,128]{2,1,0:T(8,128)(2,1)S(1)} %get-tuple-element.63.grad, bf16[9,128,256]{2,1,0:T(8,128)(2,1)S(1)} %bitcast.13), custom_call_target="tpu_custom_call" | custom-call | flops 679477248 | bytes 1671168 | tf_op jit(solution)/shard_map/pallas_call | solution.py:277
  31.5 1.0 %collective-permute-start.9 = (bf16[8,128,128]{2,1,0:T(8,128)(2,1)S(1)}, bf16[8,128,128]{2,1,0:T(8,128)(2,1)S(1)}, u32[]{:S(2)}, u32[]{:S(2)}) collective-permute-start(bf16[8,128,128]{2,1,0:T(8,128)(2,1)S(1)} %get-tuple-element.65), channel_id=1, source_target_pairs={{0,1},{1,0},{2,3},{3,2},{4,5},{5,4},{6,7},{7,6},{8,9},{9,8},{10,11... | collective-permute-start | bytes 786440 | tf_op jit(solution)/shard_map/ppermute | solution.py:433
  32.5 2.6 %collective-permute-start.18 = (bf16[18,16,128]{2,1,0:T(8,128)(2,1)S(1)}, bf16[18,16,128]{2,1,0:T(8,128)(2,1)S(1)}, u32[]{:S(2)}, u32[]{:S(2)}) collective-permute-start(bf16[18,16,128]{2,1,0:T(8,128)(2,1)S(1)} %add_convert_fusion.2), channel_id=1, source_target_pairs={{0,16},{2,18},{4,20},{6,22},{8,24},{10,26},{12,28},{14,30},{16,0},... | collective-permute-start | bytes 221192 | tf_op jit(solution)/shard_map/ppermute | solution.py:312
  35.3 1.6 %collective-permute-start.11 = (bf16[9,16,256]{2,1,0:T(8,128)(2,1)S(1)}, bf16[9,16,256]{2,1,0:T(8,128)(2,1)S(1)}, u32[]{:S(2)}, u32[]{:S(2)}) collective-permute-start(bf16[9,16,256]{2,1,0:T(8,128)(2,1)S(1)} %select_convert_fusion.3), channel_id=1, source_target_pairs={{0,4},{2,10},{4,0},{6,14},{8,12},{10,2},{12,8},{14,6},{16,20},{18,... | collective-permute-start | bytes 221192 | tf_op jit(solution)/shard_map/ppermute | solution.py:302
  36.8 1.0 %collective-permute-done.18 = bf16[18,16,128]{2,1,0:T(8,128)(2,1)S(1)} collective-permute-done((bf16[18,16,128]{2,1,0:T(8,128)(2,1)S(1)}, bf16[18,16,128]{2,1,0:T(8,128)(2,1)S(1)}, u32[]{:S(2)}, u32[]{:S(2)}) %collective-permute-start.18) | collective-permute-done | bytes 73760 | tf_op jit(solution)/shard_map/ppermute | solution.py:312
  37.9 1.3 %collective-permute-start.19 = (bf16[9,16,128]{2,1,0:T(8,128)(2,1)S(1)}, bf16[9,16,128]{2,1,0:T(8,128)(2,1)S(1)}, u32[]{:S(2)}, u32[]{:S(2)}) collective-permute-start(bf16[9,16,128]{2,1,0:T(8,128)(2,1)S(1)} %slice.53), channel_id=1, source_target_pairs={{0,1},{1,0},{2,3},{3,2},{4,5},{5,4},{6,7},{7,6},{8,9},{9,8},{10,11... | collective-permute-start | bytes 110600 | tf_op jit(solution)/shard_map/ppermute | solution.py:441
  39.7 2.8 %collective-permute-start.12 = (bf16[9,16,256]{2,1,0:T(8,128)(2,1)S(1)}, bf16[9,16,256]{2,1,0:T(8,128)(2,1)S(1)}, u32[]{:S(2)}, u32[]{:S(2)}) collective-permute-start(bf16[9,16,256]{2,1,0:T(8,128)(2,1)S(1)} %add_convert_fusion.4), channel_id=1, source_target_pairs={{0,16},{2,18},{4,20},{6,22},{8,24},{10,26},{12,28},{14,30},{16,0},... | collective-permute-start | bytes 221192 | tf_op jit(solution)/shard_map/ppermute | solution.py:312
  42.6 0.9 %copy.7 = bf16[128,8,128]{2,1,0:T(8,128)(2,1)} copy(bf16[128,8,128]{0,2,1:T(8,128)(2,1)S(1)} %fusion) | data formatting | bytes 524288
  43.5 1.2 %collective-permute-start.20 = (bf16[9,16,256]{2,1,0:T(8,128)(2,1)S(1)}, bf16[9,16,256]{2,1,0:T(8,128)(2,1)S(1)}, u32[]{:S(2)}, u32[]{:S(2)}) collective-permute-start(bf16[9,16,256]{2,1,0:T(8,128)(2,1)S(1)} %pad_maximum_fusion.5), channel_id=1, source_target_pairs={{0,8},{2,6},{4,12},{6,2},{8,0},{10,14},{12,4},{14,10},{16,24},{18,... | collective-permute-start | bytes 221192 | tf_op jit(solution)/shard_map/ppermute | solution.py:318
  45.2 1.6 %collective-permute-start.13 = (bf16[9,16,256]{2,1,0:T(8,128)(2,1)S(1)}, bf16[9,16,256]{2,1,0:T(8,128)(2,1)S(1)}, u32[]{:S(2)}, u32[]{:S(2)}) collective-permute-start(bf16[9,16,256]{2,1,0:T(8,128)(2,1)S(1)} %add_convert_fusion.3), channel_id=1, source_target_pairs={{0,4},{2,10},{4,0},{6,14},{8,12},{10,2},{12,8},{14,6},{16,20},{18,... | collective-permute-start | bytes 221192 | tf_op jit(solution)/shard_map/ppermute | solution.py:318
  46.8 1.3 %collective-permute-done.20 = bf16[9,16,256]{2,1,0:T(8,128)(2,1)S(1)} collective-permute-done((bf16[9,16,256]{2,1,0:T(8,128)(2,1)S(1)}, bf16[9,16,256]{2,1,0:T(8,128)(2,1)S(1)}, u32[]{:S(2)}, u32[]{:S(2)}) %collective-permute-start.20) | collective-permute-done | bytes 73760 | tf_op jit(solution)/shard_map/ppermute | solution.py:318
  48.1 1.3 %collective-permute-start.21 = (bf16[9,32,256]{2,1,0:T(8,128)(2,1)S(1)}, bf16[9,32,256]{2,1,0:T(8,128)(2,1)S(1)}, u32[]{:S(2)}, u32[]{:S(2)}) collective-permute-start(bf16[9,32,256]{2,1,0:T(8,128)(2,1)S(1)} %pad_maximum_fusion.4), channel_id=1, source_target_pairs={{0,4},{2,10},{4,0},{6,14},{8,12},{10,2},{12,8},{14,6},{16,20},{18,... | collective-permute-start | bytes 442376 | tf_op jit(solution)/shard_map/ppermute | solution.py:318
  49.4 1.0 %collective-permute-done.13 = bf16[9,16,256]{2,1,0:T(8,128)(2,1)S(1)} collective-permute-done((bf16[9,16,256]{2,1,0:T(8,128)(2,1)S(1)}, bf16[9,16,256]{2,1,0:T(8,128)(2,1)S(1)}, u32[]{:S(2)}, u32[]{:S(2)}) %collective-permute-start.13) | collective-permute-done | bytes 73760 | tf_op jit(solution)/shard_map/ppermute | solution.py:318
  50.4 1.4 %collective-permute-start.14 = (bf16[9,32,256]{2,1,0:T(8,128)(2,1)S(1)}, bf16[9,32,256]{2,1,0:T(8,128)(2,1)S(1)}, u32[]{:S(2)}, u32[]{:S(2)}) collective-permute-start(bf16[9,32,256]{2,1,0:T(8,128)(2,1)S(1)} %pad_maximum_fusion.3), channel_id=1, source_target_pairs={{0,8},{2,6},{4,12},{6,2},{8,0},{10,14},{12,4},{14,10},{16,24},{18,... | collective-permute-start | bytes 442376 | tf_op jit(solution)/shard_map/ppermute | solution.py:318
  51.8 1.5 %collective-permute-done.21 = bf16[9,32,256]{2,1,0:T(8,128)(2,1)S(1)} collective-permute-done((bf16[9,32,256]{2,1,0:T(8,128)(2,1)S(1)}, bf16[9,32,256]{2,1,0:T(8,128)(2,1)S(1)}, u32[]{:S(2)}, u32[]{:S(2)}) %collective-permute-start.21) | collective-permute-done | bytes 147488 | tf_op jit(solution)/shard_map/ppermute | solution.py:318
  53.5 2.1 %collective-permute-done.14 = bf16[9,32,256]{2,1,0:T(8,128)(2,1)S(1)} collective-permute-done((bf16[9,32,256]{2,1,0:T(8,128)(2,1)S(1)}, bf16[9,32,256]{2,1,0:T(8,128)(2,1)S(1)}, u32[]{:S(2)}, u32[]{:S(2)}) %collective-permute-start.14) | collective-permute-done | bytes 147488 | tf_op jit(solution)/shard_map/ppermute | solution.py:318
  55.9 1.1 %convert_bitcast_fusion = f32[128,9,256]{2,0,1:T(8,128)} fusion(bf16[9,64,256]{2,1,0:T(8,128)(2,1)S(1)} %get-tuple-element.77, bf16[9,64,256]{2,1,0:T(8,128)(2,1)S(1)} %get-tuple-element.76), kind=kLoop, calls=%fused_computation | loop fusion | flops 1179648 | bytes 1769472 | tf_op jit(solution)/shard_map/transpose | solution.py:326
  57.5 1.1 %convert_bitcast_fusion.1 = f32[128,9,256]{2,0,1:T(8,128)} fusion(bf16[9,64,256]{2,1,0:T(8,128)(2,1)S(1)} %get-tuple-element.79, bf16[9,64,256]{2,1,0:T(8,128)(2,1)S(1)} %get-tuple-element.78), kind=kLoop, calls=%fused_computation.1 | loop fusion | flops 1179648 | bytes 1769472 | tf_op jit(solution)/shard_map/transpose | solution.py:326
  (54 shorter events, 4.2 us)
Async XLA Ops:
  0.6 14.8 %copy-start = (bf16[128,9,256]{2,0,1:T(8,128)(2,1)S(1)}, bf16[128,9,256]{2,0,1:T(8,128)(2,1)}, u32[]{:S(2)}) copy-start(bf16[128,9,256]{2,0,1:T(8,128)(2,1)} %param.5) | copy-start | bytes 1769476
  2.1 11.0 %collective-permute-start.4 = (bf16[41,32,128]{2,1,0:T(8,128)(2,1)S(1)}, bf16[41,32,128]{2,1,0:T(8,128)(2,1)S(1)}, u32[]{:S(2)}, u32[]{:S(2)}) collective-permute-start(bf16[41,32,128]{2,1,0:T(8,128)(2,1)S(1)} %get-tuple-element.44), channel_id=1, source_target_pairs={{0,1},{1,0},{2,3},{3,2},{4,5},{5,4},{6,7},{7,6},{8,9},{9,8},{10,11... | collective-permute-start | bytes 1007624 | tf_op jit(solution)/shard_map/ppermute | solution.py:370
  5.1 5.9 %collective-permute-start = (bf16[2,8,4,128]{3,2,1,0:T(4,128)(2,1)S(1)}, bf16[2,8,4,128]{3,2,1,0:T(4,128)(2,1)S(1)}, u32[]{:S(2)}, u32[]{:S(2)}) collective-permute-start(bf16[2,8,4,128]{3,2,1,0:T(4,128)(2,1)S(1)} %get-tuple-element.40), channel_id=1, source_target_pairs={{0,2},{2,4},{4,6},{6,8},{8,10},{10,12},{12,14},{14,16},{16,18},{18... | collective-permute-start | bytes 49160 | tf_op jit(solution)/shard_map/ppermute | solution.py:371
  5.1 5.9 %collective-permute-start.1 = (bf16[2,8,4,128]{3,2,1,0:T(4,128)(2,1)S(1)}, bf16[2,8,4,128]{3,2,1,0:T(4,128)(2,1)S(1)}, u32[]{:S(2)}, u32[]{:S(2)}) collective-permute-start(bf16[2,8,4,128]{3,2,1,0:T(4,128)(2,1)S(1)} %get-tuple-element.41), channel_id=1, source_target_pairs={{2,0},{4,2},{6,4},{8,6},{10,8},{12,10},{14,12},{16,14},{18,16},{20... | collective-permute-start | bytes 49160 | tf_op jit(solution)/shard_map/ppermute | solution.py:372
  11.0 4.4 %collective-permute-start.3 = (bf16[2,2,8,4,128]{4,3,2,1,0:T(4,128)(2,1)S(1)}, bf16[2,2,8,4,128]{4,3,2,1,0:T(4,128)(2,1)S(1)}, u32[]{:S(2)}, u32[]{:S(2)}) collective-permute-start(bf16[2,2,8,4,128]{4,3,2,1,0:T(4,128)(2,1)S(1)} %pad_maximum_fusion.6.both), channel_id=1, source_target_pairs={{0,1},{1,0},{2,3},{3,2},{4,5},{5,4},{6,7},{7,6},{8,9},{9,8},{10,11... | collective-permute-start | bytes 98312 | tf_op jit(solution)/shard_map/ppermute | solution.py:374
  11.2 8.7 %collective-permute-start.2 = (bf16[8,128,128]{2,1,0:T(8,128)(2,1)S(1)}, bf16[8,128,128]{2,1,0:T(8,128)(2,1)S(1)}, u32[]{:S(2)}, u32[]{:S(2)}) collective-permute-start(bf16[8,128,128]{2,1,0:T(8,128)(2,1)S(1)} %get-tuple-element.42.cot_own), channel_id=1, source_target_pairs={{0,1},{1,0},{2,3},{3,2},{4,5},{5,4},{6,7},{7,6},{8,9},{9,8},{10,11... | collective-permute-start | bytes 786440 | tf_op jit(solution)/shard_map/ppermute | solution.py:375
  15.4 4.4 %collective-permute-start.5 = (bf16[9,32,128]{2,1,0:T(8,128)(2,1)S(1)}, bf16[9,32,128]{2,1,0:T(8,128)(2,1)S(1)}, u32[]{:S(2)}, u32[]{:S(2)}) collective-permute-start(bf16[9,32,128]{2,1,0:T(8,128)(2,1)S(1)} %slice.44), channel_id=1, source_target_pairs={{0,4},{2,6},{4,0},{6,2},{8,12},{10,14},{12,8},{14,10},{16,20},{18,... | collective-permute-start | bytes 221192 | tf_op jit(solution)/shard_map/ppermute | solution.py:377
  19.8 1.4 %collective-permute-start.6 = (bf16[2,9,32,128]{3,2,1,0:T(8,128)(2,1)S(1)}, bf16[2,9,32,128]{3,2,1,0:T(8,128)(2,1)S(1)}, u32[]{:S(2)}, u32[]{:S(2)}) collective-permute-start(bf16[2,9,32,128]{3,2,1,0:T(8,128)(2,1)S(1)} %pad_maximum_fusion.2.weight_pair), channel_id=1, source_target_pairs={{0,2},{2,0},{4,6},{6,4},{8,10},{10,8},{12,14},{14,12},{16,18},{18,... | collective-permute-start | bytes 442376 | tf_op jit(solution)/shard_map/ppermute | solution.py:394
  20.5 1.9 %collective-permute-start.7 = (bf16[18,64,128]{2,1,0:T(8,128)(2,1)S(1)}, bf16[18,64,128]{2,1,0:T(8,128)(2,1)S(1)}, u32[]{:S(2)}, u32[]{:S(2)}) collective-permute-start(bf16[18,64,128]{2,1,0:T(8,128)(2,1)S(1)} %get-tuple-element.54), channel_id=1, source_target_pairs={{0,2},{2,0},{4,6},{6,4},{8,10},{10,8},{12,14},{14,12},{16,18},{18,... | collective-permute-start | bytes 884744 | tf_op jit(solution)/shard_map/ppermute | solution.py:410
  22.5 5.2 %collective-permute-start.16 = (bf16[18,32,128]{2,1,0:T(8,128)(2,1)S(1)}, bf16[18,32,128]{2,1,0:T(8,128)(2,1)S(1)}, u32[]{:S(2)}, u32[]{:S(2)}) collective-permute-start(bf16[18,32,128]{2,1,0:T(8,128)(2,1)S(1)} %select_convert_fusion.1), channel_id=1, source_target_pairs={{0,4},{2,10},{4,0},{6,14},{8,12},{10,2},{12,8},{14,6},{16,20},{18,... | collective-permute-start | bytes 442376 | tf_op jit(solution)/shard_map/ppermute | solution.py:302
  25.4 3.5 %collective-permute-start.8 = (bf16[9,64,256]{2,1,0:T(8,128)(2,1)S(1)}, bf16[9,64,256]{2,1,0:T(8,128)(2,1)S(1)}, u32[]{:S(2)}, u32[]{:S(2)}) collective-permute-start(bf16[9,64,256]{2,1,0:T(8,128)(2,1)S(1)} %get-tuple-element.62), channel_id=1, source_target_pairs={{0,2},{2,0},{4,6},{6,4},{8,10},{10,8},{12,14},{14,12},{16,18},{18,... | collective-permute-start | bytes 884744 | tf_op jit(solution)/shard_map/ppermute | solution.py:302
  27.8 4.7 %collective-permute-start.17 = (bf16[18,16,128]{2,1,0:T(8,128)(2,1)S(1)}, bf16[18,16,128]{2,1,0:T(8,128)(2,1)S(1)}, u32[]{:S(2)}, u32[]{:S(2)}) collective-permute-start(bf16[18,16,128]{2,1,0:T(8,128)(2,1)S(1)} %select_convert_fusion.2), channel_id=1, source_target_pairs={{0,8},{2,6},{4,12},{6,2},{8,0},{10,14},{12,4},{14,10},{16,24},{18,... | collective-permute-start | bytes 221192 | tf_op jit(solution)/shard_map/ppermute | solution.py:302
  29.0 6.2 %collective-permute-start.10 = (bf16[9,32,256]{2,1,0:T(8,128)(2,1)S(1)}, bf16[9,32,256]{2,1,0:T(8,128)(2,1)S(1)}, u32[]{:S(2)}, u32[]{:S(2)}) collective-permute-start(bf16[9,32,256]{2,1,0:T(8,128)(2,1)S(1)} %select_convert_fusion), channel_id=1, source_target_pairs={{0,8},{2,6},{4,12},{6,2},{8,0},{10,14},{12,4},{14,10},{16,24},{18,... | collective-permute-start | bytes 442376 | tf_op jit(solution)/shard_map/ppermute | solution.py:302
  31.5 11.0 %collective-permute-start.9 = (bf16[8,128,128]{2,1,0:T(8,128)(2,1)S(1)}, bf16[8,128,128]{2,1,0:T(8,128)(2,1)S(1)}, u32[]{:S(2)}, u32[]{:S(2)}) collective-permute-start(bf16[8,128,128]{2,1,0:T(8,128)(2,1)S(1)} %get-tuple-element.65), channel_id=1, source_target_pairs={{0,1},{1,0},{2,3},{3,2},{4,5},{5,4},{6,7},{7,6},{8,9},{9,8},{10,11... | collective-permute-start | bytes 786440 | tf_op jit(solution)/shard_map/ppermute | solution.py:433
  32.5 5.3 %collective-permute-start.18 = (bf16[18,16,128]{2,1,0:T(8,128)(2,1)S(1)}, bf16[18,16,128]{2,1,0:T(8,128)(2,1)S(1)}, u32[]{:S(2)}, u32[]{:S(2)}) collective-permute-start(bf16[18,16,128]{2,1,0:T(8,128)(2,1)S(1)} %add_convert_fusion.2), channel_id=1, source_target_pairs={{0,16},{2,18},{4,20},{6,22},{8,24},{10,26},{12,28},{14,30},{16,0},... | collective-permute-start | bytes 221192 | tf_op jit(solution)/shard_map/ppermute | solution.py:312
  35.3 4.4 %collective-permute-start.11 = (bf16[9,16,256]{2,1,0:T(8,128)(2,1)S(1)}, bf16[9,16,256]{2,1,0:T(8,128)(2,1)S(1)}, u32[]{:S(2)}, u32[]{:S(2)}) collective-permute-start(bf16[9,16,256]{2,1,0:T(8,128)(2,1)S(1)} %select_convert_fusion.3), channel_id=1, source_target_pairs={{0,4},{2,10},{4,0},{6,14},{8,12},{10,2},{12,8},{14,6},{16,20},{18,... | collective-permute-start | bytes 221192 | tf_op jit(solution)/shard_map/ppermute | solution.py:302
  37.9 5.6 %collective-permute-start.19 = (bf16[9,16,128]{2,1,0:T(8,128)(2,1)S(1)}, bf16[9,16,128]{2,1,0:T(8,128)(2,1)S(1)}, u32[]{:S(2)}, u32[]{:S(2)}) collective-permute-start(bf16[9,16,128]{2,1,0:T(8,128)(2,1)S(1)} %slice.53), channel_id=1, source_target_pairs={{0,1},{1,0},{2,3},{3,2},{4,5},{5,4},{6,7},{7,6},{8,9},{9,8},{10,11... | collective-permute-start | bytes 110600 | tf_op jit(solution)/shard_map/ppermute | solution.py:441
  39.7 5.4 %collective-permute-start.12 = (bf16[9,16,256]{2,1,0:T(8,128)(2,1)S(1)}, bf16[9,16,256]{2,1,0:T(8,128)(2,1)S(1)}, u32[]{:S(2)}, u32[]{:S(2)}) collective-permute-start(bf16[9,16,256]{2,1,0:T(8,128)(2,1)S(1)} %add_convert_fusion.4), channel_id=1, source_target_pairs={{0,16},{2,18},{4,20},{6,22},{8,24},{10,26},{12,28},{14,30},{16,0},... | collective-permute-start | bytes 221192 | tf_op jit(solution)/shard_map/ppermute | solution.py:312
  43.5 4.5 %collective-permute-start.20 = (bf16[9,16,256]{2,1,0:T(8,128)(2,1)S(1)}, bf16[9,16,256]{2,1,0:T(8,128)(2,1)S(1)}, u32[]{:S(2)}, u32[]{:S(2)}) collective-permute-start(bf16[9,16,256]{2,1,0:T(8,128)(2,1)S(1)} %pad_maximum_fusion.5), channel_id=1, source_target_pairs={{0,8},{2,6},{4,12},{6,2},{8,0},{10,14},{12,4},{14,10},{16,24},{18,... | collective-permute-start | bytes 221192 | tf_op jit(solution)/shard_map/ppermute | solution.py:318
  45.2 5.2 %collective-permute-start.13 = (bf16[9,16,256]{2,1,0:T(8,128)(2,1)S(1)}, bf16[9,16,256]{2,1,0:T(8,128)(2,1)S(1)}, u32[]{:S(2)}, u32[]{:S(2)}) collective-permute-start(bf16[9,16,256]{2,1,0:T(8,128)(2,1)S(1)} %add_convert_fusion.3), channel_id=1, source_target_pairs={{0,4},{2,10},{4,0},{6,14},{8,12},{10,2},{12,8},{14,6},{16,20},{18,... | collective-permute-start | bytes 221192 | tf_op jit(solution)/shard_map/ppermute | solution.py:318
  48.1 5.2 %collective-permute-start.21 = (bf16[9,32,256]{2,1,0:T(8,128)(2,1)S(1)}, bf16[9,32,256]{2,1,0:T(8,128)(2,1)S(1)}, u32[]{:S(2)}, u32[]{:S(2)}) collective-permute-start(bf16[9,32,256]{2,1,0:T(8,128)(2,1)S(1)} %pad_maximum_fusion.4), channel_id=1, source_target_pairs={{0,4},{2,10},{4,0},{6,14},{8,12},{10,2},{12,8},{14,6},{16,20},{18,... | collective-permute-start | bytes 442376 | tf_op jit(solution)/shard_map/ppermute | solution.py:318
  50.4 5.2 %collective-permute-start.14 = (bf16[9,32,256]{2,1,0:T(8,128)(2,1)S(1)}, bf16[9,32,256]{2,1,0:T(8,128)(2,1)S(1)}, u32[]{:S(2)}, u32[]{:S(2)}) collective-permute-start(bf16[9,32,256]{2,1,0:T(8,128)(2,1)S(1)} %pad_maximum_fusion.3), channel_id=1, source_target_pairs={{0,8},{2,6},{4,12},{6,2},{8,0},{10,14},{12,4},{14,10},{16,24},{18,... | collective-permute-start | bytes 442376 | tf_op jit(solution)/shard_map/ppermute | solution.py:318
  53.4 2.4 %collective-permute-start.22 = (bf16[9,64,256]{2,1,0:T(8,128)(2,1)S(1)}, bf16[9,64,256]{2,1,0:T(8,128)(2,1)S(1)}, u32[]{:S(2)}, u32[]{:S(2)}) collective-permute-start(bf16[9,64,256]{2,1,0:T(8,128)(2,1)S(1)} %pad_maximum_fusion.1), channel_id=1, source_target_pairs={{0,2},{2,0},{4,6},{6,4},{8,10},{10,8},{12,14},{14,12},{16,18},{18,... | collective-permute-start | bytes 884744 | tf_op jit(solution)/shard_map/ppermute | solution.py:318
  55.7 1.6 %collective-permute-start.15 = (bf16[9,64,256]{2,1,0:T(8,128)(2,1)S(1)}, bf16[9,64,256]{2,1,0:T(8,128)(2,1)S(1)}, u32[]{:S(2)}, u32[]{:S(2)}) collective-permute-start(bf16[9,64,256]{2,1,0:T(8,128)(2,1)S(1)} %pad_maximum_fusion), channel_id=1, source_target_pairs={{0,2},{2,0},{4,6},{6,4},{8,10},{10,8},{12,14},{14,12},{16,18},{18,... | collective-permute-start | bytes 884744 | tf_op jit(solution)/shard_map/ppermute | solution.py:318
